TPU v7x, 256 devices: a whole 4x4x8 slice. The times are simulated.
256 devices in a mesh: dp: 4 (over x), ctx: 64 (over y, z, core).
Axes of the slice: x: 4, y: 4, z: 8, core: 2. Of those that a mesh axis runs over, the one named last changes fastest.
Arguments:
- win_query: bfloat16 [4, 16384, 1280], P('dp', 'ctx'), may hold values from -180 to 180
- win_key: bfloat16 [4, 16384, 1280], P('dp', 'ctx'), may hold values from -6 to 6
- win_value: bfloat16 [4, 16384, 1280], P('dp', 'ctx'), may hold values from -6 to 6
- win_grad_out: bfloat16 [4, 16384, 1280], P('dp', 'ctx'), may hold values from -6 to 6
- full_query: bfloat16 [4, 16384, 1280], P('dp', 'ctx'), may hold values from -180 to 180
- full_key: bfloat16 [4, 16384, 1280], P('dp', 'ctx'), may hold values from -6 to 6
- full_value: bfloat16 [4, 16384, 1280], P('dp', 'ctx'), may hold values from -6 to 6
- full_grad_out: bfloat16 [4, 16384, 1280], P('dp', 'ctx'), may hold values from -3 to 3
- proj_weight: bfloat16 [1280, 1280], P('ctx'), may hold values from -0.15625 to 0.15625
- positions: int32 [2, 4, 16384], P(None, 'dp', 'ctx'), may hold values from 0 to 31
- tile_perm: int32 [4, 16, 16], P('dp'), may hold values from 0 to 15, each once within a row
- tile_counts: int32 [4, 16, 4], P('dp'), may hold values from 1 to 8, 16 in all within a row
Outputs:
- win_dquery: bfloat16 [4, 32768, 1280], P('dp', 'ctx')
- win_dkey: bfloat16 [4, 32768, 1280], P('dp', 'ctx')
- win_dvalue: bfloat16 [4, 32768, 1280], P('dp', 'ctx')
- full_dquery: bfloat16 [4, 16384, 1280], P('dp', 'ctx')
- full_dkey: bfloat16 [4, 16384, 1280], P('dp', 'ctx')
- full_dvalue: bfloat16 [4, 16384, 1280], P('dp', 'ctx')
- proj_dweight: float32 [1280, 1280], P('ctx')
Inputs may be any that keep to these rules, and one draw needn't show every extreme that they name: `tile_perm`: each row names every tile of its slice once. `tile_counts`: the 4 counts of a slice sum to 16, and in every draw some owner takes exactly 8.
All inputs are finite; a program needn't handle non-finite values.
Results may differ from a plain program's by a relative error of at most 0.013.
Values may be sent and summed in bfloat16 or wider, within the bound.
No kernel may reach another device: no remote copies, remote signals or barrier semaphores. Data moves between devices by JAX's collectives and lax.ppermute only.
A program may use at most 128 MiB of HBM per device.

v0:
```python
import jax
import jax.numpy as jnp
from jax import lax
from jax.sharding import PartitionSpec as P

HEADS = 16
HEAD_DIM = 80
WIN = 8
TILES = 16
GROUP = 4
CAP = 8


def from_partner(block, axis, bit):
    count = lax.axis_size(axis)
    route = []
    for low in range(count):
        high = low | 1 << bit
        if high != low and high < count:
            route += [(low, high), (high, low)]
    return lax.ppermute(block, axis, route)


def rotary_tables(row_index, col_index):
    quarter = HEAD_DIM // 4
    inverse = 1.0 / 10000.0 ** (jnp.arange(quarter).astype(jnp.float32) * 4.0 / HEAD_DIM)
    angle = jnp.concatenate([row_index[..., None] * inverse, col_index[..., None] * inverse], -1)
    angle = jnp.concatenate([angle, angle], -1)
    return (jnp.cos(angle), jnp.sin(angle))


def half_turn(tensor):
    middle = tensor.shape[-1] // 2
    return jnp.concatenate([-tensor[..., middle:], tensor[..., :middle]], -1)


def half_turn_back(tensor):
    middle = tensor.shape[-1] // 2
    return jnp.concatenate([tensor[..., middle:], -tensor[..., :middle]], -1)


def rotate(tensor, cos_table, sin_table):
    return tensor * cos_table[..., None, :] + half_turn(tensor) * sin_table[..., None, :]


def unrotate(tensor, cos_table, sin_table):
    return tensor * cos_table[..., None, :] + half_turn_back(tensor * sin_table[..., None, :])


def attend_backward(query_rows, incoming_keys, incoming_values, incoming_gradient):
    logit_scale = HEAD_DIM ** (-0.5)
    attention_logits = (
        jnp.einsum("tyj,cyj->ytc", query_rows, incoming_keys, preferred_element_type=jnp.float32)
        * logit_scale
    )
    attn_probs = jax.nn.softmax(attention_logits, -1)
    probability_reduced = attn_probs.astype(jnp.bfloat16)
    attention_output = jnp.einsum(
        "sjx,xso->jso", probability_reduced, incoming_values, preferred_element_type=jnp.float32
    )
    probability_gradient = jnp.einsum(
        "tyj,cyj->ytc", incoming_gradient, incoming_values, preferred_element_type=jnp.float32
    )
    center = jnp.sum(incoming_gradient.astype(jnp.float32) * attention_output, -1).T
    dscores = attn_probs * (probability_gradient - center[:, :, None])
    score_gradient_reduced = dscores.astype(jnp.bfloat16)
    query_gradient_rows = (
        jnp.einsum(
            "sjx,xso->jso",
            score_gradient_reduced,
            incoming_keys,
            preferred_element_type=jnp.float32,
        )
        * logit_scale
    )
    key_gradient_rows = (
        jnp.einsum(
            "fqe,qfv->efv", score_gradient_reduced, query_rows, preferred_element_type=jnp.float32
        )
        * logit_scale
    )
    value_gradient_rows = jnp.einsum(
        "fqe,qfv->efv", probability_reduced, incoming_gradient, preferred_element_type=jnp.float32
    )
    return (attention_output, query_gradient_rows, key_gradient_rows, value_gradient_rows)


def window_backward(query_tile, key_tile, value_tile, grad_tile, cos_table, sin_table):
    tile_count, tile_rows, feature_width = query_tile.shape

    def heads_view(tensor):
        return tensor.reshape(tile_count, tile_rows, HEADS, HEAD_DIM)

    attention_output, query_gradient_rows, key_gradient_rows, value_gradient_rows = jax.vmap(
        attend_backward
    )(heads_view(query_tile), heads_view(key_tile), heads_view(value_tile), heads_view(grad_tile))
    query_gradient_rows = unrotate(query_gradient_rows, cos_table, sin_table)
    key_gradient_rows = unrotate(key_gradient_rows, cos_table, sin_table)
    return tuple(
        (
            piece_out.astype(jnp.bfloat16).reshape(tile_count, tile_rows, feature_width)
            for piece_out in (query_gradient_rows, key_gradient_rows, value_gradient_rows)
        )
    )


def join_halves(mine, other, upper_half):
    return jnp.where(
        upper_half, jnp.concatenate([other, mine], 0), jnp.concatenate([mine, other], 0)
    )


def gather_owner(pieces_in, shard_index):
    key_part, value_part, query_tile, key_tile, value_tile, grad_tile, spot_tile = pieces_in
    for bit_level in range(GROUP.bit_length() - 1):
        others = from_partner(
            (key_part, value_part, query_tile, key_tile, value_tile, grad_tile, spot_tile),
            "ctx",
            bit_level,
        )
        upper_half = (shard_index >> bit_level) % 2 == 1
        mine = (key_part, value_part, query_tile, key_tile, value_tile, grad_tile, spot_tile)
        key_part, value_part, query_tile, key_tile, value_tile, grad_tile, spot_tile = [
            join_halves(first, second, upper_half) for first, second in zip(mine, others)
        ]
    return (key_part, value_part, query_tile, key_tile, value_tile, grad_tile, spot_tile)


def reduce_slice(key_sum, value_sum, shard_index):
    for bit_level in reversed(range(GROUP.bit_length() - 1)):
        half_rows = key_sum.shape[0] // 2
        upper_half = (shard_index >> bit_level) % 2 == 1
        keep_key = jnp.where(upper_half, key_sum[half_rows:], key_sum[:half_rows])
        send_key = jnp.where(upper_half, key_sum[:half_rows], key_sum[half_rows:])
        keep_value = jnp.where(upper_half, value_sum[half_rows:], value_sum[:half_rows])
        send_value = jnp.where(upper_half, value_sum[:half_rows], value_sum[half_rows:])
        got_key, got_value = from_partner((send_key, send_value), "ctx", bit_level)
        key_sum = keep_key + got_key
        value_sum = keep_value + got_value
    return (key_sum, value_sum)


def head_blocks(tensor, row_count):
    return jnp.moveaxis(tensor.reshape(row_count, 4, HEADS // 4, HEAD_DIM), 1, 0)


def unblock(tensor, row_count):
    return jnp.moveaxis(tensor, 0, 1).reshape(row_count, HEADS, HEAD_DIM)


def shards(
    win_query,
    win_key,
    win_value,
    win_grad_out,
    full_query,
    full_key,
    full_value,
    full_grad_out,
    proj_weight,
    positions,
    tile_perm,
    tile_counts,
):
    rows_dev = win_query.shape[1]
    feature_width = win_query.shape[2]
    tile_rows = WIN * WIN
    shard_index = lax.axis_index("ctx")
    member = shard_index % GROUP
    slice_id = shard_index // GROUP
    row_index = positions[0, 0].astype(jnp.float32)
    col_index = positions[1, 0].astype(jnp.float32)
    cos_table, sin_table = rotary_tables(row_index, col_index)

    def turned(tensor):
        heads_in = tensor[0].reshape(rows_dev, HEADS, HEAD_DIM).astype(jnp.float32)
        return (
            rotate(heads_in, cos_table, sin_table)
            .astype(jnp.bfloat16)
            .reshape(rows_dev, feature_width)
        )

    win_q = turned(win_query)
    win_k = turned(win_key)
    full_q = turned(full_query)
    full_k = turned(full_key)
    counts = tile_counts[0][slice_id]
    perm_row = tile_perm[0][slice_id]
    before = jnp.sum(jnp.where(jnp.arange(GROUP) < member, counts, 0))
    slot_ids = jnp.arange(CAP)
    chosen = perm_row[jnp.minimum(before + slot_ids, TILES - 1)]
    slot_live = slot_ids < counts[member]

    def pick_tiles(tensor):
        return jnp.take(tensor.reshape((TILES, tile_rows) + tensor.shape[1:]), chosen, axis=0)

    def blank_slots(tensor):
        kept = jnp.where(slot_live[:, None, None], tensor, jnp.zeros_like(tensor))
        return kept.reshape(1, CAP * tile_rows, feature_width)

    spot_rows = jnp.stack([row_index, col_index], 1).astype(jnp.bfloat16)
    slice_keys, slice_values, all_q, all_k, all_v, all_g, all_spots = gather_owner(
        (full_k, full_value[0], win_q, win_k, win_value[0], win_grad_out[0], spot_rows), shard_index
    )
    spot_pick = pick_tiles(all_spots).astype(jnp.float32)
    tile_cos, tile_sin = rotary_tables(spot_pick[..., 0], spot_pick[..., 1])
    query_gradient_rows, key_gradient_rows, value_gradient_rows = window_backward(
        pick_tiles(all_q),
        pick_tiles(all_k),
        pick_tiles(all_v),
        pick_tiles(all_g),
        tile_cos,
        tile_sin,
    )
    win_dquery = blank_slots(query_gradient_rows)
    win_dkey = blank_slots(key_gradient_rows)
    win_dvalue = blank_slots(value_gradient_rows)
    grad_rows = full_grad_out[0]
    dattn = jnp.einsum(
        "td,rd->tr",
        grad_rows,
        lax.all_gather(proj_weight, "ctx", axis=0, tiled=True),
        preferred_element_type=jnp.float32,
    ).astype(jnp.bfloat16)
    key_rows = slice_keys.shape[0]
    blocks_in = (
        head_blocks(full_q, rows_dev),
        head_blocks(slice_keys, key_rows),
        head_blocks(slice_values, key_rows),
        head_blocks(dattn, rows_dev),
    )
    attention_output, query_part, key_part, value_part = lax.map(
        lambda block_set: attend_backward(*block_set), blocks_in
    )
    attention_output = unblock(attention_output, rows_dev)
    out_low = attention_output.reshape(rows_dev, feature_width).astype(jnp.bfloat16)
    weight_part = lax.psum_scatter(
        jnp.einsum("tr,td->rd", out_low, grad_rows, preferred_element_type=jnp.float32),
        "ctx",
        scatter_dimension=0,
        tiled=True,
    )
    proj_dweight = lax.psum(weight_part.astype(jnp.bfloat16), "dp").astype(jnp.float32)
    key_sum, value_sum = reduce_slice(
        unblock(key_part, key_rows).reshape(key_rows, feature_width),
        unblock(value_part, key_rows).reshape(key_rows, feature_width),
        shard_index,
    )
    full_dquery = (
        unrotate(unblock(query_part, rows_dev), cos_table, sin_table)
        .astype(jnp.bfloat16)
        .reshape(1, rows_dev, feature_width)
    )
    full_dkey = (
        unrotate(key_sum.reshape(rows_dev, HEADS, HEAD_DIM), cos_table, sin_table)
        .astype(jnp.bfloat16)
        .reshape(1, rows_dev, feature_width)
    )
    full_dvalue = value_sum.astype(jnp.bfloat16).reshape(1, rows_dev, feature_width)
    return (win_dquery, win_dkey, win_dvalue, full_dquery, full_dkey, full_dvalue, proj_dweight)


def solution(mesh):
    in_specs = (
        P("dp", "ctx", None),
        P("dp", "ctx", None),
        P("dp", "ctx", None),
        P("dp", "ctx", None),
        P("dp", "ctx", None),
        P("dp", "ctx", None),
        P("dp", "ctx", None),
        P("dp", "ctx", None),
        P("ctx", None),
        P(None, "dp", "ctx"),
        P("dp", None, None),
        P("dp", None, None),
    )
    out_specs = (
        P("dp", "ctx", None),
        P("dp", "ctx", None),
        P("dp", "ctx", None),
        P("dp", "ctx", None),
        P("dp", "ctx", None),
        P("dp", "ctx", None),
        P("ctx", None),
    )
    return jax.shard_map(shards, mesh=mesh, in_specs=in_specs, out_specs=out_specs, check_vma=False)
```

profile of v0, /device:TPU:1, one launch (start us, length us, event | category | flops | bytes accessed | tf_op | source)
XLA Modules:
  0.0 701.5 jit_solution(6787399437400363310)
XLA Ops:
  12.9 3.2 collective-permute-start.12
  55.9 3.2 maximum_select_fusion.8
  60.5 3.2 maximum_select_fusion.9
  67.7 21.4 %collective-permute-done.13 = bf16[512,1280]{0,1:T(8,128)(2,1)S(1)} collective-permute-done((bf16[512,1280]{0,1:T(8,128)(2,1)S(1)}, bf16[512,1280]{0,1:T(8,128)(2,1)S(1)}, u32[]{:S(2)}, u32[]{:S(2)}) %collective-permute-start.13) | collective-permute-done | bytes 1310752 | tf_op jit(solution)/shard_map/ppermute | solution.py:21
  89.9 27.9 %collective-permute-done.11 = bf16[512,1280]{0,1:T(8,128)(2,1)S(1)} collective-permute-done((bf16[512,1280]{0,1:T(8,128)(2,1)S(1)}, bf16[512,1280]{0,1:T(8,128)(2,1)S(1)}, u32[]{:S(2)}, u32[]{:S(2)}) %collective-permute-start.11) | collective-permute-done | bytes 1310752 | tf_op jit(solution)/shard_map/ppermute | solution.py:21
  119.7 6.1 reshape.607
  125.8 3.8 convolution_convert_fusion
  131.8 48.9 %while.16 = (s32[]{:T(128)}, bf16[4,256,4,80]{1,3,2,0:T(8,128)(2,1)}, f32[4,256,4,80]{1,3,2,0:T(8,128)}, f32[4,1024,4,80]{1,3,2,0:T(8,128)}, f32[4,1024,4,80]{1,...) while((s32[]{:T(128)}, ...), condition=%wide.region_8.10_spmd, body=%wide.region_4.9_spmd.sunk | while | flops 1017774080 | bytes 59304152 | solution.py:232
  180.8 4.9 fusion.73
  185.7 3.3 slice_select_fusion.1
  193.6 248.0 %fusion = f32[24,1280]{1,0:T(8,128)S(1)} fusion(f32[1280,1280]{1,0:T(8,128)} %fusion.73), kind=kCustom, calls=%all-reduce-scatter | all-reduce-scatter fusion | flops 1966081 | bytes 6677504
  447.8 2.9 collective-permute-start.15
  463.8 5.1 collective-permute-start.23
  470.8 4.3 collective-permute-start.25
  475.6 4.4 maximum_select_fusion.2
  480.7 6.0 collective-permute-start.26
  486.7 14.4 %collective-permute-start.27 = (bf16[24,1280]{1,0:T(8,128)(2,1)}, bf16[24,1280]{1,0:T(8,128)(2,1)}, u32[]{:S(2)}, u32[]{:S(2)}) collective-permute-start(bf16[24,1280]{1,0:T(8,128)(2,1)} %convert.59), channel_id=1, source_target_pairs={{0,10},{1,11},{2,12},{3,13},{4,14},{5,15},{6,16},{7,17},{8,18},{9,... | collective-permute-start | bytes 184328
  502.2 4.5 maximum_select_fusion.3
  506.7 4.4 copy.111
  511.1 4.4 copy.113
  515.5 3.5 gather_fusion.4
  519.0 3.5 gather_fusion.5
  522.4 17.9 %concatenate.223 = bf16[276,1280]{1,0:T(8,128)(2,1)} concatenate(bf16[12,1280]{1,0:T(8,128)(2,1)} %copy-done.39, bf16[24,1280]{1,0:T(8,128)(2,1)} %collective-permute-done.27, bf16[24,1280]{1,0:T(8,128)(2,1)} %collective-permute-done.26, bf16[24,1280]{1,0:T(8,128)(2,1)} %collective-permute-done.25, bf16[24,1280]{1,0:T(8,128)(2,1)} %collective-permute-done.24, ...), dimensions={0} | concatenate | bytes 1474560
  541.2 2.8 maximum_select_fusion.6
  544.6 13.8 %psum.7 = bf16[20,1280]{1,0:T(8,128)(2,1)S(1)} all-reduce(bf16[20,1280]{1,0:T(8,128)(2,1)S(1)} %dynamic-slice_convert_fusion), channel_id=1, replica_groups=mesh['dp'=4,'ctx'=64] {'dp'}, use_global_device_ids=true, to_apply=%region_10.12 | all-reduce | flops 25600 | bytes 102400 | tf_op jit(solution)/shard_map/psum | solution.py:243
  559.1 3.1 maximum_select_fusion.7
  569.9 4.8 collective-permute-done.1
  574.7 3.4 maximum_select_fusion
  580.9 3.4 gather_fusion.2
  584.3 18.5 %collective-permute-done.3 = bf16[512,1280]{0,1:T(8,128)(2,1)} collective-permute-done((bf16[512,1280]{0,1:T(8,128)(2,1)}, bf16[512,1280]{0,1:T(8,128)(2,1)}, u32[]{:S(2)}, u32[]{:S(2)}) %collective-permute-start.3) | collective-permute-done | bytes 1310752 | tf_op jit(solution)/shard_map/ppermute | solution.py:21
  602.8 3.5 maximum_select_fusion.1
  609.0 3.6 gather_fusion.3
  612.6 4.3 broadcast_select_fusion.2
  616.9 4.1 reshape.533
  621.0 5.0 reshape.534
  626.0 2.8 fusion.48
  628.8 3.2 fusion.93
  632.0 5.1 reshape.535
  637.0 5.2 reshape.536
  642.3 5.1 convert_bitcast_fusion
  654.8 4.0 fusion.87
  658.8 4.9 fusion.88
  663.7 5.4 fusion.40
  671.8 4.5 reshape.537
  679.1 4.5 reshape.538
  683.6 3.0 copy.127
  686.6 3.3 reshape.539
  689.8 4.4 broadcast_select_fusion.4
  (296 shorter events, 159.5 us)
Async XLA Ops:
  7.2 118.7 %copy-start = (bf16[1,256,1280]{2,1,0:T(8,128)(2,1)S(1)}, bf16[1,256,1280]{2,1,0:T(8,128)(2,1)}, u32[]{:S(2)}) copy-start(bf16[1,256,1280]{2,1,0:T(8,128)(2,1)} %param.23) | copy-start | bytes 1966084
  7.2 112.5 %all-gather.3.cloned.1.call-start = ((), (), s32[]{:S(2)}) async-start(), calls=%async_computation | async-start | bytes 3993600 | tf_op jit(solution)/shard_map/all_gather | solution.py:222
  10.4 28.2 %copy-start.25 = (f32[256,80]{0,1:T(8,128)}, f32[256,80]{0,1:T(8,128)S(1)}, u32[]{:S(2)}) copy-start(f32[256,80]{0,1:T(8,128)S(1)} %get-tuple-element.149) | copy-start | bytes 245764
  12.9 7.0 %copy-start.32 = (bf16[1,256,1280]{2,1,0:T(8,128)(2,1)S(1)}, bf16[1,256,1280]{2,1,0:T(8,128)(2,1)}, u32[]{:S(2)}) copy-start(bf16[1,256,1280]{2,1,0:T(8,128)(2,1)} %param.18) | copy-start | bytes 1966084
  12.9 35.2 %collective-permute-start.12 = (bf16[256,1280]{0,1:T(8,128)(2,1)}, bf16[256,1280]{0,1:T(8,128)(2,1)}, u32[]{:S(2)}, u32[]{:S(2)}) collective-permute-start(bf16[256,1280]{0,1:T(8,128)(2,1)} %fusion.65), channel_id=1, source_target_pairs={{0,1},{1,0},{2,3},{3,2},{4,5},{5,4},{6,7},{7,6},{8,9},{9,8},{10,11... | collective-permute-start | bytes 1966088 | tf_op jit(solution)/shard_map/ppermute | solution.py:21
  17.2 34.4 %collective-permute-start.10 = (bf16[256,1280]{0,1:T(8,128)(2,1)}, bf16[256,1280]{0,1:T(8,128)(2,1)}, u32[]{:S(2)}, u32[]{:S(2)}) collective-permute-start(bf16[256,1280]{0,1:T(8,128)(2,1)} %bitcast.42), channel_id=1, source_target_pairs={{0,1},{1,0},{2,3},{3,2},{4,5},{5,4},{6,7},{7,6},{8,9},{9,8},{10,11... | collective-permute-start | bytes 1966088 | tf_op jit(solution)/shard_map/ppermute | solution.py:21
  19.5 36.4 %collective-permute-start.4 = (bf16[256,1280]{0,1:T(8,128)(2,1)}, bf16[256,1280]{0,1:T(8,128)(2,1)}, u32[]{:S(2)}, u32[]{:S(2)}) collective-permute-start(bf16[256,1280]{0,1:T(8,128)(2,1)} %bitcast.27), channel_id=1, source_target_pairs={{0,1},{1,0},{2,3},{3,2},{4,5},{5,4},{6,7},{7,6},{8,9},{9,8},{10,11... | collective-permute-start | bytes 1966088 | tf_op jit(solution)/shard_map/ppermute | solution.py:21
  21.0 39.5 %collective-permute-start.6 = (bf16[256,1280]{0,1:T(8,128)(2,1)}, bf16[256,1280]{0,1:T(8,128)(2,1)}, u32[]{:S(2)}, u32[]{:S(2)}) collective-permute-start(bf16[256,1280]{0,1:T(8,128)(2,1)} %bitcast.29), channel_id=1, source_target_pairs={{0,1},{1,0},{2,3},{3,2},{4,5},{5,4},{6,7},{7,6},{8,9},{9,8},{10,11... | collective-permute-start | bytes 1966088 | tf_op jit(solution)/shard_map/ppermute | solution.py:21
  21.1 19.7 %collective-permute-start.8 = (bf16[256,2]{0,1:T(2,128)(2,1)S(1)}, bf16[256,2]{0,1:T(2,128)(2,1)S(1)}, u32[]{:S(2)}, u32[]{:S(2)}) collective-permute-start(bf16[256,2]{0,1:T(2,128)(2,1)S(1)} %pad_maximum_fusion.5), channel_id=1, source_target_pairs={{0,1},{1,0},{2,3},{3,2},{4,5},{5,4},{6,7},{7,6},{8,9},{9,8},{10,11... | collective-permute-start | bytes 3080 | tf_op jit(solution)/shard_map/ppermute | solution.py:21
  40.2 5.8 copy-start.42
  40.8 6.4 collective-permute-start.9
  50.1 39.0 %collective-permute-start.13 = (bf16[512,1280]{0,1:T(8,128)(2,1)S(1)}, bf16[512,1280]{0,1:T(8,128)(2,1)S(1)}, u32[]{:S(2)}, u32[]{:S(2)}) collective-permute-start(bf16[512,1280]{0,1:T(8,128)(2,1)S(1)} %maximum_select_fusion.12), channel_id=1, source_target_pairs={{0,2},{2,0},{1,3},{3,1},{4,6},{6,4},{5,7},{7,5},{8,10},{10,8},{9,1... | collective-permute-start | bytes 3932168 | tf_op jit(solution)/shard_map/ppermute | solution.py:21
  53.7 64.1 %collective-permute-start.11 = (bf16[512,1280]{0,1:T(8,128)(2,1)S(1)}, bf16[512,1280]{0,1:T(8,128)(2,1)S(1)}, u32[]{:S(2)}, u32[]{:S(2)}) collective-permute-start(bf16[512,1280]{0,1:T(8,128)(2,1)S(1)} %maximum_select_fusion.10), channel_id=1, source_target_pairs={{0,2},{2,0},{1,3},{3,1},{4,6},{6,4},{5,7},{7,5},{8,10},{10,8},{9,1... | collective-permute-start | bytes 3932168 | tf_op jit(solution)/shard_map/ppermute | solution.py:21
  55.9 8.0 %copy-start.22 = (bf16[256,4,4,80]{0,3,2,1:T(8,128)(2,1)S(1)}, bf16[256,4,4,80]{0,3,2,1:T(8,128)(2,1)}, u32[]{:S(2)}) copy-start(bf16[256,4,4,80]{0,3,2,1:T(8,128)(2,1)} %get-tuple-element.129) | copy-start | bytes 1966084
  59.1 398.8 %collective-permute-start.5 = (bf16[512,1280]{0,1:T(8,128)(2,1)}, bf16[512,1280]{0,1:T(8,128)(2,1)}, u32[]{:S(2)}, u32[]{:S(2)}) collective-permute-start(bf16[512,1280]{0,1:T(8,128)(2,1)} %maximum_select_fusion.8), channel_id=1, source_target_pairs={{0,2},{2,0},{1,3},{3,1},{4,6},{6,4},{5,7},{7,5},{8,10},{10,8},{9,1... | collective-permute-start | bytes 3932168 | tf_op jit(solution)/shard_map/ppermute | solution.py:21
  63.7 395.6 %collective-permute-start.7 = (bf16[512,1280]{0,1:T(8,128)(2,1)}, bf16[512,1280]{0,1:T(8,128)(2,1)}, u32[]{:S(2)}, u32[]{:S(2)}) collective-permute-start(bf16[512,1280]{0,1:T(8,128)(2,1)} %maximum_select_fusion.9), channel_id=1, source_target_pairs={{0,2},{2,0},{1,3},{3,1},{4,6},{6,4},{5,7},{7,5},{8,10},{10,8},{9,1... | collective-permute-start | bytes 3932168 | tf_op jit(solution)/shard_map/ppermute | solution.py:21
  180.7 4.9 slice-start.2
  180.7 4.9 slice-start.3
  185.7 4.7 slice-start
  189.0 258.8 %collective-permute-start.16 = (f32[512,1280]{0,1:T(8,128)}, f32[512,1280]{0,1:T(8,128)}, u32[]{:S(2)}, u32[]{:S(2)}) collective-permute-start(f32[512,1280]{0,1:T(8,128)} %bitcast.77), channel_id=1, source_target_pairs={{0,2},{2,0},{1,3},{3,1},{4,6},{6,4},{5,7},{7,5},{8,10},{10,8},{9,1... | collective-permute-start | bytes 7864328 | tf_op jit(solution)/shard_map/ppermute | solution.py:21
  192.6 251.7 %collective-permute-start.14 = (f32[512,1280]{0,1:T(8,128)}, f32[512,1280]{0,1:T(8,128)}, u32[]{:S(2)}, u32[]{:S(2)}) collective-permute-start(f32[512,1280]{0,1:T(8,128)} %bitcast.71), channel_id=1, source_target_pairs={{0,2},{2,0},{1,3},{3,1},{4,6},{6,4},{5,7},{7,5},{8,10},{10,8},{9,1... | collective-permute-start | bytes 7864328 | tf_op jit(solution)/shard_map/ppermute | solution.py:21
  442.3 21.5 %collective-permute-start.18 = (bf16[24,1280]{1,0:T(8,128)(2,1)}, bf16[24,1280]{1,0:T(8,128)(2,1)S(1)}, u32[]{:S(2)}, u32[]{:S(2)}) collective-permute-start(bf16[24,1280]{1,0:T(8,128)(2,1)} %convert.59), channel_id=1, source_target_pairs={{0,1},{1,2},{2,3},{3,4},{4,5},{5,6},{6,7},{7,8},{8,9},{9,10},{10,1... | collective-permute-start | bytes 184328
  444.3 24.7 %collective-permute-start.19 = (bf16[24,1280]{1,0:T(8,128)(2,1)}, bf16[24,1280]{1,0:T(8,128)(2,1)S(1)}, u32[]{:S(2)}, u32[]{:S(2)}) collective-permute-start(bf16[24,1280]{1,0:T(8,128)(2,1)} %convert.59), channel_id=1, source_target_pairs={{0,2},{1,3},{2,4},{3,5},{4,6},{5,7},{6,8},{7,9},{8,10},{9,11},{10,... | collective-permute-start | bytes 184328
  447.8 6.2 collective-permute-start.15
  454.1 6.6 collective-permute-start.28
  457.9 13.0 %collective-permute-start.20 = (bf16[24,1280]{1,0:T(8,128)(2,1)}, bf16[24,1280]{1,0:T(8,128)(2,1)S(1)}, u32[]{:S(2)}, u32[]{:S(2)}) collective-permute-start(bf16[24,1280]{1,0:T(8,128)(2,1)} %convert.59), channel_id=1, source_target_pairs={{0,3},{1,4},{2,5},{3,6},{4,7},{5,8},{6,9},{7,10},{8,11},{9,12},{10... | collective-permute-start | bytes 184328
  459.3 15.8 %collective-permute-start.21 = (bf16[24,1280]{1,0:T(8,128)(2,1)}, bf16[24,1280]{1,0:T(8,128)(2,1)S(1)}, u32[]{:S(2)}, u32[]{:S(2)}) collective-permute-start(bf16[24,1280]{1,0:T(8,128)(2,1)} %convert.59), channel_id=1, source_target_pairs={{0,4},{1,5},{2,6},{3,7},{4,8},{5,9},{6,10},{7,11},{8,12},{9,13},{1... | collective-permute-start | bytes 184328
  460.6 14.5 %collective-permute-start.22 = (bf16[24,1280]{1,0:T(8,128)(2,1)}, bf16[24,1280]{1,0:T(8,128)(2,1)S(1)}, u32[]{:S(2)}, u32[]{:S(2)}) collective-permute-start(bf16[24,1280]{1,0:T(8,128)(2,1)} %convert.59), channel_id=1, source_target_pairs={{0,5},{1,6},{2,7},{3,8},{4,9},{5,10},{6,11},{7,12},{8,13},{9,14},{... | collective-permute-start | bytes 184328
  463.8 16.3 %collective-permute-start.23 = (bf16[24,1280]{1,0:T(8,128)(2,1)}, bf16[24,1280]{1,0:T(8,128)(2,1)S(1)}, u32[]{:S(2)}, u32[]{:S(2)}) collective-permute-start(bf16[24,1280]{1,0:T(8,128)(2,1)} %convert.59), channel_id=1, source_target_pairs={{0,6},{1,7},{2,8},{3,9},{4,10},{5,11},{6,12},{7,13},{8,14},{9,15},... | collective-permute-start | bytes 184328
  468.9 11.1 %copy-start.34 = (bf16[24,1280]{1,0:T(8,128)(2,1)}, bf16[24,1280]{1,0:T(8,128)(2,1)S(1)}, u32[]{:S(2)}) copy-start(bf16[24,1280]{1,0:T(8,128)(2,1)S(1)} %collective-permute-done.19) | copy-start | bytes 184324
  468.9 17.8 %collective-permute-start.24 = (bf16[24,1280]{1,0:T(8,128)(2,1)}, bf16[24,1280]{1,0:T(8,128)(2,1)}, u32[]{:S(2)}, u32[]{:S(2)}) collective-permute-start(bf16[24,1280]{1,0:T(8,128)(2,1)} %convert.59), channel_id=1, source_target_pairs={{0,7},{1,8},{2,9},{3,10},{4,11},{5,12},{6,13},{7,14},{8,15},{9,16}... | collective-permute-start | bytes 184328
  470.8 9.2 %copy-start.35 = (bf16[24,1280]{1,0:T(8,128)(2,1)}, bf16[24,1280]{1,0:T(8,128)(2,1)S(1)}, u32[]{:S(2)}) copy-start(bf16[24,1280]{1,0:T(8,128)(2,1)S(1)} %collective-permute-done.20) | copy-start | bytes 184324
  470.8 30.3 %collective-permute-start.25 = (bf16[24,1280]{1,0:T(8,128)(2,1)}, bf16[24,1280]{1,0:T(8,128)(2,1)}, u32[]{:S(2)}, u32[]{:S(2)}) collective-permute-start(bf16[24,1280]{1,0:T(8,128)(2,1)} %convert.59), channel_id=1, source_target_pairs={{0,8},{1,9},{2,10},{3,11},{4,12},{5,13},{6,14},{7,15},{8,16},{9,17... | collective-permute-start | bytes 184328
  475.1 5.0 copy-start.36
  475.1 88.1 %collective-permute-start.17 = (f32[256,1280]{0,1:T(8,128)}, f32[256,1280]{0,1:T(8,128)}, u32[]{:S(2)}, u32[]{:S(2)}) collective-permute-start(f32[256,1280]{0,1:T(8,128)} %slice_select_fusion.4), channel_id=1, source_target_pairs={{0,1},{1,0},{2,3},{3,2},{4,5},{5,4},{6,7},{7,6},{8,9},{9,8},{10,11... | collective-permute-start | bytes 3932168 | tf_op jit(solution)/shard_map/ppermute | solution.py:21
  475.1 5.0 copy-start.37
  475.1 66.1 %collective-permute-start = (bf16[256,1280]{0,1:T(8,128)(2,1)}, bf16[256,1280]{0,1:T(8,128)(2,1)S(1)}, u32[]{:S(2)}, u32[]{:S(2)}) collective-permute-start(bf16[256,1280]{0,1:T(8,128)(2,1)} %get-tuple-element.143), channel_id=1, source_target_pairs={{0,1},{1,0},{2,3},{3,2},{4,5},{5,4},{6,7},{7,6},{8,9},{9,8},{10,11... | collective-permute-start | bytes 1966088 | tf_op jit(solution)/shard_map/ppermute | solution.py:21
  480.7 41.7 %collective-permute-start.26 = (bf16[24,1280]{1,0:T(8,128)(2,1)}, bf16[24,1280]{1,0:T(8,128)(2,1)}, u32[]{:S(2)}, u32[]{:S(2)}) collective-permute-start(bf16[24,1280]{1,0:T(8,128)(2,1)} %convert.59), channel_id=1, source_target_pairs={{0,9},{1,10},{2,11},{3,12},{4,13},{5,14},{6,15},{7,16},{8,17},{9,1... | collective-permute-start | bytes 184328
  486.7 35.7 %collective-permute-start.27 = (bf16[24,1280]{1,0:T(8,128)(2,1)}, bf16[24,1280]{1,0:T(8,128)(2,1)}, u32[]{:S(2)}, u32[]{:S(2)}) collective-permute-start(bf16[24,1280]{1,0:T(8,128)(2,1)} %convert.59), channel_id=1, source_target_pairs={{0,10},{1,11},{2,12},{3,13},{4,14},{5,15},{6,16},{7,17},{8,18},{9,... | collective-permute-start | bytes 184328
  501.2 57.9 %collective-permute-start.2 = (bf16[256,1280]{0,1:T(8,128)(2,1)}, bf16[256,1280]{0,1:T(8,128)(2,1)}, u32[]{:S(2)}, u32[]{:S(2)}) collective-permute-start(bf16[256,1280]{0,1:T(8,128)(2,1)} %get-tuple-element.142), channel_id=1, source_target_pairs={{0,1},{1,0},{2,3},{3,2},{4,5},{5,4},{6,7},{7,6},{8,9},{9,8},{10,11... | collective-permute-start | bytes 1966088 | tf_op jit(solution)/shard_map/ppermute | solution.py:21
  544.0 30.7 %collective-permute-start.1 = (bf16[512,1280]{0,1:T(8,128)(2,1)}, bf16[512,1280]{0,1:T(8,128)(2,1)}, u32[]{:S(2)}, u32[]{:S(2)}) collective-permute-start(bf16[512,1280]{0,1:T(8,128)(2,1)} %maximum_select_fusion.6), channel_id=1, source_target_pairs={{0,2},{2,0},{1,3},{3,1},{4,6},{6,4},{5,7},{7,5},{8,10},{10,8},{9,1... | collective-permute-start | bytes 3932168 | tf_op jit(solution)/shard_map/ppermute | solution.py:21
  562.1 40.7 %collective-permute-start.3 = (bf16[512,1280]{0,1:T(8,128)(2,1)}, bf16[512,1280]{0,1:T(8,128)(2,1)}, u32[]{:S(2)}, u32[]{:S(2)}) collective-permute-start(bf16[512,1280]{0,1:T(8,128)(2,1)} %maximum_select_fusion.7), channel_id=1, source_target_pairs={{0,2},{2,0},{1,3},{3,1},{4,6},{6,4},{5,7},{7,5},{8,10},{10,8},{9,1... | collective-permute-start | bytes 3932168 | tf_op jit(solution)/shard_map/ppermute | solution.py:21
  642.2 5.1 copy-start.14
  642.2 5.1 copy-start.23
  642.2 6.1 copy-start.24
  658.8 4.9 copy-start.3
  658.8 4.9 copy-start.29
  686.6 7.7 %copy-start.1 = (bf16[1,256,1280]{2,1,0:T(8,128)(2,1)S(1)}, bf16[1,256,1280]{2,1,0:T(8,128)(2,1)}, u32[]{:S(2)}) copy-start(bf16[1,256,1280]{2,1,0:T(8,128)(2,1)} %param.23) | copy-start | bytes 1966084
  (41 other events, 94.2 us)
Sparse Core Ops, SparseCore 0:
  10.7 83.9 all-gather.2
where the time goes:
time: 713 us; the launch traced here: 701 us
  blocking collectives  262 us (37%)
  local copies, waits for them, and re-layouts  127 us (18%)
  other arithmetic  108 us (15%)
  waiting for transfers between devices  73.4 us (10%)
  matrix products  57.8 us (8%)
  starting transfers between devices  56.5 us (8%)
  between operations  15.9 us (2%)
    unnamed x1, blocking collectives  248 us
    ppermute x18, waiting for transfers between devices, from_partner(): return lax.ppermute(block, axis, route)  72.7 us
    unnamed x100, local copies, waits for them, and re-layouts  43.3 us
    unnamed x11, starting transfers between devices  40.5 us
    select_n x14, other arithmetic, join_halves(): jnp.where(upper_half, jnp.concatenate([other, mine], 0), jnp.concatenate(...  35.9 us
    reshape x4, local copies, waits for them, and re-layouts, heads_view(): return tensor.reshape(tile_count, tile_rows, HEADS, HEAD_DIM)  19.3 us
    ppermute x18, starting transfers between devices, from_partner(): return lax.ppermute(block, axis, route)  16 us
    gather x5, local copies, waits for them, and re-layouts, pick_tiles(): jnp.take(tensor.reshape((TILES, tile_rows) + tensor.shape[1:]), chosen, a...  14.5 us
  transfers between devices with their start and end apart: 30, of which 4 were waited for; matrix products, arithmetic and copies ran while one was open for 63% of the time, Pallas kernels for 0%

commit v1 on v0

v1 whole, which is shorter than its diff:
```python
import functools

import jax
import jax.numpy as jnp
from jax import lax
from jax.experimental import pallas as pl
from jax.experimental.pallas import tpu as pltpu
from jax.sharding import PartitionSpec as P

HEADS = 16
HEAD_DIM = 80
HALF = HEAD_DIM // 2
TILE = 64
TILES = 16
GROUP = 4
CAP = 8
D = HEADS * HEAD_DIM
QUARTER = D // GROUP
SCALE = HEAD_DIM**-0.5
SCALE2 = SCALE * 1.4426950408889634
BF = jnp.bfloat16
F32 = jnp.float32
VM = pl.BlockSpec(memory_space=pltpu.VMEM)
SM = pl.BlockSpec(memory_space=pltpu.SMEM)
HINT = pl.CostEstimate(flops=100_000, bytes_accessed=100_000, transcendentals=0)


def params(mib=56):
    return pltpu.CompilerParams(vmem_limit_bytes=mib << 20)


def dot(left, right, left_dim, right_dim):
    return lax.dot_general(
        left, right, (((left_dim,), (right_dim,)), ((), ())), preferred_element_type=F32
    )


def turn(rows, cos, sin):
    low, high = rows[:HALF], rows[HALF:]
    return jnp.concatenate([low * cos - high * sin, high * cos + low * sin], 0)


def turn_back(rows, cos, sin):
    low, high = rows[:HALF], rows[HALF:]
    return jnp.concatenate([low * cos + high * sin, high * cos - low * sin], 0)


def load_turned(source, target, scratch, cos, sin):
    width = source.shape[1]
    for block in range(0, width, 128):
        scratch[block : block + 128, :] = source[:, block : block + 128].astype(F32).T
    for head in range(0, width, HEAD_DIM):
        rows = scratch[head : head + HEAD_DIM, :]
        if cos is not None:
            rows = turn(rows, cos, sin)
        target[head : head + HEAD_DIM, :] = rows.astype(BF)


def store_natural(scratch, target):
    for block in range(0, scratch.shape[0], 128):
        target[:, block : block + 128] = scratch[block : block + 128, :].T.astype(BF)


def split_kernel(place, query, key, value, cos_ref, sin_ref, out0, out1, out2, out3, scratch, qt, kt, vt):
    cos, sin = cos_ref[...], sin_ref[...]
    load_turned(query, qt, scratch, cos, sin)
    load_turned(key, kt, scratch, cos, sin)
    load_turned(value, vt, scratch, None, None)
    member = place[0]
    for step, out in enumerate((out0, out1, out2, out3)):
        for part, source in enumerate((qt, kt, vt)):
            for block in range(GROUP):
                start = pl.multiple_of((member ^ step) * HEAD_DIM + block * QUARTER, HEAD_DIM)
                target = part * QUARTER + block * HEAD_DIM
                out[target : target + HEAD_DIM, :] = source[pl.ds(start, HEAD_DIM), :]


def split_heads(place, query, key, value, cos, sin):
    rows = query.shape[0]
    return pl.pallas_call(
        split_kernel,
        out_shape=[jax.ShapeDtypeStruct((3 * QUARTER, rows), BF)] * GROUP,
        in_specs=[SM] + [VM] * 5,
        out_specs=[VM] * GROUP,
        scratch_shapes=[pltpu.VMEM((D, rows), F32)] + [pltpu.VMEM((D, rows), BF)] * 3,
        compiler_params=params(),
        cost_estimate=HINT,
        name="split_heads",
    )(place, query, key, value, cos, sin)


def window_kernel(place, query, key, value, grad, cos_ref, sin_ref, *refs):
    del place
    outs, (scratch, qt, kt, vt, gt, dqt, dkt, dvt) = refs[:-8], refs[-8:]
    cos, sin = cos_ref[...], sin_ref[...]
    load_turned(query, qt, scratch, cos, sin)
    load_turned(key, kt, scratch, cos, sin)
    load_turned(value, vt, scratch, None, None)
    load_turned(grad, gt, scratch, None, None)
    rows, width = query.shape
    same = (
        lax.broadcasted_iota(jnp.int32, (rows, rows), 0) // TILE
        == lax.broadcasted_iota(jnp.int32, (rows, rows), 1) // TILE
    )

    def head_step(head, carry):
        here = pl.ds(pl.multiple_of(head * HEAD_DIM, HEAD_DIM), HEAD_DIM)
        q, k, v, g = qt[here, :], kt[here, :], vt[here, :], gt[here, :]
        logits = jnp.where(same, dot(k, q, 0, 0), -1e30)
        raised = jnp.exp2((logits - jnp.max(logits, 0, keepdims=True)) * SCALE2)
        inverse = 1.0 / jnp.sum(raised, 0, keepdims=True)
        low = raised.astype(BF)
        g = (g.astype(F32) * inverse).astype(BF)
        center = jnp.sum(g.astype(F32) * (dot(v, low, 1, 0) * inverse), 0, keepdims=True)
        dscores = (raised * (dot(v, g, 0, 0) - center)).astype(BF)
        dqt[here, :] = turn_back(dot(k, dscores, 1, 0) * SCALE, cos, sin)
        dkt[here, :] = turn_back(dot(q, dscores, 1, 1) * SCALE, cos, sin)
        dvt[here, :] = dot(g, low, 1, 1)
        return carry

    lax.fori_loop(0, width // HEAD_DIM, head_step, 0, unroll=2)
    places = [out.at[at : at + rows] for out in outs for at in range(0, out.shape[0], rows)]
    for source, target in zip((dqt, dkt, dvt), places):
        store_natural(source, target)


def window_grads(place, query, key, value, grad, cos, sin, half, packs):
    rows, width = query.shape[0], D // 2
    block = pl.BlockSpec((rows, width), lambda step: (0, half))
    return pl.pallas_call(
        window_kernel,
        grid=(1,),
        out_shape=[jax.ShapeDtypeStruct((pack * rows, width), BF) for pack in packs],
        in_specs=[SM] + [block] * 4 + [VM] * 2,
        out_specs=[VM] * len(packs),
        scratch_shapes=[pltpu.VMEM((width, rows), F32)] + [pltpu.VMEM((width, rows), BF)] * 4 + [pltpu.VMEM((width, rows), F32)] * 3,
        compiler_params=params(),
        cost_estimate=HINT,
        name="window_grads",
    )(place, query, key, value, grad, cos, sin)


def heads_of(pieces, first, part, width):
    rows = pl.ds(pl.multiple_of(first + part * width, 16), HEAD_DIM)
    return jnp.concatenate([piece[rows, :] for piece in pieces], 1)


def probs_kernel(place, piece0, piece1, piece2, piece3, raised_low, out, inverses):
    del place
    pieces = (piece0, piece1, piece2, piece3)
    rows = piece0.shape[1]
    first = pl.multiple_of(pl.program_id(0) * HEAD_DIM, HEAD_DIM)
    here = pl.ds(first, HEAD_DIM)
    k_rows, v = heads_of(pieces, first, 1, QUARTER).T, heads_of(pieces, first, 2, QUARTER)
    for step in range(GROUP):
        block = slice(step * rows, (step + 1) * rows)
        logits = dot(k_rows, pieces[step][here, :], 1, 0)
        raised = jnp.exp2((logits - jnp.max(logits, 0, keepdims=True)) * SCALE2)
        inverse = 1.0 / jnp.sum(raised, 0, keepdims=True)
        low = raised.astype(BF)
        raised_low[0, :, block] = low
        inverses[pl.program_id(0), :, block] = inverse
        out[here, block] = dot(v, low, 1, 0) * inverse


def full_probs(place, pieces):
    length = GROUP * pieces[0].shape[1]
    heads = HEADS // GROUP
    return pl.pallas_call(
        probs_kernel,
        grid=(heads,),
        out_shape=[
            jax.ShapeDtypeStruct((heads, length, length), BF),
            jax.ShapeDtypeStruct((QUARTER, length), F32),
            jax.ShapeDtypeStruct((heads, 1, length), F32),
        ],
        in_specs=[SM] + [VM] * 4,
        out_specs=[pl.BlockSpec((1, length, length), lambda head: (head, 0, 0)), VM, VM],
        compiler_params=params(),
        cost_estimate=HINT,
        name="full_probs",
    )(place, *pieces)


def share_kernel(*refs):
    place, out, grads, weights, shares, dattn = refs[0], refs[1], refs[2:6], refs[6:10], refs[10:14], refs[14]
    product, weight = refs[15:]
    rows = grads[0].shape[0]
    starts = [pl.multiple_of((place[1] ^ step) * HEAD_DIM, HEAD_DIM) for step in range(GROUP)]
    for step in range(GROUP):
        weight[pl.ds(starts[step], HEAD_DIM), :] = weights[step][...]
    for step in range(GROUP):
        block = slice(step * rows, (step + 1) * rows)
        dattn[:, block] = dot(weight[...], grads[step][...], 1, 1).astype(BF)
        share = dot(out[:, block].astype(BF), grads[step][...], 1, 0)
        product[...] = share if step == 0 else product[...] + share
    for step in range(GROUP):
        shares[step][...] = product[pl.ds(starts[step], HEAD_DIM), :].astype(BF)


def weight_shares(place, out, grads, weights):
    return pl.pallas_call(
        share_kernel,
        out_shape=[jax.ShapeDtypeStruct((HEAD_DIM, D), BF)] * GROUP + [jax.ShapeDtypeStruct(out.shape, BF)],
        in_specs=[SM] + [VM] * 9,
        out_specs=[VM] * 5,
        scratch_shapes=[pltpu.VMEM((QUARTER, D), F32), pltpu.VMEM((QUARTER, D), BF)],
        compiler_params=params(),
        cost_estimate=HINT,
        name="weight_shares",
    )(place, out, *grads, *weights)


def grads_kernel(*refs):
    pieces, dattn, out, inverses, raised_low, backs = refs[1:5], refs[5], refs[6], refs[7], refs[8], refs[9:]
    rows = pieces[0].shape[1]
    first = pl.multiple_of(pl.program_id(0) * HEAD_DIM, HEAD_DIM)
    here = pl.ds(first, HEAD_DIM)
    k, v_rows = heads_of(pieces, first, 1, QUARTER), heads_of(pieces, first, 2, QUARTER).T
    dk = jnp.zeros((HEAD_DIM, GROUP * rows), F32)
    dv = jnp.zeros((HEAD_DIM, GROUP * rows), F32)
    for step in range(GROUP):
        block = slice(step * rows, (step + 1) * rows)
        q, low = pieces[step][here, :], raised_low[0, :, block]
        g = (dattn[here, block].astype(F32) * inverses[pl.program_id(0), :, block]).astype(BF)
        center = jnp.sum(g.astype(F32) * out[here, block], 0, keepdims=True)
        dscores = (low.astype(F32) * (dot(v_rows, g, 1, 0) - center)).astype(BF)
        backs[step][here, :] = (dot(k, dscores, 1, 0) * SCALE).astype(BF)
        dk += dot(q, dscores, 1, 1)
        dv += dot(g, low, 1, 1)
    for step in range(GROUP):
        block = slice(step * rows, (step + 1) * rows)
        backs[step][pl.ds(pl.multiple_of(first + QUARTER, 16), HEAD_DIM), :] = (dk[:, block] * SCALE).astype(BF)
        backs[step][pl.ds(pl.multiple_of(first + 2 * QUARTER, 16), HEAD_DIM), :] = dv[:, block].astype(BF)


def full_grads(place, pieces, dattn, out, inverses, raised_low):
    rows = pieces[0].shape[1]
    length = GROUP * rows
    return pl.pallas_call(
        grads_kernel,
        grid=(HEADS // GROUP,),
        out_shape=[jax.ShapeDtypeStruct((3 * QUARTER, rows), BF)] * GROUP,
        in_specs=[SM] + [VM] * 7 + [pl.BlockSpec((1, length, length), lambda head: (head, 0, 0))],
        out_specs=[VM] * GROUP,
        compiler_params=params(),
        cost_estimate=HINT,
        name="full_grads",
    )(place, *pieces, dattn, out, inverses, raised_low)


def join_kernel(place, part0, part1, part2, part3, cos_ref, sin_ref, dquery, dkey, dvalue, scratch):
    cos, sin = cos_ref[...], sin_ref[...]
    member = place[0]
    for which, target in enumerate((dquery, dkey, dvalue)):
        for step, part in enumerate((part0, part1, part2, part3)):
            for block in range(GROUP):
                source = which * QUARTER + block * HEAD_DIM
                rows = part[source : source + HEAD_DIM, :].astype(F32)
                if which < 2:
                    rows = turn_back(rows, cos, sin)
                start = pl.multiple_of((member ^ step) * HEAD_DIM + block * QUARTER, HEAD_DIM)
                scratch[pl.ds(start, HEAD_DIM), :] = rows
        store_natural(scratch, target)


def join_heads(place, parts, cos, sin):
    rows = parts[0].shape[1]
    return pl.pallas_call(
        join_kernel,
        out_shape=[jax.ShapeDtypeStruct((rows, D), BF)] * 3,
        in_specs=[SM] + [VM] * 6,
        out_specs=[VM] * 3,
        scratch_shapes=[pltpu.VMEM((D, rows), F32)],
        compiler_params=params(),
        cost_estimate=HINT,
        name="join_heads",
    )(place, *parts, cos, sin)


def deal_kernel(starts, place, perm, counts, *refs):
    sources, out = (refs[:GROUP], refs[GROUP : 2 * GROUP]), refs[2 * GROUP]
    member, slice_id = place[0], place[2]
    width = sources[0][0].shape[1]
    before = jnp.int32(0)
    for owner in range(GROUP - 1):
        before += jnp.where(owner < member, counts[slice_id, owner], 0)
    taken = counts[slice_id, member]
    for slot in range(CAP):
        tile = perm[slice_id, jnp.minimum(before + slot, TILES - 1)]
        live = slot < taken
        where = (tile // GROUP) ^ member
        row = (tile % GROUP) * TILE
        target = slice(slot * TILE, (slot + 1) * TILE)
        for step in range(GROUP):

            @pl.when(live & (where == step))
            def _():
                for half, pieces in enumerate(sources):
                    here = pl.ds(pl.multiple_of(row + starts[half], TILE), TILE)
                    out[target, half * width : (half + 1) * width] = pieces[step][here, :]

        @pl.when(jnp.logical_not(live))
        def _():
            out[target, :] = jnp.zeros((TILE, out.shape[1]), BF)


def deal_tiles(place, perm, counts, first, second, starts):
    return pl.pallas_call(
        functools.partial(deal_kernel, starts),
        out_shape=jax.ShapeDtypeStruct((CAP * TILE, D), BF),
        in_specs=[SM] * 3 + [VM] * 8,
        out_specs=VM,
        compiler_params=params(),
        cost_estimate=HINT,
        name="deal_tiles",
    )(place, perm, counts, *first, *second)


def swap(array, axis, distance):
    count = lax.axis_size(axis)
    return lax.ppermute(array, axis, [(i, i ^ distance) for i in range(count)])


def rotary_tables(row_index, col_index):
    quarter = HEAD_DIM // 4
    inverse = 1.0 / 10000.0 ** (jnp.arange(quarter).astype(F32) * 4.0 / HEAD_DIM)
    angle = jnp.concatenate([inverse[:, None] * row_index[None], inverse[:, None] * col_index[None]], 0)
    return jnp.cos(angle), jnp.sin(angle)


def relabel(count, pair):
    where = lambda x, y, s, m: ((x * count + y) * count + s) * count + m
    span = range(count)
    route = [pair(x, y, s, m) for x in span for y in span for s in span for m in span]
    return [(where(*source), where(*target)) for source, target in route]


def gather_route(count):
    return relabel(count, lambda x, y, s, m: ((s, y, m, x), (x, y, s, m)))


def share_route(count, step):
    return relabel(count, lambda x, y, s, m: ((x, y, s, m), (s ^ step, y, m, x)))


def shards(
    win_query,
    win_key,
    win_value,
    win_grad_out,
    full_query,
    full_key,
    full_value,
    full_grad_out,
    proj_weight,
    positions,
    tile_perm,
    tile_counts,
):
    index = lax.axis_index("ctx")
    member, slice_id = index % GROUP, index // GROUP
    plane = slice_id // GROUP
    across = lax.axis_index("dp")
    place = jnp.stack([member, plane, slice_id]).astype(jnp.int32)
    tie = lax.optimization_barrier

    def total(arrays):
        return sum((array.astype(F32) for array in arrays[1:]), arrays[0].astype(F32))

    corner = lax.ppermute(proj_weight, ("dp", "ctx"), gather_route(GROUP))
    cos, sin = rotary_tables(positions[0, 0].astype(F32), positions[1, 0].astype(F32))
    pieces = split_heads(place, full_query[0], full_key[0], full_value[0], cos, sin)

    place, *pieces = tie((place, *pieces))
    piece1, piece2 = swap(pieces[1], "ctx", 1), swap(pieces[2], "ctx", 2)
    window_in = (win_query[0], win_key[0], win_value[0], win_grad_out[0], cos, sin)
    first = window_grads(place, *window_in, 0, (3,))

    place, first, corner, piece1, piece2, sent3 = tie((place, first, corner, piece1, piece2, pieces[3]))
    piece3 = swap(sent3, "ctx", 3)
    corners = [corner] + [swap(corner, "dp", step) for step in range(1, GROUP)]
    second = window_grads(place, *window_in, 1, (2, 1))

    place, first, second, piece3, corners, grad0 = tie((place, first, second, piece3, corners, full_grad_out[0]))
    pieces = (pieces[0], piece1, piece2, piece3)
    grad1, grad2 = swap(grad0, "ctx", 1), swap(grad0, "ctx", 2)
    low_bit, high_bit = across % 2 == 1, across // 2 == 1
    pairs = [jnp.where(low_bit, corners[i ^ 1], corners[i]) for i in range(GROUP)]
    weight0 = jnp.concatenate([jnp.where(high_bit, pairs[i ^ 2], pairs[i]) for i in range(GROUP)], 0)
    weights = [weight0] + [swap(weight0, "ctx", step * 16) for step in range(1, GROUP)]
    window = [*first, *second]
    raised_low, out, inverses = full_probs(place, pieces)

    place, raised_low, out, grad1, grad2, weights, window = tie(
        (place, raised_low, out, grad1, grad2, weights, window)
    )
    crossed = [swap(window[0], "ctx", 2)]
    grads = (grad0, grad1, grad2, swap(grad2, "ctx", 1))
    *shares, dattn = weight_shares(place, out, grads, weights)

    place, dattn, *shares = tie((place, dattn, *shares))
    crossed.append(swap(window[1], "ctx", 2))
    swapped = [swap(shares[step], "ctx", step * 16) for step in range(1, GROUP)]
    backs = full_grads(place, pieces, dattn, out, inverses, raised_low)

    place, backs, swapped, crossed, window = tie((place, backs, swapped, crossed, window))
    parts = [backs[0]] + [swap(backs[step], "ctx", step) for step in range(1, GROUP)]
    crossed.append(swap(window[2], "ctx", 2))
    sibling = [swap(array, "ctx", 1) for array in window]
    opposite = [swap(array, "ctx", 1) for array in crossed]
    rows = total([shares[0], *swapped]).reshape(GROUP, HEAD_DIM // GROUP, D).astype(BF)
    rows = [lax.dynamic_index_in_dim(rows, across ^ step, 0, keepdims=False) for step in range(GROUP)]
    summed = [rows[0]] + [swap(rows[step], "dp", step) for step in range(1, GROUP)]
    share = total(summed).astype(BF)
    sets = list(zip(window, sibling, crossed, opposite))
    tile_rows = first[0].shape[0] // 3

    def deal(which):
        other, start = (1, which * tile_rows) if which < 2 else (2, 0)
        starts = (which * tile_rows, start)
        return deal_tiles(place, tile_perm[0], tile_counts[0], sets[0], sets[other], starts)[None]

    dealt = [deal(0), deal(1)]
    place, share, parts, opposite, dealt = tie((place, share, parts, opposite, dealt))
    sets = list(zip(window, sibling, crossed, opposite))
    shared = [lax.ppermute(share, ("dp", "ctx"), share_route(GROUP, step)) for step in range(GROUP)]
    dealt.append(deal(2))
    full = join_heads(place, parts, cos, sin)
    return (*dealt, *[array[None] for array in full], total(shared))


def solution(mesh):
    rows = P("dp", "ctx", None)
    in_specs = (rows,) * 8 + (P("ctx", None), P(None, "dp", "ctx"), P("dp", None, None), P("dp", None, None))
    out_specs = (rows,) * 6 + (P("ctx", None),)
    return jax.shard_map(shards, mesh=mesh, in_specs=in_specs, out_specs=out_specs, check_vma=False)
```

time: 713 us -> 177 us (0.25)
  the two profiles are of different devices: /device:TPU:1 before, /device:TPU:41 now
where the time goes in v1:
time: 177 us; the launch traced here: 176 us
  Pallas kernels  71.3 us (40%)
  starting transfers between devices  54.9 us (31%)
  waiting for transfers between devices  40.7 us (23%)
  other arithmetic  5.04 us (3%)
  local copies, waits for them, and re-layouts  3.24 us (2%)
    ppermute x30, waiting for transfers between devices, swap(): return lax.ppermute(array, axis, [(i, i ^ distance) for i in range(count)])  35 us
    ppermute x30, starting transfers between devices, swap(): return lax.ppermute(array, axis, [(i, i ^ distance) for i in range(count)])  30.7 us
    ppermute x4, starting transfers between devices, shards(): lax.ppermute(share, ('dp', 'ctx'), share_route(GROUP, step))  18.4 us
    pallas_call x2, Pallas kernels, window_grads(): pl.pallas_call(window_kernel, grid=(1,), out_shape=[jax.ShapeDtypeStruct(...  15.9 us
    pallas_call x1, Pallas kernels, full_grads(): pl.pallas_call(grads_kernel, grid=(HEADS // GROUP,), out_shape=[jax.Shape...  15.4 us
    pallas_call x1, Pallas kernels, full_probs(): pl.pallas_call(probs_kernel, grid=(heads,), out_shape=[jax.ShapeDtypeStru...  15.1 us
    pallas_call x3, Pallas kernels, deal_tiles(): pl.pallas_call(functools.partial(deal_kernel, starts), out_shape=jax.Shap...  12.6 us
    ppermute x1, starting transfers between devices, shards(): corner = lax.ppermute(proj_weight, ('dp', 'ctx'), gather_route(GROUP))  5.72 us
  transfers between devices with their start and end apart: 35, of which 9 were waited for; matrix products, arithmetic and copies ran while one was open for 2% of the time, Pallas kernels for 38%

profile of v1, /device:TPU:41, one launch (start us, length us, event | category | flops | bytes accessed | tf_op | source)
XLA Modules:
  0.0 176.3 jit_solution(14685351585888616838)
XLA Ops:
  0.7 0.7 slice_convert_fusion.1
  1.5 0.8 fusion.3
  2.3 0.6 pad_add_fusion.place.refs_0_
  2.9 3.6 %split_heads.1 = (bf16[960,256]{1,0:T(8,128)(2,1)}, bf16[960,256]{1,0:T(8,128)(2,1)}, bf16[960,256]{1,0:T(8,128)(2,1)}, bf16[960,256]{1,0:T(8,128)(2,1)}) custom-call(s32[3]{0:T(128)} %pad_add_fusion.place.refs_0_, bf16[256,1280]{1,0:T(8,128)(2,1)} %bitcast.44, bf16[256,1280]{1,0:T(8,128)(2,1)} %bitcast.45, bf16[256,1280]{1,0:T(8,128)(2,1)} %bitcast.46, ...), custom_call_target="tpu_custom_call" | custom-call | flops 100000 | bytes 100000 | tf_op jit(solution)/shard_map/split_heads/pallas_call | solution.py:80
  6.5 0.7 collective-permute-start.1
  7.2 5.7 %collective-permute-start = (bf16[20,1280]{1,0:T(8,128)(2,1)S(1)}, bf16[20,1280]{1,0:T(8,128)(2,1)S(1)}, u32[]{:S(2)}, u32[]{:S(2)}) collective-permute-start(bf16[20,1280]{1,0:T(8,128)(2,1)S(1)} %copy-done.26), channel_id=1, source_target_pairs={{0,0},{4,1},{8,2},{12,3},{64,4},{68,5},{72,6},{76,7},{128,8},{132,... | collective-permute-start | bytes 153608 | tf_op jit(solution)/shard_map/ppermute | solution.py:371
  12.9 8.0 %window_grads.2.refs_0_ = bf16[768,640]{1,0:T(8,128)(2,1)} custom-call(s32[3]{0:T(128)} %pad_add_fusion.place.refs_0_, bf16[256,1280]{1,0:T(8,128)(2,1)} %bitcast.30, bf16[256,1280]{1,0:T(8,128)(2,1)} %bitcast.32, bf16[256,1280]{1,0:T(8,128)(2,1)} %bitcast.34, bf16[256,1280]{1,0:T(8,128)(2,1)} %bitcast.36, f32[40,256]{1,0:T(8,128)} %get-tuple-element.181.cos_ref, ...), custom_call_target="tpu_custom_call" | custom-call | flops 100000 | bytes 100000 | tf_op jit(solution)/shard_map/window_grads/pallas_call | solution.py:130
  20.9 5.7 %collective-permute-done = bf16[20,1280]{1,0:T(8,128)(2,1)S(1)} collective-permute-done((bf16[20,1280]{1,0:T(8,128)(2,1)S(1)}, bf16[20,1280]{1,0:T(8,128)(2,1)S(1)}, u32[]{:S(2)}, u32[]{:S(2)}) %collective-permute-start) | collective-permute-done | bytes 51232 | tf_op jit(solution)/shard_map/ppermute | solution.py:371
  26.7 0.9 collective-permute-start.4
  27.8 2.8 %collective-permute-start.6 = (bf16[20,1280]{1,0:T(8,128)(2,1)S(1)}, bf16[20,1280]{1,0:T(8,128)(2,1)S(1)}, u32[]{:S(2)}, u32[]{:S(2)}) collective-permute-start(bf16[20,1280]{1,0:T(8,128)(2,1)S(1)} %collective-permute-done), channel_id=1, source_target_pairs={{0,192},{64,128},{128,64},{192,0},{1,193},{65,129},{129,65},{193,1... | collective-permute-start | bytes 153608 | tf_op jit(solution)/shard_map/ppermute | solution.py:322
  30.7 7.9 %window_grads.3 = (bf16[512,640]{1,0:T(8,128)(2,1)}, bf16[256,640]{1,0:T(8,128)(2,1)}) custom-call(s32[3]{0:T(128)} %pad_add_fusion.place.refs_0_, bf16[256,1280]{1,0:T(8,128)(2,1)} %bitcast.31, bf16[256,1280]{1,0:T(8,128)(2,1)} %bitcast.33, bf16[256,1280]{1,0:T(8,128)(2,1)} %bitcast.35, bf16[256,1280]{1,0:T(8,128)(2,1)} %bitcast.37, ...), custom_call_target="tpu_custom_call" | custom-call | flops 100000 | bytes 100000 | tf_op jit(solution)/shard_map/window_grads/pallas_call | solution.py:130
  38.7 1.0 collective-permute-start.7
  39.7 1.7 collective-permute-start.8
  41.5 2.1 %collective-permute-start.10 = (bf16[80,1280]{1,0:T(8,128)(2,1)S(1)}, bf16[80,1280]{1,0:T(8,128)(2,1)S(1)}, u32[]{:S(2)}, u32[]{:S(2)}) collective-permute-start(bf16[80,1280]{1,0:T(8,128)(2,1)S(1)} %pad_maximum_fusion.refs_6_), channel_id=1, source_target_pairs={{0,32},{1,33},{2,34},{3,35},{4,36},{5,37},{6,38},{7,39},{8,40},{9,... | collective-permute-start | bytes 614408 | tf_op jit(solution)/shard_map/ppermute | solution.py:322
  43.6 1.8 %collective-permute-start.9 = (bf16[80,1280]{1,0:T(8,128)(2,1)S(1)}, bf16[80,1280]{1,0:T(8,128)(2,1)S(1)}, u32[]{:S(2)}, u32[]{:S(2)}) collective-permute-start(bf16[80,1280]{1,0:T(8,128)(2,1)S(1)} %pad_maximum_fusion.refs_6_), channel_id=1, source_target_pairs={{0,16},{1,17},{2,18},{3,19},{4,20},{5,21},{6,22},{7,23},{8,24},{9,... | collective-permute-start | bytes 614408 | tf_op jit(solution)/shard_map/ppermute | solution.py:322
  45.4 15.1 %full_probs.1 = (bf16[4,1024,1024]{2,1,0:T(8,128)(2,1)}, f32[320,1024]{1,0:T(8,128)}, f32[4,1,1024]{2,1,0:T(1,128)}) custom-call(s32[3]{0:T(128)} %pad_add_fusion.place.refs_0_, bf16[960,256]{1,0:T(8,128)(2,1)} %get-tuple-element.105.piece0.refs_1_, bf16[960,256]{1,0:T(8,128)(2,1)} %copy-done.4, bf16[960,256]{1,0:T(8,128)(2,1)} %copy-done.5, ...), custom_call_target="tpu_custom_call" | custom-call | flops 100000 | bytes 100000 | tf_op jit(solution)/shard_map/full_probs/pallas_call | solution.py:169
  60.8 1.3 collective-permute-start.12
  62.1 1.6 collective-permute-start.17
  63.8 0.8 copy-done.11
  64.7 5.3 %weight_shares.1 = (bf16[80,1280]{1,0:T(8,128)(2,1)}, bf16[80,1280]{1,0:T(8,128)(2,1)}, bf16[80,1280]{1,0:T(8,128)(2,1)}, bf16[80,1280]{1,0:T(8,128)(2,1)}, bf16[320,1024]{1,0:T(8,128)(2,1)}) custom-call(s32[3]{0:T(128)} %pad_add_fusion.place.refs_0_, f32[320,1024]{1,0:T(8,128)} %get-tuple-element.120.refs_1_.refs_6_, bf16[256,1280]{1,0:T(8,128)(2,1)} %bitcast.41, ...), custom_call_target="tpu_custom_call" | custom-call | flops 100000 | bytes 100000 | tf_op jit(solution)/shard_map/weight_shares/pallas_call | solution.py:202
  70.0 2.5 %collective-permute-start.14 = (bf16[80,1280]{1,0:T(8,128)(2,1)}, bf16[80,1280]{1,0:T(8,128)(2,1)S(1)}, u32[]{:S(2)}, u32[]{:S(2)}) collective-permute-start(bf16[80,1280]{1,0:T(8,128)(2,1)} %get-tuple-element.141), channel_id=1, source_target_pairs={{0,32},{1,33},{2,34},{3,35},{4,36},{5,37},{6,38},{7,39},{8,40},{9,... | collective-permute-start | bytes 614408 | tf_op jit(solution)/shard_map/ppermute | solution.py:322
  72.6 15.4 %full_grads.1 = (bf16[960,256]{1,0:T(8,128)(2,1)}, bf16[960,256]{1,0:T(8,128)(2,1)}, bf16[960,256]{1,0:T(8,128)(2,1)}, bf16[960,256]{1,0:T(8,128)(2,1)}) custom-call(s32[3]{0:T(128)} %pad_add_fusion.place.refs_0_, bf16[960,256]{1,0:T(8,128)(2,1)} %get-tuple-element.105.piece0.refs_1_, bf16[960,256]{1,0:T(8,128)(2,1)} %copy-done.4, ...), custom_call_target="tpu_custom_call" | custom-call | flops 100000 | bytes 100000 | tf_op jit(solution)/shard_map/full_grads/pallas_call | solution.py:240
  88.0 8.8 %collective-permute-done.17.refs_6_ = bf16[512,640]{1,0:T(8,128)(2,1)S(1)} collective-permute-done((bf16[512,640]{1,0:T(8,128)(2,1)}, bf16[512,640]{1,0:T(8,128)(2,1)S(1)}, u32[]{:S(2)}, u32[]{:S(2)}) %collective-permute-start.17) | collective-permute-done | bytes 655392 | tf_op jit(solution)/shard_map/ppermute | solution.py:322
  96.9 0.8 copy-done.3
  97.8 2.1 %collective-permute-start.24 = (bf16[768,640]{1,0:T(8,128)(2,1)S(1)}, bf16[768,640]{1,0:T(8,128)(2,1)S(1)}, u32[]{:S(2)}, u32[]{:S(2)}) collective-permute-start(bf16[768,640]{1,0:T(8,128)(2,1)S(1)} %collective-permute-done.16.refs_2_), channel_id=1, source_target_pairs={{0,1},{1,0},{2,3},{3,2},{4,5},{5,4},{6,7},{7,6},{8,9},{9,8},{10,11... | collective-permute-start | bytes 2949128 | tf_op jit(solution)/shard_map/ppermute | solution.py:322
  99.9 0.5 collective-permute-start.25
  100.4 1.1 add_convert_fusion
  101.9 3.1 %collective-permute-done.18 = bf16[20,1280]{1,0:T(8,128)(2,1)S(1)} collective-permute-done((bf16[20,1280]{1,0:T(8,128)(2,1)S(1)}, bf16[20,1280]{1,0:T(8,128)(2,1)S(1)}, u32[]{:S(2)}, u32[]{:S(2)}) %collective-permute-start.18) | collective-permute-done | bytes 51232 | tf_op jit(solution)/shard_map/ppermute | solution.py:322
  105.0 1.5 collective-permute-start.19
  106.5 3.1 %collective-permute-done.19 = bf16[20,1280]{1,0:T(8,128)(2,1)S(1)} collective-permute-done((bf16[20,1280]{1,0:T(8,128)(2,1)S(1)}, bf16[20,1280]{1,0:T(8,128)(2,1)S(1)}, u32[]{:S(2)}, u32[]{:S(2)}) %collective-permute-start.19) | collective-permute-done | bytes 51232 | tf_op jit(solution)/shard_map/ppermute | solution.py:322
  109.6 1.8 %collective-permute-start.20 = (bf16[20,1280]{1,0:T(8,128)(2,1)S(1)}, bf16[20,1280]{1,0:T(8,128)(2,1)S(1)}, u32[]{:S(2)}, u32[]{:S(2)}) collective-permute-start(bf16[20,1280]{1,0:T(8,128)(2,1)S(1)} %get-tuple-element.174), channel_id=1, source_target_pairs={{0,192},{64,128},{128,64},{192,0},{1,193},{65,129},{129,65},{193,1... | collective-permute-start | bytes 153608 | tf_op jit(solution)/shard_map/ppermute | solution.py:322
  111.4 2.5 %collective-permute-done.20 = bf16[20,1280]{1,0:T(8,128)(2,1)S(1)} collective-permute-done((bf16[20,1280]{1,0:T(8,128)(2,1)S(1)}, bf16[20,1280]{1,0:T(8,128)(2,1)S(1)}, u32[]{:S(2)}, u32[]{:S(2)}) %collective-permute-start.20) | collective-permute-done | bytes 51232 | tf_op jit(solution)/shard_map/ppermute | solution.py:322
  114.0 6.1 %collective-permute-done.26.refs_6_ = bf16[256,640]{1,0:T(8,128)(2,1)S(1)} collective-permute-done((bf16[256,640]{1,0:T(8,128)(2,1)}, bf16[256,640]{1,0:T(8,128)(2,1)S(1)}, u32[]{:S(2)}, u32[]{:S(2)}) %collective-permute-start.26) | collective-permute-done | bytes 327712 | tf_op jit(solution)/shard_map/ppermute | solution.py:322
  120.0 5.1 %collective-permute-start.21 = (bf16[960,256]{1,0:T(8,128)(2,1)}, bf16[960,256]{1,0:T(8,128)(2,1)}, u32[]{:S(2)}, u32[]{:S(2)}) collective-permute-start(bf16[960,256]{1,0:T(8,128)(2,1)} %get-tuple-element.152), channel_id=1, source_target_pairs={{0,1},{1,0},{2,3},{3,2},{4,5},{5,4},{6,7},{7,6},{8,9},{9,8},{10,11... | collective-permute-start | bytes 1474568 | tf_op jit(solution)/shard_map/ppermute | solution.py:322
  125.2 1.6 collective-permute-start.23
  126.9 0.7 copy.22.counts
  128.1 0.9 fusion.2
  129.0 4.3 %deal_tiles.4 = bf16[512,1280]{1,0:T(8,128)(2,1)} custom-call(s32[3]{0:T(128)} %pad_add_fusion.place.refs_0_, s32[16,16]{1,0:T(8,128)} %bitcast.47, s32[16,4]{1,0:T(8,128)} %copy.22.counts, bf16[768,640]{1,0:T(8,128)(2,1)} %window_grads.2.refs_0_, bf16[768,640]{1,0:T(8,128)(2,1)} %collective-permute-done.28.refs_1_, bf16[768,640]{1,0:T(8,128)(2,1)} %copy-done.1, ...), custom_call_target="tpu_custom_call" | custom-call | flops 100000 | bytes 100000 | tf_op jit(solution)/shard_map/deal_tiles/pallas_call | solution.py:309
  133.3 4.3 %deal_tiles.3 = bf16[512,1280]{1,0:T(8,128)(2,1)} custom-call(s32[3]{0:T(128)} %pad_add_fusion.place.refs_0_, s32[16,16]{1,0:T(8,128)} %bitcast.48, s32[16,4]{1,0:T(8,128)} %copy.22.counts, bf16[768,640]{1,0:T(8,128)(2,1)} %window_grads.2.refs_0_, bf16[768,640]{1,0:T(8,128)(2,1)} %collective-permute-done.28.refs_1_, bf16[768,640]{1,0:T(8,128)(2,1)} %copy-done.1, ...), custom_call_target="tpu_custom_call" | custom-call | flops 100000 | bytes 100000 | tf_op jit(solution)/shard_map/deal_tiles/pallas_call | solution.py:309
  137.7 0.7 collective-permute-done.22.part2
  138.4 10.6 %collective-permute-done.23.part3 = bf16[960,256]{1,0:T(8,128)(2,1)} collective-permute-done((bf16[960,256]{1,0:T(8,128)(2,1)}, bf16[960,256]{1,0:T(8,128)(2,1)}, u32[]{:S(2)}, u32[]{:S(2)}) %collective-permute-start.23) | collective-permute-done | bytes 491552 | tf_op jit(solution)/shard_map/ppermute | solution.py:322
  149.0 8.1 %collective-permute-start.31 = (bf16[20,1280]{1,0:T(8,128)(2,1)S(1)}, bf16[20,1280]{1,0:T(8,128)(2,1)S(1)}, u32[]{:S(2)}, u32[]{:S(2)}) collective-permute-start(bf16[20,1280]{1,0:T(8,128)(2,1)S(1)} %fusion.2), channel_id=1, source_target_pairs={{0,0},{1,4},{2,8},{3,12},{4,64},{5,68},{6,72},{7,76},{8,128},{9,13... | collective-permute-start | bytes 153608 | tf_op jit(solution)/shard_map/ppermute | solution.py:427
  157.3 6.2 %collective-permute-start.33 = (bf16[20,1280]{1,0:T(8,128)(2,1)S(1)}, bf16[20,1280]{1,0:T(8,128)(2,1)S(1)}, u32[]{:S(2)}, u32[]{:S(2)}) collective-permute-start(bf16[20,1280]{1,0:T(8,128)(2,1)S(1)} %fusion.2), channel_id=1, source_target_pairs={{0,128},{1,132},{2,136},{3,140},{4,192},{5,196},{6,200},{7,204},{8... | collective-permute-start | bytes 153608 | tf_op jit(solution)/shard_map/ppermute | solution.py:427
  163.6 3.9 %collective-permute-start.34 = (bf16[20,1280]{1,0:T(8,128)(2,1)S(1)}, bf16[20,1280]{1,0:T(8,128)(2,1)S(1)}, u32[]{:S(2)}, u32[]{:S(2)}) collective-permute-start(bf16[20,1280]{1,0:T(8,128)(2,1)S(1)} %fusion.2), channel_id=1, source_target_pairs={{0,192},{1,196},{2,200},{3,204},{4,128},{5,132},{6,136},{7,140},{8... | collective-permute-start | bytes 153608 | tf_op jit(solution)/shard_map/ppermute | solution.py:427
  167.5 3.5 %join_heads.1 = (bf16[256,1280]{1,0:T(8,128)(2,1)}, bf16[256,1280]{1,0:T(8,128)(2,1)}, bf16[256,1280]{1,0:T(8,128)(2,1)}) custom-call(s32[3]{0:T(128)} %pad_add_fusion.place.refs_0_, bf16[960,256]{1,0:T(8,128)(2,1)} %get-tuple-element.165.part0, bf16[960,256]{1,0:T(8,128)(2,1)} %collective-permute-done.21.part1, ...), custom_call_target="tpu_custom_call" | custom-call | flops 100000 | bytes 100000 | tf_op jit(solution)/shard_map/join_heads/pallas_call | solution.py:269
  170.9 0.7 copy-done.13
  171.6 3.9 %deal_tiles.5 = bf16[512,1280]{1,0:T(8,128)(2,1)} custom-call(s32[3]{0:T(128)} %pad_add_fusion.place.refs_0_, s32[16,16]{1,0:T(8,128)} %bitcast.49, s32[16,4]{1,0:T(8,128)} %copy.22.counts, bf16[768,640]{1,0:T(8,128)(2,1)} %window_grads.2.refs_0_, bf16[768,640]{1,0:T(8,128)(2,1)} %collective-permute-done.28.refs_1_, bf16[768,640]{1,0:T(8,128)(2,1)} %copy-done.1, ...), custom_call_target="tpu_custom_call" | custom-call | flops 100000 | bytes 100000 | tf_op jit(solution)/shard_map/deal_tiles/pallas_call | solution.py:309
  175.6 0.7 convert_add_fusion.1
  (99 shorter events, 2.3 us)
Async XLA Ops:
  6.5 20.1 %collective-permute-start.1 = (bf16[960,256]{1,0:T(8,128)(2,1)}, bf16[960,256]{1,0:T(8,128)(2,1)S(1)}, u32[]{:S(2)}, u32[]{:S(2)}) collective-permute-start(bf16[960,256]{1,0:T(8,128)(2,1)} %get-tuple-element.95), channel_id=1, source_target_pairs={{0,1},{1,0},{2,3},{3,2},{4,5},{5,4},{6,7},{7,6},{8,9},{9,8},{10,11... | collective-permute-start | bytes 1474568 | tf_op jit(solution)/shard_map/ppermute | solution.py:322
  7.2 19.4 %collective-permute-start.2 = (bf16[960,256]{1,0:T(8,128)(2,1)}, bf16[960,256]{1,0:T(8,128)(2,1)S(1)}, u32[]{:S(2)}, u32[]{:S(2)}) collective-permute-start(bf16[960,256]{1,0:T(8,128)(2,1)} %get-tuple-element.96), channel_id=1, source_target_pairs={{0,2},{1,3},{2,0},{3,1},{4,6},{5,7},{6,4},{7,5},{8,10},{9,11},{10,... | collective-permute-start | bytes 1474568 | tf_op jit(solution)/shard_map/ppermute | solution.py:322
  7.2 19.4 %collective-permute-start = (bf16[20,1280]{1,0:T(8,128)(2,1)S(1)}, bf16[20,1280]{1,0:T(8,128)(2,1)S(1)}, u32[]{:S(2)}, u32[]{:S(2)}) collective-permute-start(bf16[20,1280]{1,0:T(8,128)(2,1)S(1)} %copy-done.26), channel_id=1, source_target_pairs={{0,0},{4,1},{8,2},{12,3},{64,4},{68,5},{72,6},{76,7},{128,8},{132,... | collective-permute-start | bytes 153608 | tf_op jit(solution)/shard_map/ppermute | solution.py:371
  12.9 13.7 %copy-start.25 = (bf16[960,256]{1,0:T(8,128)(2,1)S(1)}, bf16[960,256]{1,0:T(8,128)(2,1)}, u32[]{:S(2)}) copy-start(bf16[960,256]{1,0:T(8,128)(2,1)} %get-tuple-element.102) | copy-start | bytes 1474564
  26.6 12.0 %copy-start.4 = (bf16[960,256]{1,0:T(8,128)(2,1)}, bf16[960,256]{1,0:T(8,128)(2,1)S(1)}, u32[]{:S(2)}) copy-start(bf16[960,256]{1,0:T(8,128)(2,1)S(1)} %collective-permute-done.1.piece1.refs_2_) | copy-start | bytes 1474564
  26.6 12.0 %copy-start.5 = (bf16[960,256]{1,0:T(8,128)(2,1)}, bf16[960,256]{1,0:T(8,128)(2,1)S(1)}, u32[]{:S(2)}) copy-start(bf16[960,256]{1,0:T(8,128)(2,1)S(1)} %collective-permute-done.2.piece2.refs_3_) | copy-start | bytes 1474564
  26.6 12.0 %collective-permute-start.3 = (bf16[960,256]{1,0:T(8,128)(2,1)S(1)}, bf16[960,256]{1,0:T(8,128)(2,1)S(1)}, u32[]{:S(2)}, u32[]{:S(2)}) collective-permute-start(bf16[960,256]{1,0:T(8,128)(2,1)S(1)} %copy-done.25), channel_id=1, source_target_pairs={{0,3},{1,2},{2,1},{3,0},{4,7},{5,6},{6,5},{7,4},{8,11},{9,10},{10,... | collective-permute-start | bytes 1474568 | tf_op jit(solution)/shard_map/ppermute | solution.py:322
  26.7 11.9 %collective-permute-start.4 = (bf16[20,1280]{1,0:T(8,128)(2,1)S(1)}, bf16[20,1280]{1,0:T(8,128)(2,1)S(1)}, u32[]{:S(2)}, u32[]{:S(2)}) collective-permute-start(bf16[20,1280]{1,0:T(8,128)(2,1)S(1)} %collective-permute-done), channel_id=1, source_target_pairs={{0,64},{64,0},{128,192},{192,128},{1,65},{65,1},{129,193},{193,129... | collective-permute-start | bytes 153608 | tf_op jit(solution)/shard_map/ppermute | solution.py:322
  27.7 10.9 %collective-permute-start.5 = (bf16[20,1280]{1,0:T(8,128)(2,1)S(1)}, bf16[20,1280]{1,0:T(8,128)(2,1)S(1)}, u32[]{:S(2)}, u32[]{:S(2)}) collective-permute-start(bf16[20,1280]{1,0:T(8,128)(2,1)S(1)} %collective-permute-done), channel_id=1, source_target_pairs={{0,128},{64,192},{128,0},{192,64},{1,129},{65,193},{129,1},{193,65... | collective-permute-start | bytes 153608 | tf_op jit(solution)/shard_map/ppermute | solution.py:322
  27.8 10.8 %collective-permute-start.6 = (bf16[20,1280]{1,0:T(8,128)(2,1)S(1)}, bf16[20,1280]{1,0:T(8,128)(2,1)S(1)}, u32[]{:S(2)}, u32[]{:S(2)}) collective-permute-start(bf16[20,1280]{1,0:T(8,128)(2,1)S(1)} %collective-permute-done), channel_id=1, source_target_pairs={{0,192},{64,128},{128,64},{192,0},{1,193},{65,129},{129,65},{193,1... | collective-permute-start | bytes 153608 | tf_op jit(solution)/shard_map/ppermute | solution.py:322
  38.7 22.0 %collective-permute-start.7 = (bf16[256,1280]{1,0:T(8,128)(2,1)S(1)}, bf16[256,1280]{1,0:T(8,128)(2,1)S(1)}, u32[]{:S(2)}, u32[]{:S(2)}) collective-permute-start(bf16[256,1280]{1,0:T(8,128)(2,1)S(1)} %bitcast.42), channel_id=1, source_target_pairs={{0,1},{1,0},{2,3},{3,2},{4,5},{5,4},{6,7},{7,6},{8,9},{9,8},{10,11... | collective-permute-start | bytes 1966088 | tf_op jit(solution)/shard_map/ppermute | solution.py:322
  39.7 21.0 %collective-permute-start.8 = (bf16[256,1280]{1,0:T(8,128)(2,1)S(1)}, bf16[256,1280]{1,0:T(8,128)(2,1)S(1)}, u32[]{:S(2)}, u32[]{:S(2)}) collective-permute-start(bf16[256,1280]{1,0:T(8,128)(2,1)S(1)} %bitcast.43), channel_id=1, source_target_pairs={{0,2},{1,3},{2,0},{3,1},{4,6},{5,7},{6,4},{7,5},{8,10},{9,11},{10,... | collective-permute-start | bytes 1966088 | tf_op jit(solution)/shard_map/ppermute | solution.py:322
  41.4 19.3 %copy-start = (bf16[768,640]{1,0:T(8,128)(2,1)S(1)}, bf16[768,640]{1,0:T(8,128)(2,1)}, u32[]{:S(2)}) copy-start(bf16[768,640]{1,0:T(8,128)(2,1)} %window_grads.2.refs_0_) | copy-start | bytes 2949124
  41.5 22.3 %copy-start.7 = (bf16[80,1280]{1,0:T(8,128)(2,1)}, bf16[80,1280]{1,0:T(8,128)(2,1)S(1)}, u32[]{:S(2)}) copy-start(bf16[80,1280]{1,0:T(8,128)(2,1)S(1)} %pad_maximum_fusion.refs_6_) | copy-start | bytes 614404
  41.5 19.1 %collective-permute-start.10 = (bf16[80,1280]{1,0:T(8,128)(2,1)S(1)}, bf16[80,1280]{1,0:T(8,128)(2,1)S(1)}, u32[]{:S(2)}, u32[]{:S(2)}) collective-permute-start(bf16[80,1280]{1,0:T(8,128)(2,1)S(1)} %pad_maximum_fusion.refs_6_), channel_id=1, source_target_pairs={{0,32},{1,33},{2,34},{3,35},{4,36},{5,37},{6,38},{7,39},{8,40},{9,... | collective-permute-start | bytes 614408 | tf_op jit(solution)/shard_map/ppermute | solution.py:322
  43.6 17.0 %collective-permute-start.11 = (bf16[80,1280]{1,0:T(8,128)(2,1)S(1)}, bf16[80,1280]{1,0:T(8,128)(2,1)S(1)}, u32[]{:S(2)}, u32[]{:S(2)}) collective-permute-start(bf16[80,1280]{1,0:T(8,128)(2,1)S(1)} %pad_maximum_fusion.refs_6_), channel_id=1, source_target_pairs={{0,48},{1,49},{2,50},{3,51},{4,52},{5,53},{6,54},{7,55},{8,56},{9,... | collective-permute-start | bytes 614408 | tf_op jit(solution)/shard_map/ppermute | solution.py:322
  43.6 17.0 %collective-permute-start.9 = (bf16[80,1280]{1,0:T(8,128)(2,1)S(1)}, bf16[80,1280]{1,0:T(8,128)(2,1)S(1)}, u32[]{:S(2)}, u32[]{:S(2)}) collective-permute-start(bf16[80,1280]{1,0:T(8,128)(2,1)S(1)} %pad_maximum_fusion.refs_6_), channel_id=1, source_target_pairs={{0,16},{1,17},{2,18},{3,19},{4,20},{5,21},{6,22},{7,23},{8,24},{9,... | collective-permute-start | bytes 614408 | tf_op jit(solution)/shard_map/ppermute | solution.py:322
  60.7 36.2 %collective-permute-start.16 = (bf16[768,640]{1,0:T(8,128)(2,1)S(1)}, bf16[768,640]{1,0:T(8,128)(2,1)S(1)}, u32[]{:S(2)}, u32[]{:S(2)}) collective-permute-start(bf16[768,640]{1,0:T(8,128)(2,1)S(1)} %copy-done), channel_id=1, source_target_pairs={{0,2},{1,3},{2,0},{3,1},{4,6},{5,7},{6,4},{7,5},{8,10},{9,11},{10,... | collective-permute-start | bytes 2949128 | tf_op jit(solution)/shard_map/ppermute | solution.py:322
  60.8 3.0 %collective-permute-start.12 = (bf16[256,1280]{1,0:T(8,128)(2,1)S(1)}, bf16[256,1280]{1,0:T(8,128)(2,1)S(1)}, u32[]{:S(2)}, u32[]{:S(2)}) collective-permute-start(bf16[256,1280]{1,0:T(8,128)(2,1)S(1)} %collective-permute-done.8.refs_4_), channel_id=1, source_target_pairs={{0,1},{1,0},{2,3},{3,2},{4,5},{5,4},{6,7},{7,6},{8,9},{9,8},{10,11... | collective-permute-start | bytes 1966088 | tf_op jit(solution)/shard_map/ppermute | solution.py:322
  62.1 34.8 %collective-permute-start.17 = (bf16[512,640]{1,0:T(8,128)(2,1)}, bf16[512,640]{1,0:T(8,128)(2,1)S(1)}, u32[]{:S(2)}, u32[]{:S(2)}) collective-permute-start(bf16[512,640]{1,0:T(8,128)(2,1)} %get-tuple-element.159.refs_4_), channel_id=1, source_target_pairs={{0,2},{1,3},{2,0},{3,1},{4,6},{5,7},{6,4},{7,5},{8,10},{9,11},{10,... | collective-permute-start | bytes 1966088 | tf_op jit(solution)/shard_map/ppermute | solution.py:322
  70.0 26.9 %collective-permute-start.13 = (bf16[80,1280]{1,0:T(8,128)(2,1)}, bf16[80,1280]{1,0:T(8,128)(2,1)S(1)}, u32[]{:S(2)}, u32[]{:S(2)}) collective-permute-start(bf16[80,1280]{1,0:T(8,128)(2,1)} %get-tuple-element.140), channel_id=1, source_target_pairs={{0,16},{1,17},{2,18},{3,19},{4,20},{5,21},{6,22},{7,23},{8,24},{9,... | collective-permute-start | bytes 614408 | tf_op jit(solution)/shard_map/ppermute | solution.py:322
  70.0 26.9 %collective-permute-start.14 = (bf16[80,1280]{1,0:T(8,128)(2,1)}, bf16[80,1280]{1,0:T(8,128)(2,1)S(1)}, u32[]{:S(2)}, u32[]{:S(2)}) collective-permute-start(bf16[80,1280]{1,0:T(8,128)(2,1)} %get-tuple-element.141), channel_id=1, source_target_pairs={{0,32},{1,33},{2,34},{3,35},{4,36},{5,37},{6,38},{7,39},{8,40},{9,... | collective-permute-start | bytes 614408 | tf_op jit(solution)/shard_map/ppermute | solution.py:322
  72.5 24.4 %collective-permute-start.15 = (bf16[80,1280]{1,0:T(8,128)(2,1)}, bf16[80,1280]{1,0:T(8,128)(2,1)S(1)}, u32[]{:S(2)}, u32[]{:S(2)}) collective-permute-start(bf16[80,1280]{1,0:T(8,128)(2,1)} %get-tuple-element.142), channel_id=1, source_target_pairs={{0,48},{1,49},{2,50},{3,51},{4,52},{5,53},{6,54},{7,55},{8,56},{9,... | collective-permute-start | bytes 614408 | tf_op jit(solution)/shard_map/ppermute | solution.py:322
  72.6 27.8 %copy-start.15 = (bf16[80,1280]{1,0:T(8,128)(2,1)S(1)}, bf16[80,1280]{1,0:T(8,128)(2,1)}, u32[]{:S(2)}) copy-start(bf16[80,1280]{1,0:T(8,128)(2,1)} %get-tuple-element.147) | copy-start | bytes 614404
  88.0 38.9 %copy-start.24 = (s32[1,16,4]{1,2,0:T(4,128)S(1)}, s32[1,16,4]{1,2,0:T(4,128)}, u32[]{:S(2)}) copy-start(s32[1,16,4]{1,2,0:T(4,128)} %param.23) | copy-start | bytes 772
  96.9 32.1 %copy-start.1 = (bf16[768,640]{1,0:T(8,128)(2,1)}, bf16[768,640]{1,0:T(8,128)(2,1)S(1)}, u32[]{:S(2)}) copy-start(bf16[768,640]{1,0:T(8,128)(2,1)S(1)} %collective-permute-done.16.refs_2_) | copy-start | bytes 2949124
  97.8 29.8 %collective-permute-start.24 = (bf16[768,640]{1,0:T(8,128)(2,1)S(1)}, bf16[768,640]{1,0:T(8,128)(2,1)S(1)}, u32[]{:S(2)}, u32[]{:S(2)}) collective-permute-start(bf16[768,640]{1,0:T(8,128)(2,1)S(1)} %collective-permute-done.16.refs_2_), channel_id=1, source_target_pairs={{0,1},{1,0},{2,3},{3,2},{4,5},{5,4},{6,7},{7,6},{8,9},{9,8},{10,11... | collective-permute-start | bytes 2949128 | tf_op jit(solution)/shard_map/ppermute | solution.py:322
  99.9 27.9 %collective-permute-start.28 = (bf16[768,640]{1,0:T(8,128)(2,1)S(1)}, bf16[768,640]{1,0:T(8,128)(2,1)}, u32[]{:S(2)}, u32[]{:S(2)}) collective-permute-start(bf16[768,640]{1,0:T(8,128)(2,1)S(1)} %copy-done), channel_id=1, source_target_pairs={{0,1},{1,0},{2,3},{3,2},{4,5},{5,4},{6,7},{7,6},{8,9},{9,8},{10,11... | collective-permute-start | bytes 2949128 | tf_op jit(solution)/shard_map/ppermute | solution.py:322
  99.9 25.2 %collective-permute-start.25 = (bf16[512,640]{1,0:T(8,128)(2,1)}, bf16[512,640]{1,0:T(8,128)(2,1)}, u32[]{:S(2)}, u32[]{:S(2)}) collective-permute-start(bf16[512,640]{1,0:T(8,128)(2,1)} %copy-done.3), channel_id=1, source_target_pairs={{0,1},{1,0},{2,3},{3,2},{4,5},{5,4},{6,7},{7,6},{8,9},{9,8},{10,11... | collective-permute-start | bytes 1966088 | tf_op jit(solution)/shard_map/ppermute | solution.py:322
  100.4 24.8 %collective-permute-start.29 = (bf16[512,640]{1,0:T(8,128)(2,1)}, bf16[512,640]{1,0:T(8,128)(2,1)}, u32[]{:S(2)}, u32[]{:S(2)}) collective-permute-start(bf16[512,640]{1,0:T(8,128)(2,1)} %get-tuple-element.159.refs_4_), channel_id=1, source_target_pairs={{0,1},{1,0},{2,3},{3,2},{4,5},{5,4},{6,7},{7,6},{8,9},{9,8},{10,11... | collective-permute-start | bytes 1966088 | tf_op jit(solution)/shard_map/ppermute | solution.py:322
  101.6 3.4 %collective-permute-start.18 = (bf16[20,1280]{1,0:T(8,128)(2,1)S(1)}, bf16[20,1280]{1,0:T(8,128)(2,1)S(1)}, u32[]{:S(2)}, u32[]{:S(2)}) collective-permute-start(bf16[20,1280]{1,0:T(8,128)(2,1)S(1)} %get-tuple-element.173), channel_id=1, source_target_pairs={{0,64},{64,0},{128,192},{192,128},{1,65},{65,1},{129,193},{193,129... | collective-permute-start | bytes 153608 | tf_op jit(solution)/shard_map/ppermute | solution.py:322
  105.0 15.0 %copy-start.21 = (bf16[20,1280]{1,0:T(8,128)(2,1)}, bf16[20,1280]{1,0:T(8,128)(2,1)S(1)}, u32[]{:S(2)}) copy-start(bf16[20,1280]{1,0:T(8,128)(2,1)S(1)} %collective-permute-done.18) | copy-start | bytes 153604
  105.0 4.6 %collective-permute-start.19 = (bf16[20,1280]{1,0:T(8,128)(2,1)S(1)}, bf16[20,1280]{1,0:T(8,128)(2,1)S(1)}, u32[]{:S(2)}, u32[]{:S(2)}) collective-permute-start(bf16[20,1280]{1,0:T(8,128)(2,1)S(1)} %get-tuple-element.175), channel_id=1, source_target_pairs={{0,128},{64,192},{128,0},{192,64},{1,129},{65,193},{129,1},{193,65... | collective-permute-start | bytes 153608 | tf_op jit(solution)/shard_map/ppermute | solution.py:322
  109.6 15.5 %copy-start.22 = (bf16[20,1280]{1,0:T(8,128)(2,1)}, bf16[20,1280]{1,0:T(8,128)(2,1)S(1)}, u32[]{:S(2)}) copy-start(bf16[20,1280]{1,0:T(8,128)(2,1)S(1)} %collective-permute-done.19) | copy-start | bytes 153604
  109.6 4.3 %collective-permute-start.20 = (bf16[20,1280]{1,0:T(8,128)(2,1)S(1)}, bf16[20,1280]{1,0:T(8,128)(2,1)S(1)}, u32[]{:S(2)}, u32[]{:S(2)}) collective-permute-start(bf16[20,1280]{1,0:T(8,128)(2,1)S(1)} %get-tuple-element.174), channel_id=1, source_target_pairs={{0,192},{64,128},{128,64},{192,0},{1,193},{65,129},{129,65},{193,1... | collective-permute-start | bytes 153608 | tf_op jit(solution)/shard_map/ppermute | solution.py:322
  113.9 11.3 %copy-start.23 = (bf16[20,1280]{1,0:T(8,128)(2,1)}, bf16[20,1280]{1,0:T(8,128)(2,1)S(1)}, u32[]{:S(2)}) copy-start(bf16[20,1280]{1,0:T(8,128)(2,1)S(1)} %collective-permute-done.20) | copy-start | bytes 153604
  113.9 6.1 %collective-permute-start.26 = (bf16[256,640]{1,0:T(8,128)(2,1)}, bf16[256,640]{1,0:T(8,128)(2,1)S(1)}, u32[]{:S(2)}, u32[]{:S(2)}) collective-permute-start(bf16[256,640]{1,0:T(8,128)(2,1)} %get-tuple-element.157.refs_4_), channel_id=1, source_target_pairs={{0,2},{1,3},{2,0},{3,1},{4,6},{5,7},{6,4},{7,5},{8,10},{9,11},{10,... | collective-permute-start | bytes 983048 | tf_op jit(solution)/shard_map/ppermute | solution.py:322
  120.0 13.3 %copy-start.12 = (bf16[256,640]{1,0:T(8,128)(2,1)}, bf16[256,640]{1,0:T(8,128)(2,1)S(1)}, u32[]{:S(2)}) copy-start(bf16[256,640]{1,0:T(8,128)(2,1)S(1)} %collective-permute-done.26.refs_6_) | copy-start | bytes 983044
  120.0 17.7 %collective-permute-start.21 = (bf16[960,256]{1,0:T(8,128)(2,1)}, bf16[960,256]{1,0:T(8,128)(2,1)}, u32[]{:S(2)}, u32[]{:S(2)}) collective-permute-start(bf16[960,256]{1,0:T(8,128)(2,1)} %get-tuple-element.152), channel_id=1, source_target_pairs={{0,1},{1,0},{2,3},{3,2},{4,5},{5,4},{6,7},{7,6},{8,9},{9,8},{10,11... | collective-permute-start | bytes 1474568 | tf_op jit(solution)/shard_map/ppermute | solution.py:322
  125.1 13.2 %collective-permute-start.22 = (bf16[960,256]{1,0:T(8,128)(2,1)}, bf16[960,256]{1,0:T(8,128)(2,1)}, u32[]{:S(2)}, u32[]{:S(2)}) collective-permute-start(bf16[960,256]{1,0:T(8,128)(2,1)} %get-tuple-element.153), channel_id=1, source_target_pairs={{0,2},{1,3},{2,0},{3,1},{4,6},{5,7},{6,4},{7,5},{8,10},{9,11},{10,... | collective-permute-start | bytes 1474568 | tf_op jit(solution)/shard_map/ppermute | solution.py:322
  125.2 23.8 %collective-permute-start.23 = (bf16[960,256]{1,0:T(8,128)(2,1)}, bf16[960,256]{1,0:T(8,128)(2,1)}, u32[]{:S(2)}, u32[]{:S(2)}) collective-permute-start(bf16[960,256]{1,0:T(8,128)(2,1)} %get-tuple-element.154), channel_id=1, source_target_pairs={{0,3},{1,2},{2,1},{3,0},{4,7},{5,6},{6,5},{7,4},{8,11},{9,10},{10,... | collective-permute-start | bytes 1474568 | tf_op jit(solution)/shard_map/ppermute | solution.py:322
  127.5 43.4 %collective-permute-start.30 = (bf16[256,640]{1,0:T(8,128)(2,1)}, bf16[256,640]{1,0:T(8,128)(2,1)S(1)}, u32[]{:S(2)}, u32[]{:S(2)}) collective-permute-start(bf16[256,640]{1,0:T(8,128)(2,1)} %get-tuple-element.157.refs_4_), channel_id=1, source_target_pairs={{0,1},{1,0},{2,3},{3,2},{4,5},{5,4},{6,7},{7,6},{8,9},{9,8},{10,11... | collective-permute-start | bytes 983048 | tf_op jit(solution)/shard_map/ppermute | solution.py:322
  127.8 21.2 %collective-permute-start.27 = (bf16[256,640]{1,0:T(8,128)(2,1)S(1)}, bf16[256,640]{1,0:T(8,128)(2,1)S(1)}, u32[]{:S(2)}, u32[]{:S(2)}) collective-permute-start(bf16[256,640]{1,0:T(8,128)(2,1)S(1)} %collective-permute-done.26.refs_6_), channel_id=1, source_target_pairs={{0,1},{1,0},{2,3},{3,2},{4,5},{5,4},{6,7},{7,6},{8,9},{9,8},{10,11... | collective-permute-start | bytes 983048 | tf_op jit(solution)/shard_map/ppermute | solution.py:322
  149.0 21.9 %copy-start.14 = (bf16[256,640]{1,0:T(8,128)(2,1)}, bf16[256,640]{1,0:T(8,128)(2,1)S(1)}, u32[]{:S(2)}) copy-start(bf16[256,640]{1,0:T(8,128)(2,1)S(1)} %collective-permute-done.27.refs_7_) | copy-start | bytes 983044
  149.0 26.6 %collective-permute-start.31 = (bf16[20,1280]{1,0:T(8,128)(2,1)S(1)}, bf16[20,1280]{1,0:T(8,128)(2,1)S(1)}, u32[]{:S(2)}, u32[]{:S(2)}) collective-permute-start(bf16[20,1280]{1,0:T(8,128)(2,1)S(1)} %fusion.2), channel_id=1, source_target_pairs={{0,0},{1,4},{2,8},{3,12},{4,64},{5,68},{6,72},{7,76},{8,128},{9,13... | collective-permute-start | bytes 153608 | tf_op jit(solution)/shard_map/ppermute | solution.py:427
  157.1 18.5 %collective-permute-start.32 = (bf16[20,1280]{1,0:T(8,128)(2,1)S(1)}, bf16[20,1280]{1,0:T(8,128)(2,1)S(1)}, u32[]{:S(2)}, u32[]{:S(2)}) collective-permute-start(bf16[20,1280]{1,0:T(8,128)(2,1)S(1)} %fusion.2), channel_id=1, source_target_pairs={{0,64},{1,68},{2,72},{3,76},{4,0},{5,4},{6,8},{7,12},{8,192},{9,19... | collective-permute-start | bytes 153608 | tf_op jit(solution)/shard_map/ppermute | solution.py:427
  157.3 18.2 %collective-permute-start.33 = (bf16[20,1280]{1,0:T(8,128)(2,1)S(1)}, bf16[20,1280]{1,0:T(8,128)(2,1)S(1)}, u32[]{:S(2)}, u32[]{:S(2)}) collective-permute-start(bf16[20,1280]{1,0:T(8,128)(2,1)S(1)} %fusion.2), channel_id=1, source_target_pairs={{0,128},{1,132},{2,136},{3,140},{4,192},{5,196},{6,200},{7,204},{8... | collective-permute-start | bytes 153608 | tf_op jit(solution)/shard_map/ppermute | solution.py:427
  163.6 12.0 %collective-permute-start.34 = (bf16[20,1280]{1,0:T(8,128)(2,1)S(1)}, bf16[20,1280]{1,0:T(8,128)(2,1)S(1)}, u32[]{:S(2)}, u32[]{:S(2)}) collective-permute-start(bf16[20,1280]{1,0:T(8,128)(2,1)S(1)} %fusion.2), channel_id=1, source_target_pairs={{0,192},{1,196},{2,200},{3,204},{4,128},{5,132},{6,136},{7,140},{8... | collective-permute-start | bytes 153608 | tf_op jit(solution)/shard_map/ppermute | solution.py:427
  (14 other events, 45.5 us)

commit v2 on v1

--- a/solution.py
+++ b/solution.py
@@ -278,7 +278,7 @@
     )(place, *parts, cos, sin)
 
 
-def deal_kernel(starts, place, perm, counts, *refs):
+def deal_kernel(place, perm, counts, *refs):
     sources, out = (refs[:GROUP], refs[GROUP : 2 * GROUP]), refs[2 * GROUP]
     member, slice_id = place[0], place[2]
     width = sources[0][0].shape[1]
@@ -290,14 +290,13 @@
         tile = perm[slice_id, jnp.minimum(before + slot, TILES - 1)]
         live = slot < taken
         where = (tile // GROUP) ^ member
-        row = (tile % GROUP) * TILE
+        here = pl.ds(pl.multiple_of((tile % GROUP) * TILE, TILE), TILE)
         target = slice(slot * TILE, (slot + 1) * TILE)
         for step in range(GROUP):
 
             @pl.when(live & (where == step))
             def _():
                 for half, pieces in enumerate(sources):
-                    here = pl.ds(pl.multiple_of(row + starts[half], TILE), TILE)
                     out[target, half * width : (half + 1) * width] = pieces[step][here, :]
 
         @pl.when(jnp.logical_not(live))
@@ -305,11 +304,14 @@
             out[target, :] = jnp.zeros((TILE, out.shape[1]), BF)
 
 
-def deal_tiles(place, perm, counts, first, second, starts):
-    return pl.pallas_call(
-        functools.partial(deal_kernel, starts),
+def deal_tiles(place, perm, counts, first, second, blocks):
+    rows = GROUP * TILE
+    specs = [pl.BlockSpec((rows, D // 2), lambda step, block=block: (block, 0)) for block in blocks for _ in first]
+    return pl.pallas_call(
+        deal_kernel,
+        grid=(1,),
         out_shape=jax.ShapeDtypeStruct((CAP * TILE, D), BF),
-        in_specs=[SM] * 3 + [VM] * 8,
+        in_specs=[SM] * 3 + specs,
         out_specs=VM,
         compiler_params=params(),
         cost_estimate=HINT,
@@ -340,8 +342,8 @@
     return relabel(count, lambda x, y, s, m: ((s, y, m, x), (x, y, s, m)))
 
 
-def share_route(count, step):
-    return relabel(count, lambda x, y, s, m: ((x, y, s, m), (s ^ step, y, m, x)))
+def share_route(count):
+    return relabel(count, lambda x, y, s, m: ((x, y, s, m), (s, y, m, x)))
 
 
 def shards(
@@ -380,9 +382,12 @@
     place, first, corner, piece1, piece2, sent3 = tie((place, first, corner, piece1, piece2, pieces[3]))
     piece3 = swap(sent3, "ctx", 3)
     corners = [corner] + [swap(corner, "dp", step) for step in range(1, GROUP)]
-    second = window_grads(place, *window_in, 1, (2, 1))
-
-    place, first, second, piece3, corners, grad0 = tie((place, first, second, piece3, corners, full_grad_out[0]))
+    sibling = [swap(first[0], "ctx", 1)]
+    second = window_grads(place, *window_in, 1, (1, 2))
+
+    place, first, second, sibling, piece3, corners, grad0 = tie(
+        (place, first, second, sibling, piece3, corners, full_grad_out[0])
+    )
     pieces = (pieces[0], piece1, piece2, piece3)
     grad1, grad2 = swap(grad0, "ctx", 1), swap(grad0, "ctx", 2)
     low_bit, high_bit = across % 2 == 1, across // 2 == 1
@@ -396,38 +401,40 @@
         (place, raised_low, out, grad1, grad2, weights, window)
     )
     crossed = [swap(window[0], "ctx", 2)]
+    sibling += [swap(array, "ctx", 1) for array in window[1:]]
     grads = (grad0, grad1, grad2, swap(grad2, "ctx", 1))
     *shares, dattn = weight_shares(place, out, grads, weights)
 
-    place, dattn, *shares = tie((place, dattn, *shares))
+    place, dattn, sibling, *shares = tie((place, dattn, sibling, *shares))
     crossed.append(swap(window[1], "ctx", 2))
     swapped = [swap(shares[step], "ctx", step * 16) for step in range(1, GROUP)]
     backs = full_grads(place, pieces, dattn, out, inverses, raised_low)
 
     place, backs, swapped, crossed, window = tie((place, backs, swapped, crossed, window))
-    parts = [backs[0]] + [swap(backs[step], "ctx", step) for step in range(1, GROUP)]
-    crossed.append(swap(window[2], "ctx", 2))
-    sibling = [swap(array, "ctx", 1) for array in window]
-    opposite = [swap(array, "ctx", 1) for array in crossed]
+    part2, last = swap(backs[2], "ctx", 2), swap(window[2], "ctx", 2)
     rows = total([shares[0], *swapped]).reshape(GROUP, HEAD_DIM // GROUP, D).astype(BF)
     rows = [lax.dynamic_index_in_dim(rows, across ^ step, 0, keepdims=False) for step in range(GROUP)]
     summed = [rows[0]] + [swap(rows[step], "dp", step) for step in range(1, GROUP)]
+    opposite = [swap(array, "ctx", 1) for array in crossed]
+
+    place, summed, part2, last, opposite, sent = tie((place, summed, part2, last, opposite, (backs[1], backs[3])))
+    part3, part1 = swap(sent[1], "ctx", 3), swap(sent[0], "ctx", 1)
+    crossed.append(last)
+    opposite.append(swap(last, "ctx", 1))
     share = total(summed).astype(BF)
     sets = list(zip(window, sibling, crossed, opposite))
-    tile_rows = first[0].shape[0] // 3
 
     def deal(which):
-        other, start = (1, which * tile_rows) if which < 2 else (2, 0)
-        starts = (which * tile_rows, start)
-        return deal_tiles(place, tile_perm[0], tile_counts[0], sets[0], sets[other], starts)[None]
-
-    dealt = [deal(0), deal(1)]
-    place, share, parts, opposite, dealt = tie((place, share, parts, opposite, dealt))
-    sets = list(zip(window, sibling, crossed, opposite))
-    shared = [lax.ppermute(share, ("dp", "ctx"), share_route(GROUP, step)) for step in range(GROUP)]
-    dealt.append(deal(2))
-    full = join_heads(place, parts, cos, sin)
-    return (*dealt, *[array[None] for array in full], total(shared))
+        other, block = (1, 0) if which == 0 else (2, which - 1)
+        return deal_tiles(place, tile_perm[0], tile_counts[0], sets[0], sets[other], (which, block))
+
+    dealt = [deal(0), deal(1), deal(2)]
+    around = [share] + [swap(share, "ctx", step * GROUP) for step in range(1, GROUP)]
+
+    place, part1, part3, dealt, around = tie((place, part1, part3, dealt, around))
+    share = lax.ppermute(total(around).astype(BF), ("dp", "ctx"), share_route(GROUP))
+    full = join_heads(place, (backs[0], part1, part2, part3), cos, sin)
+    return (*[array[None] for array in dealt], *[array[None] for array in full], share.astype(F32))
 
 
 def solution(mesh):

time: 177 us -> 156 us (0.88)
  the two profiles are of different devices: /device:TPU:41 before, /device:TPU:1 now
where the time goes in v2:
time: 156 us; the launch traced here: 155 us
  Pallas kernels  68.2 us (44%)
  starting transfers between devices  53.3 us (34%)
  waiting for transfers between devices  23.9 us (15%)
  other arithmetic  4.95 us (3%)
  local copies, waits for them, and re-layouts  3.39 us (2%)
    ppermute x33, starting transfers between devices, swap(): return lax.ppermute(array, axis, [(i, i ^ distance) for i in range(count)])  46.6 us
    ppermute x33, waiting for transfers between devices, swap(): return lax.ppermute(array, axis, [(i, i ^ distance) for i in range(count)])  23.9 us
    pallas_call x2, Pallas kernels, window_grads(): pl.pallas_call(window_kernel, grid=(1,), out_shape=[jax.ShapeDtypeStruct(...  15.9 us
    pallas_call x1, Pallas kernels, full_grads(): pl.pallas_call(grads_kernel, grid=(HEADS // GROUP,), out_shape=[jax.Shape...  15.4 us
    pallas_call x1, Pallas kernels, full_probs(): pl.pallas_call(probs_kernel, grid=(heads,), out_shape=[jax.ShapeDtypeStru...  15.2 us
    pallas_call x3, Pallas kernels, deal_tiles(): pl.pallas_call(deal_kernel, grid=(1,), out_shape=jax.ShapeDtypeStruct((CA...  9.45 us
    pallas_call x1, Pallas kernels, weight_shares(): pl.pallas_call(share_kernel, out_shape=[jax.ShapeDtypeStruct((HEAD_DIM, D...  5.34 us
    pallas_call x1, Pallas kernels, split_heads(): pl.pallas_call(split_kernel, out_shape=[jax.ShapeDtypeStruct((3 * QUARTER...  3.56 us
  transfers between devices with their start and end apart: 35, of which 8 were waited for; matrix products, arithmetic and copies ran while one was open for 2% of the time, Pallas kernels for 42%

profile of v2, /device:TPU:1, one launch (start us, length us, event | category | flops | bytes accessed | tf_op | source)
XLA Modules:
  0.0 154.9 jit_solution(5541316644975652000)
XLA Ops:
  0.7 0.7 slice_convert_fusion.1
  1.5 0.8 fusion
  2.3 0.7 pad_add_fusion.place.refs_0_
  2.9 3.6 %split_heads.1 = (bf16[960,256]{1,0:T(8,128)(2,1)}, bf16[960,256]{1,0:T(8,128)(2,1)}, bf16[960,256]{1,0:T(8,128)(2,1)}, bf16[960,256]{1,0:T(8,128)(2,1)}) custom-call(s32[3]{0:T(128)} %pad_add_fusion.place.refs_0_, bf16[256,1280]{1,0:T(8,128)(2,1)} %bitcast.43, bf16[256,1280]{1,0:T(8,128)(2,1)} %bitcast.44, bf16[256,1280]{1,0:T(8,128)(2,1)} %bitcast.45, ...), custom_call_target="tpu_custom_call" | custom-call | flops 100000 | bytes 100000 | tf_op jit(solution)/shard_map/split_heads/pallas_call | solution.py:80
  6.5 3.2 %collective-permute-start.1 = (bf16[960,256]{1,0:T(8,128)(2,1)}, bf16[960,256]{1,0:T(8,128)(2,1)S(1)}, u32[]{:S(2)}, u32[]{:S(2)}) collective-permute-start(bf16[960,256]{1,0:T(8,128)(2,1)} %get-tuple-element.110), channel_id=1, source_target_pairs={{0,1},{1,0},{2,3},{3,2},{4,5},{5,4},{6,7},{7,6},{8,9},{9,8},{10,11... | collective-permute-start | bytes 1474568 | tf_op jit(solution)/shard_map/ppermute | solution.py:324
  9.7 3.2 %collective-permute-start = (bf16[20,1280]{1,0:T(8,128)(2,1)S(1)}, bf16[20,1280]{1,0:T(8,128)(2,1)S(1)}, u32[]{:S(2)}, u32[]{:S(2)}) collective-permute-start(bf16[20,1280]{1,0:T(8,128)(2,1)S(1)} %copy-done.26), channel_id=1, source_target_pairs={{0,0},{4,1},{8,2},{12,3},{64,4},{68,5},{72,6},{76,7},{128,8},{132,... | collective-permute-start | bytes 153608 | tf_op jit(solution)/shard_map/ppermute | solution.py:373
  12.9 8.0 %window_grads.2.refs_0_ = bf16[768,640]{1,0:T(8,128)(2,1)} custom-call(s32[3]{0:T(128)} %pad_add_fusion.place.refs_0_, bf16[256,1280]{1,0:T(8,128)(2,1)} %bitcast.29, bf16[256,1280]{1,0:T(8,128)(2,1)} %bitcast.31, bf16[256,1280]{1,0:T(8,128)(2,1)} %bitcast.33, bf16[256,1280]{1,0:T(8,128)(2,1)} %bitcast.35, f32[40,256]{1,0:T(8,128)} %get-tuple-element.212.cos_ref, ...), custom_call_target="tpu_custom_call" | custom-call | flops 100000 | bytes 100000 | tf_op jit(solution)/shard_map/window_grads/pallas_call | solution.py:130
  20.9 3.3 %collective-permute-done.2.piece2.refs_3_ = bf16[960,256]{1,0:T(8,128)(2,1)} collective-permute-done((bf16[960,256]{1,0:T(8,128)(2,1)}, bf16[960,256]{1,0:T(8,128)(2,1)}, u32[]{:S(2)}, u32[]{:S(2)}) %collective-permute-start.2) | collective-permute-done | bytes 491552 | tf_op jit(solution)/shard_map/ppermute | solution.py:324
  24.2 1.2 collective-permute-start.3
  25.4 4.1 %collective-permute-start.4 = (bf16[960,256]{1,0:T(8,128)(2,1)S(1)}, bf16[960,256]{1,0:T(8,128)(2,1)S(1)}, u32[]{:S(2)}, u32[]{:S(2)}) collective-permute-start(bf16[960,256]{1,0:T(8,128)(2,1)S(1)} %copy-done.25), channel_id=1, source_target_pairs={{0,3},{1,2},{2,1},{3,0},{4,7},{5,6},{6,5},{7,4},{8,11},{9,10},{10,... | collective-permute-start | bytes 1474568 | tf_op jit(solution)/shard_map/ppermute | solution.py:324
  29.4 0.8 collective-permute-start.5
  30.3 3.1 %collective-permute-start.6 = (bf16[20,1280]{1,0:T(8,128)(2,1)S(1)}, bf16[20,1280]{1,0:T(8,128)(2,1)S(1)}, u32[]{:S(2)}, u32[]{:S(2)}) collective-permute-start(bf16[20,1280]{1,0:T(8,128)(2,1)S(1)} %collective-permute-done), channel_id=1, source_target_pairs={{0,128},{64,192},{128,0},{192,64},{1,129},{65,193},{129,1},{193,65... | collective-permute-start | bytes 153608 | tf_op jit(solution)/shard_map/ppermute | solution.py:324
  33.4 7.9 %window_grads.3 = (bf16[256,640]{1,0:T(8,128)(2,1)}, bf16[512,640]{1,0:T(8,128)(2,1)}) custom-call(s32[3]{0:T(128)} %pad_add_fusion.place.refs_0_, bf16[256,1280]{1,0:T(8,128)(2,1)} %bitcast.30, bf16[256,1280]{1,0:T(8,128)(2,1)} %bitcast.32, bf16[256,1280]{1,0:T(8,128)(2,1)} %bitcast.34, bf16[256,1280]{1,0:T(8,128)(2,1)} %bitcast.36, ...), custom_call_target="tpu_custom_call" | custom-call | flops 100000 | bytes 100000 | tf_op jit(solution)/shard_map/window_grads/pallas_call | solution.py:130
  41.3 1.1 collective-permute-start.8
  43.0 1.4 collective-permute-start.10
  44.4 2.6 %collective-permute-start.11 = (bf16[80,1280]{1,0:T(8,128)(2,1)S(1)}, bf16[80,1280]{1,0:T(8,128)(2,1)S(1)}, u32[]{:S(2)}, u32[]{:S(2)}) collective-permute-start(bf16[80,1280]{1,0:T(8,128)(2,1)S(1)} %pad_maximum_fusion.refs_6_), channel_id=1, source_target_pairs={{0,32},{1,33},{2,34},{3,35},{4,36},{5,37},{6,38},{7,39},{8,40},{9,... | collective-permute-start | bytes 614408 | tf_op jit(solution)/shard_map/ppermute | solution.py:324
  47.0 15.2 %full_probs.1 = (bf16[4,1024,1024]{2,1,0:T(8,128)(2,1)}, f32[320,1024]{1,0:T(8,128)}, f32[4,1,1024]{2,1,0:T(1,128)}) custom-call(s32[3]{0:T(128)} %pad_add_fusion.place.refs_0_, bf16[960,256]{1,0:T(8,128)(2,1)} %get-tuple-element.120.piece0.refs_1_, bf16[960,256]{1,0:T(8,128)(2,1)} %copy-done.8, bf16[960,256]{1,0:T(8,128)(2,1)} %collective-permute-done.2.piece2.refs_3_, ...), custom_call_target="tpu_custom_call" | custom-call | flops 100000 | bytes 100000 | tf_op jit(solution)/shard_map/full_probs/pallas_call | solution.py:169
  62.3 1.1 collective-permute-start.19
  63.4 1.4 collective-permute-start.13
  65.9 0.7 collective-permute-done.13.refs_5_
  66.6 0.8 copy-done.14
  67.4 5.3 %weight_shares.1 = (bf16[80,1280]{1,0:T(8,128)(2,1)}, bf16[80,1280]{1,0:T(8,128)(2,1)}, bf16[80,1280]{1,0:T(8,128)(2,1)}, bf16[80,1280]{1,0:T(8,128)(2,1)}, bf16[320,1024]{1,0:T(8,128)(2,1)}) custom-call(s32[3]{0:T(128)} %pad_add_fusion.place.refs_0_, f32[320,1024]{1,0:T(8,128)} %get-tuple-element.135.refs_1_.refs_6_, bf16[256,1280]{1,0:T(8,128)(2,1)} %bitcast.40, ...), custom_call_target="tpu_custom_call" | custom-call | flops 100000 | bytes 100000 | tf_op jit(solution)/shard_map/weight_shares/pallas_call | solution.py:202
  73.0 3.8 %collective-permute-start.17 = (bf16[80,1280]{1,0:T(8,128)(2,1)}, bf16[80,1280]{1,0:T(8,128)(2,1)}, u32[]{:S(2)}, u32[]{:S(2)}) collective-permute-start(bf16[80,1280]{1,0:T(8,128)(2,1)} %get-tuple-element.159), channel_id=1, source_target_pairs={{0,32},{1,33},{2,34},{3,35},{4,36},{5,37},{6,38},{7,39},{8,40},{9,... | collective-permute-start | bytes 614408 | tf_op jit(solution)/shard_map/ppermute | solution.py:324
  76.8 15.4 %full_grads.1 = (bf16[960,256]{1,0:T(8,128)(2,1)}, bf16[960,256]{1,0:T(8,128)(2,1)}, bf16[960,256]{1,0:T(8,128)(2,1)}, bf16[960,256]{1,0:T(8,128)(2,1)}) custom-call(s32[3]{0:T(128)} %pad_add_fusion.place.refs_0_, bf16[960,256]{1,0:T(8,128)(2,1)} %get-tuple-element.120.piece0.refs_1_, bf16[960,256]{1,0:T(8,128)(2,1)} %copy-done.8, ...), custom_call_target="tpu_custom_call" | custom-call | flops 100000 | bytes 100000 | tf_op jit(solution)/shard_map/full_grads/pallas_call | solution.py:240
  93.0 1.4 collective-permute-start.26
  94.4 1.0 collective-permute-start.25
  95.9 1.9 %add_convert_fusion = bf16[80,1280]{1,0:T(8,128)(2,1)} fusion(bf16[80,1280]{1,0:T(8,128)(2,1)} %copy-done.20, bf16[80,1280]{1,0:T(8,128)(2,1)} %collective-permute-done.17, bf16[80,1280]{1,0:T(8,128)(2,1)} %collective-permute-done.16, bf16[80,1280]{1,0:T(8,128)(2,1)S(1)} %copy-done.19), kind=kLoop, calls=%fused_computation | loop fusion | flops 819200 | bytes 1024000 | tf_op jit(solution)/shard_map/convert_element_type | solution.py:415
  97.8 1.0 convert_element_type.90
  99.4 0.9 collective-permute-start.21
  100.3 2.8 %collective-permute-done.21 = bf16[20,1280]{1,0:T(8,128)(2,1)S(1)} collective-permute-done((bf16[20,1280]{1,0:T(8,128)(2,1)S(1)}, bf16[20,1280]{1,0:T(8,128)(2,1)S(1)}, u32[]{:S(2)}, u32[]{:S(2)}) %collective-permute-start.21) | collective-permute-done | bytes 51232 | tf_op jit(solution)/shard_map/ppermute | solution.py:324
  103.1 3.1 %collective-permute-start.22 = (bf16[20,1280]{1,0:T(8,128)(2,1)S(1)}, bf16[20,1280]{1,0:T(8,128)(2,1)S(1)}, u32[]{:S(2)}, u32[]{:S(2)}) collective-permute-start(bf16[20,1280]{1,0:T(8,128)(2,1)S(1)} %get-tuple-element.204), channel_id=1, source_target_pairs={{0,128},{64,192},{128,0},{192,64},{1,129},{65,193},{129,1},{193,65... | collective-permute-start | bytes 153608 | tf_op jit(solution)/shard_map/ppermute | solution.py:324
  106.2 1.6 %collective-permute-done.22 = bf16[20,1280]{1,0:T(8,128)(2,1)S(1)} collective-permute-done((bf16[20,1280]{1,0:T(8,128)(2,1)S(1)}, bf16[20,1280]{1,0:T(8,128)(2,1)S(1)}, u32[]{:S(2)}, u32[]{:S(2)}) %collective-permute-start.22) | collective-permute-done | bytes 51232 | tf_op jit(solution)/shard_map/ppermute | solution.py:324
  107.9 2.5 %collective-permute-start.23 = (bf16[20,1280]{1,0:T(8,128)(2,1)S(1)}, bf16[20,1280]{1,0:T(8,128)(2,1)S(1)}, u32[]{:S(2)}, u32[]{:S(2)}) collective-permute-start(bf16[20,1280]{1,0:T(8,128)(2,1)S(1)} %get-tuple-element.203), channel_id=1, source_target_pairs={{0,192},{64,128},{128,64},{192,0},{1,193},{65,129},{129,65},{193,1... | collective-permute-start | bytes 153608 | tf_op jit(solution)/shard_map/ppermute | solution.py:324
  110.4 1.8 %collective-permute-done.23 = bf16[20,1280]{1,0:T(8,128)(2,1)S(1)} collective-permute-done((bf16[20,1280]{1,0:T(8,128)(2,1)S(1)}, bf16[20,1280]{1,0:T(8,128)(2,1)S(1)}, u32[]{:S(2)}, u32[]{:S(2)}) %collective-permute-start.23) | collective-permute-done | bytes 51232 | tf_op jit(solution)/shard_map/ppermute | solution.py:324
  112.1 9.2 %collective-permute-done.24.part2 = bf16[960,256]{1,0:T(8,128)(2,1)} collective-permute-done((bf16[960,256]{1,0:T(8,128)(2,1)}, bf16[960,256]{1,0:T(8,128)(2,1)}, u32[]{:S(2)}, u32[]{:S(2)}) %collective-permute-start.24) | collective-permute-done | bytes 491552 | tf_op jit(solution)/shard_map/ppermute | solution.py:324
  121.4 0.9 collective-permute-start.30
  122.4 1.3 collective-permute-start.29
  123.7 3.9 %collective-permute-start.31 = (bf16[20,1280]{1,0:T(8,128)(2,1)S(1)}, bf16[20,1280]{1,0:T(8,128)(2,1)S(1)}, u32[]{:S(2)}, u32[]{:S(2)}) collective-permute-start(bf16[20,1280]{1,0:T(8,128)(2,1)S(1)} %add_convert_fusion.2), channel_id=1, source_target_pairs={{0,4},{1,5},{2,6},{3,7},{4,0},{5,1},{6,2},{7,3},{8,12},{9,13},{10,... | collective-permute-start | bytes 153608 | tf_op jit(solution)/shard_map/ppermute | solution.py:324
  127.7 4.8 %collective-permute-start.32 = (bf16[20,1280]{1,0:T(8,128)(2,1)S(1)}, bf16[20,1280]{1,0:T(8,128)(2,1)S(1)}, u32[]{:S(2)}, u32[]{:S(2)}) collective-permute-start(bf16[20,1280]{1,0:T(8,128)(2,1)S(1)} %add_convert_fusion.2), channel_id=1, source_target_pairs={{0,8},{1,9},{2,10},{3,11},{4,12},{5,13},{6,14},{7,15},{8,0},{9,1},... | collective-permute-start | bytes 153608 | tf_op jit(solution)/shard_map/ppermute | solution.py:324
  132.5 0.7 copy.22.counts
  133.3 3.1 %deal_tiles.3 = bf16[512,1280]{1,0:T(8,128)(2,1)} custom-call(s32[3]{0:T(128)} %pad_add_fusion.place.refs_0_, s32[16,16]{1,0:T(8,128)} %bitcast.46, s32[16,4]{1,0:T(8,128)} %copy.22.counts, bf16[768,640]{1,0:T(8,128)(2,1)} %window_grads.2.refs_0_, bf16[768,640]{1,0:T(8,128)(2,1)} %copy-done.1, bf16[768,640]{1,0:T(8,128)(2,1)} %copy-done.2, ...), custom_call_target="tpu_custom_call" | custom-call | flops 100000 | bytes 100000 | tf_op jit(solution)/shard_map/deal_tiles/pallas_call | solution.py:310
  136.4 3.2 %deal_tiles.5 = bf16[512,1280]{1,0:T(8,128)(2,1)} custom-call(s32[3]{0:T(128)} %pad_add_fusion.place.refs_0_, s32[16,16]{1,0:T(8,128)} %bitcast.47, s32[16,4]{1,0:T(8,128)} %copy.22.counts, bf16[768,640]{1,0:T(8,128)(2,1)} %window_grads.2.refs_0_, bf16[768,640]{1,0:T(8,128)(2,1)} %copy-done.1, bf16[768,640]{1,0:T(8,128)(2,1)} %copy-done.2, ...), custom_call_target="tpu_custom_call" | custom-call | flops 100000 | bytes 100000 | tf_op jit(solution)/shard_map/deal_tiles/pallas_call | solution.py:310
  139.6 3.1 %deal_tiles.4 = bf16[512,1280]{1,0:T(8,128)(2,1)} custom-call(s32[3]{0:T(128)} %pad_add_fusion.place.refs_0_, s32[16,16]{1,0:T(8,128)} %bitcast.48, s32[16,4]{1,0:T(8,128)} %copy.22.counts, bf16[768,640]{1,0:T(8,128)(2,1)} %window_grads.2.refs_0_, bf16[768,640]{1,0:T(8,128)(2,1)} %copy-done.1, bf16[768,640]{1,0:T(8,128)(2,1)} %copy-done.2, ...), custom_call_target="tpu_custom_call" | custom-call | flops 100000 | bytes 100000 | tf_op jit(solution)/shard_map/deal_tiles/pallas_call | solution.py:310
  142.7 2.1 %collective-permute-done.32 = bf16[20,1280]{1,0:T(8,128)(2,1)S(1)} collective-permute-done((bf16[20,1280]{1,0:T(8,128)(2,1)S(1)}, bf16[20,1280]{1,0:T(8,128)(2,1)S(1)}, u32[]{:S(2)}, u32[]{:S(2)}) %collective-permute-start.32) | collective-permute-done | bytes 51232 | tf_op jit(solution)/shard_map/ppermute | solution.py:324
  144.9 2.3 %collective-permute-done.33 = bf16[20,1280]{1,0:T(8,128)(2,1)S(1)} collective-permute-done((bf16[20,1280]{1,0:T(8,128)(2,1)S(1)}, bf16[20,1280]{1,0:T(8,128)(2,1)S(1)}, u32[]{:S(2)}, u32[]{:S(2)}) %collective-permute-start.33) | collective-permute-done | bytes 51232 | tf_op jit(solution)/shard_map/ppermute | solution.py:324
  147.2 3.5 %collective-permute-start.34 = (bf16[20,1280]{1,0:T(8,128)(2,1)S(1)}, bf16[20,1280]{1,0:T(8,128)(2,1)S(1)}, u32[]{:S(2)}, u32[]{:S(2)}) collective-permute-start(bf16[20,1280]{1,0:T(8,128)(2,1)S(1)} %add_convert_fusion.1), channel_id=1, source_target_pairs={{0,0},{1,4},{2,8},{3,12},{4,64},{5,68},{6,72},{7,76},{8,128},{9,13... | collective-permute-start | bytes 153608 | tf_op jit(solution)/shard_map/ppermute | solution.py:435
  150.7 3.5 %join_heads.1 = (bf16[256,1280]{1,0:T(8,128)(2,1)}, bf16[256,1280]{1,0:T(8,128)(2,1)}, bf16[256,1280]{1,0:T(8,128)(2,1)}) custom-call(s32[3]{0:T(128)} %pad_add_fusion.place.refs_0_, bf16[960,256]{1,0:T(8,128)(2,1)} %get-tuple-element.192.part0, bf16[960,256]{1,0:T(8,128)(2,1)} %collective-permute-done.28.part1, ...), custom_call_target="tpu_custom_call" | custom-call | flops 100000 | bytes 100000 | tf_op jit(solution)/shard_map/join_heads/pallas_call | solution.py:269
  154.2 0.7 convert_element_type.101
  (100 shorter events, 4.2 us)
Async XLA Ops:
  6.5 14.4 %collective-permute-start.1 = (bf16[960,256]{1,0:T(8,128)(2,1)}, bf16[960,256]{1,0:T(8,128)(2,1)S(1)}, u32[]{:S(2)}, u32[]{:S(2)}) collective-permute-start(bf16[960,256]{1,0:T(8,128)(2,1)} %get-tuple-element.110), channel_id=1, source_target_pairs={{0,1},{1,0},{2,3},{3,2},{4,5},{5,4},{6,7},{7,6},{8,9},{9,8},{10,11... | collective-permute-start | bytes 1474568 | tf_op jit(solution)/shard_map/ppermute | solution.py:324
  9.7 14.5 %collective-permute-start.2 = (bf16[960,256]{1,0:T(8,128)(2,1)}, bf16[960,256]{1,0:T(8,128)(2,1)}, u32[]{:S(2)}, u32[]{:S(2)}) collective-permute-start(bf16[960,256]{1,0:T(8,128)(2,1)} %get-tuple-element.111), channel_id=1, source_target_pairs={{0,2},{1,3},{2,0},{3,1},{4,6},{5,7},{6,4},{7,5},{8,10},{9,11},{10,... | collective-permute-start | bytes 1474568 | tf_op jit(solution)/shard_map/ppermute | solution.py:324
  9.7 11.2 %collective-permute-start = (bf16[20,1280]{1,0:T(8,128)(2,1)S(1)}, bf16[20,1280]{1,0:T(8,128)(2,1)S(1)}, u32[]{:S(2)}, u32[]{:S(2)}) collective-permute-start(bf16[20,1280]{1,0:T(8,128)(2,1)S(1)} %copy-done.26), channel_id=1, source_target_pairs={{0,0},{4,1},{8,2},{12,3},{64,4},{68,5},{72,6},{76,7},{128,8},{132,... | collective-permute-start | bytes 153608 | tf_op jit(solution)/shard_map/ppermute | solution.py:373
  20.9 20.3 %copy-start.8 = (bf16[960,256]{1,0:T(8,128)(2,1)}, bf16[960,256]{1,0:T(8,128)(2,1)S(1)}, u32[]{:S(2)}) copy-start(bf16[960,256]{1,0:T(8,128)(2,1)S(1)} %collective-permute-done.1.piece1.refs_2_) | copy-start | bytes 1474564
  24.2 17.1 %collective-permute-start.3 = (bf16[768,640]{1,0:T(8,128)(2,1)}, bf16[768,640]{1,0:T(8,128)(2,1)S(1)}, u32[]{:S(2)}, u32[]{:S(2)}) collective-permute-start(bf16[768,640]{1,0:T(8,128)(2,1)} %window_grads.2.refs_0_), channel_id=1, source_target_pairs={{0,1},{1,0},{2,3},{3,2},{4,5},{5,4},{6,7},{7,6},{8,9},{9,8},{10,11... | collective-permute-start | bytes 2949128 | tf_op jit(solution)/shard_map/ppermute | solution.py:324
  25.4 15.9 %collective-permute-start.4 = (bf16[960,256]{1,0:T(8,128)(2,1)S(1)}, bf16[960,256]{1,0:T(8,128)(2,1)S(1)}, u32[]{:S(2)}, u32[]{:S(2)}) collective-permute-start(bf16[960,256]{1,0:T(8,128)(2,1)S(1)} %copy-done.25), channel_id=1, source_target_pairs={{0,3},{1,2},{2,1},{3,0},{4,7},{5,6},{6,5},{7,4},{8,11},{9,10},{10,... | collective-permute-start | bytes 1474568 | tf_op jit(solution)/shard_map/ppermute | solution.py:324
  29.4 11.8 %collective-permute-start.5 = (bf16[20,1280]{1,0:T(8,128)(2,1)S(1)}, bf16[20,1280]{1,0:T(8,128)(2,1)S(1)}, u32[]{:S(2)}, u32[]{:S(2)}) collective-permute-start(bf16[20,1280]{1,0:T(8,128)(2,1)S(1)} %collective-permute-done), channel_id=1, source_target_pairs={{0,64},{64,0},{128,192},{192,128},{1,65},{65,1},{129,193},{193,129... | collective-permute-start | bytes 153608 | tf_op jit(solution)/shard_map/ppermute | solution.py:324
  30.3 11.0 %collective-permute-start.6 = (bf16[20,1280]{1,0:T(8,128)(2,1)S(1)}, bf16[20,1280]{1,0:T(8,128)(2,1)S(1)}, u32[]{:S(2)}, u32[]{:S(2)}) collective-permute-start(bf16[20,1280]{1,0:T(8,128)(2,1)S(1)} %collective-permute-done), channel_id=1, source_target_pairs={{0,128},{64,192},{128,0},{192,64},{1,129},{65,193},{129,1},{193,65... | collective-permute-start | bytes 153608 | tf_op jit(solution)/shard_map/ppermute | solution.py:324
  33.3 7.9 %collective-permute-start.7 = (bf16[20,1280]{1,0:T(8,128)(2,1)S(1)}, bf16[20,1280]{1,0:T(8,128)(2,1)S(1)}, u32[]{:S(2)}, u32[]{:S(2)}) collective-permute-start(bf16[20,1280]{1,0:T(8,128)(2,1)S(1)} %collective-permute-done), channel_id=1, source_target_pairs={{0,192},{64,128},{128,64},{192,0},{1,193},{65,129},{129,65},{193,1... | collective-permute-start | bytes 153608 | tf_op jit(solution)/shard_map/ppermute | solution.py:324
  41.3 20.9 %copy-start.1 = (bf16[768,640]{1,0:T(8,128)(2,1)}, bf16[768,640]{1,0:T(8,128)(2,1)S(1)}, u32[]{:S(2)}) copy-start(bf16[768,640]{1,0:T(8,128)(2,1)S(1)} %collective-permute-done.3.refs_1_) | copy-start | bytes 2949124
  41.3 20.9 %collective-permute-start.8 = (bf16[256,1280]{1,0:T(8,128)(2,1)S(1)}, bf16[256,1280]{1,0:T(8,128)(2,1)S(1)}, u32[]{:S(2)}, u32[]{:S(2)}) collective-permute-start(bf16[256,1280]{1,0:T(8,128)(2,1)S(1)} %bitcast.41), channel_id=1, source_target_pairs={{0,1},{1,0},{2,3},{3,2},{4,5},{5,4},{6,7},{7,6},{8,9},{9,8},{10,11... | collective-permute-start | bytes 1966088 | tf_op jit(solution)/shard_map/ppermute | solution.py:324
  42.4 19.9 %collective-permute-start.9 = (bf16[256,1280]{1,0:T(8,128)(2,1)S(1)}, bf16[256,1280]{1,0:T(8,128)(2,1)S(1)}, u32[]{:S(2)}, u32[]{:S(2)}) collective-permute-start(bf16[256,1280]{1,0:T(8,128)(2,1)S(1)} %bitcast.42), channel_id=1, source_target_pairs={{0,2},{1,3},{2,0},{3,1},{4,6},{5,7},{6,4},{7,5},{8,10},{9,11},{10,... | collective-permute-start | bytes 1966088 | tf_op jit(solution)/shard_map/ppermute | solution.py:324
  42.9 19.4 %copy-start = (bf16[768,640]{1,0:T(8,128)(2,1)S(1)}, bf16[768,640]{1,0:T(8,128)(2,1)}, u32[]{:S(2)}) copy-start(bf16[768,640]{1,0:T(8,128)(2,1)} %window_grads.2.refs_0_) | copy-start | bytes 2949124
  42.9 21.9 %copy-start.4 = (bf16[512,640]{1,0:T(8,128)(2,1)S(1)}, bf16[512,640]{1,0:T(8,128)(2,1)}, u32[]{:S(2)}) copy-start(bf16[512,640]{1,0:T(8,128)(2,1)} %get-tuple-element.168.refs_4_) | copy-start | bytes 1966084
  42.9 21.9 %copy-start.15 = (bf16[256,640]{1,0:T(8,128)(2,1)S(1)}, bf16[256,640]{1,0:T(8,128)(2,1)}, u32[]{:S(2)}) copy-start(bf16[256,640]{1,0:T(8,128)(2,1)} %get-tuple-element.179.refs_4_) | copy-start | bytes 983044
  43.0 23.5 %copy-start.10 = (bf16[80,1280]{1,0:T(8,128)(2,1)}, bf16[80,1280]{1,0:T(8,128)(2,1)S(1)}, u32[]{:S(2)}) copy-start(bf16[80,1280]{1,0:T(8,128)(2,1)S(1)} %pad_maximum_fusion.refs_6_) | copy-start | bytes 614404
  43.0 19.2 %collective-permute-start.10 = (bf16[80,1280]{1,0:T(8,128)(2,1)S(1)}, bf16[80,1280]{1,0:T(8,128)(2,1)S(1)}, u32[]{:S(2)}, u32[]{:S(2)}) collective-permute-start(bf16[80,1280]{1,0:T(8,128)(2,1)S(1)} %pad_maximum_fusion.refs_6_), channel_id=1, source_target_pairs={{0,16},{1,17},{2,18},{3,19},{4,20},{5,21},{6,22},{7,23},{8,24},{9,... | collective-permute-start | bytes 614408 | tf_op jit(solution)/shard_map/ppermute | solution.py:324
  44.4 17.8 %collective-permute-start.11 = (bf16[80,1280]{1,0:T(8,128)(2,1)S(1)}, bf16[80,1280]{1,0:T(8,128)(2,1)S(1)}, u32[]{:S(2)}, u32[]{:S(2)}) collective-permute-start(bf16[80,1280]{1,0:T(8,128)(2,1)S(1)} %pad_maximum_fusion.refs_6_), channel_id=1, source_target_pairs={{0,32},{1,33},{2,34},{3,35},{4,36},{5,37},{6,38},{7,39},{8,40},{9,... | collective-permute-start | bytes 614408 | tf_op jit(solution)/shard_map/ppermute | solution.py:324
  47.0 15.2 %collective-permute-start.12 = (bf16[80,1280]{1,0:T(8,128)(2,1)S(1)}, bf16[80,1280]{1,0:T(8,128)(2,1)S(1)}, u32[]{:S(2)}, u32[]{:S(2)}) collective-permute-start(bf16[80,1280]{1,0:T(8,128)(2,1)S(1)} %pad_maximum_fusion.refs_6_), channel_id=1, source_target_pairs={{0,48},{1,49},{2,50},{3,51},{4,52},{5,53},{6,54},{7,55},{8,56},{9,... | collective-permute-start | bytes 614408 | tf_op jit(solution)/shard_map/ppermute | solution.py:324
  62.3 29.9 %collective-permute-start.19 = (bf16[768,640]{1,0:T(8,128)(2,1)S(1)}, bf16[768,640]{1,0:T(8,128)(2,1)S(1)}, u32[]{:S(2)}, u32[]{:S(2)}) collective-permute-start(bf16[768,640]{1,0:T(8,128)(2,1)S(1)} %copy-done), channel_id=1, source_target_pairs={{0,2},{1,3},{2,0},{3,1},{4,6},{5,7},{6,4},{7,5},{8,10},{9,11},{10,... | collective-permute-start | bytes 2949128 | tf_op jit(solution)/shard_map/ppermute | solution.py:324
  63.4 3.1 %collective-permute-start.13 = (bf16[256,1280]{1,0:T(8,128)(2,1)S(1)}, bf16[256,1280]{1,0:T(8,128)(2,1)S(1)}, u32[]{:S(2)}, u32[]{:S(2)}) collective-permute-start(bf16[256,1280]{1,0:T(8,128)(2,1)S(1)} %collective-permute-done.9.refs_4_), channel_id=1, source_target_pairs={{0,1},{1,0},{2,3},{3,2},{4,5},{5,4},{6,7},{7,6},{8,9},{9,8},{10,11... | collective-permute-start | bytes 1966088 | tf_op jit(solution)/shard_map/ppermute | solution.py:324
  64.8 8.0 %collective-permute-start.15 = (bf16[512,640]{1,0:T(8,128)(2,1)S(1)}, bf16[512,640]{1,0:T(8,128)(2,1)S(1)}, u32[]{:S(2)}, u32[]{:S(2)}) collective-permute-start(bf16[512,640]{1,0:T(8,128)(2,1)S(1)} %copy-done.4), channel_id=1, source_target_pairs={{0,1},{1,0},{2,3},{3,2},{4,5},{5,4},{6,7},{7,6},{8,9},{9,8},{10,11... | collective-permute-start | bytes 1966088 | tf_op jit(solution)/shard_map/ppermute | solution.py:324
  64.8 7.9 %collective-permute-start.14 = (bf16[256,640]{1,0:T(8,128)(2,1)S(1)}, bf16[256,640]{1,0:T(8,128)(2,1)S(1)}, u32[]{:S(2)}, u32[]{:S(2)}) collective-permute-start(bf16[256,640]{1,0:T(8,128)(2,1)S(1)} %copy-done.15), channel_id=1, source_target_pairs={{0,1},{1,0},{2,3},{3,2},{4,5},{5,4},{6,7},{7,6},{8,9},{9,8},{10,11... | collective-permute-start | bytes 983048 | tf_op jit(solution)/shard_map/ppermute | solution.py:324
  65.3 26.9 %collective-permute-start.20 = (bf16[256,640]{1,0:T(8,128)(2,1)S(1)}, bf16[256,640]{1,0:T(8,128)(2,1)S(1)}, u32[]{:S(2)}, u32[]{:S(2)}) collective-permute-start(bf16[256,640]{1,0:T(8,128)(2,1)S(1)} %copy-done.15), channel_id=1, source_target_pairs={{0,2},{1,3},{2,0},{3,1},{4,6},{5,7},{6,4},{7,5},{8,10},{9,11},{10,... | collective-permute-start | bytes 983048 | tf_op jit(solution)/shard_map/ppermute | solution.py:324
  72.7 19.4 %copy-start.16 = (bf16[256,640]{1,0:T(8,128)(2,1)}, bf16[256,640]{1,0:T(8,128)(2,1)S(1)}, u32[]{:S(2)}) copy-start(bf16[256,640]{1,0:T(8,128)(2,1)S(1)} %collective-permute-done.14.refs_5_) | copy-start | bytes 983044
  72.8 19.4 %copy-start.5 = (bf16[512,640]{1,0:T(8,128)(2,1)}, bf16[512,640]{1,0:T(8,128)(2,1)S(1)}, u32[]{:S(2)}) copy-start(bf16[512,640]{1,0:T(8,128)(2,1)S(1)} %collective-permute-done.15.refs_5_) | copy-start | bytes 1966084
  72.8 19.4 %collective-permute-start.16 = (bf16[80,1280]{1,0:T(8,128)(2,1)}, bf16[80,1280]{1,0:T(8,128)(2,1)}, u32[]{:S(2)}, u32[]{:S(2)}) collective-permute-start(bf16[80,1280]{1,0:T(8,128)(2,1)} %get-tuple-element.158), channel_id=1, source_target_pairs={{0,16},{1,17},{2,18},{3,19},{4,20},{5,21},{6,22},{7,23},{8,24},{9,... | collective-permute-start | bytes 614408 | tf_op jit(solution)/shard_map/ppermute | solution.py:324
  73.0 19.3 %collective-permute-start.17 = (bf16[80,1280]{1,0:T(8,128)(2,1)}, bf16[80,1280]{1,0:T(8,128)(2,1)}, u32[]{:S(2)}, u32[]{:S(2)}) collective-permute-start(bf16[80,1280]{1,0:T(8,128)(2,1)} %get-tuple-element.159), channel_id=1, source_target_pairs={{0,32},{1,33},{2,34},{3,35},{4,36},{5,37},{6,38},{7,39},{8,40},{9,... | collective-permute-start | bytes 614408 | tf_op jit(solution)/shard_map/ppermute | solution.py:324
  76.8 15.4 %collective-permute-start.18 = (bf16[80,1280]{1,0:T(8,128)(2,1)}, bf16[80,1280]{1,0:T(8,128)(2,1)S(1)}, u32[]{:S(2)}, u32[]{:S(2)}) collective-permute-start(bf16[80,1280]{1,0:T(8,128)(2,1)} %get-tuple-element.160), channel_id=1, source_target_pairs={{0,48},{1,49},{2,50},{3,51},{4,52},{5,53},{6,54},{7,55},{8,56},{9,... | collective-permute-start | bytes 614408 | tf_op jit(solution)/shard_map/ppermute | solution.py:324
  76.8 19.1 %copy-start.19 = (bf16[80,1280]{1,0:T(8,128)(2,1)S(1)}, bf16[80,1280]{1,0:T(8,128)(2,1)}, u32[]{:S(2)}) copy-start(bf16[80,1280]{1,0:T(8,128)(2,1)} %get-tuple-element.163) | copy-start | bytes 614404
  92.2 40.4 %copy-start.24 = (s32[1,16,4]{1,2,0:T(4,128)S(1)}, s32[1,16,4]{1,2,0:T(4,128)}, u32[]{:S(2)}) copy-start(s32[1,16,4]{1,2,0:T(4,128)} %param.23) | copy-start | bytes 772
  92.3 41.0 %copy-start.2 = (bf16[768,640]{1,0:T(8,128)(2,1)}, bf16[768,640]{1,0:T(8,128)(2,1)S(1)}, u32[]{:S(2)}) copy-start(bf16[768,640]{1,0:T(8,128)(2,1)S(1)} %collective-permute-done.19.refs_2_) | copy-start | bytes 2949124
  93.0 28.4 %collective-permute-start.26 = (bf16[768,640]{1,0:T(8,128)(2,1)S(1)}, bf16[768,640]{1,0:T(8,128)(2,1)S(1)}, u32[]{:S(2)}, u32[]{:S(2)}) collective-permute-start(bf16[768,640]{1,0:T(8,128)(2,1)S(1)} %collective-permute-done.19.refs_2_), channel_id=1, source_target_pairs={{0,1},{1,0},{2,3},{3,2},{4,5},{5,4},{6,7},{7,6},{8,9},{9,8},{10,11... | collective-permute-start | bytes 2949128 | tf_op jit(solution)/shard_map/ppermute | solution.py:324
  94.4 27.0 %collective-permute-start.25 = (bf16[512,640]{1,0:T(8,128)(2,1)S(1)}, bf16[512,640]{1,0:T(8,128)(2,1)S(1)}, u32[]{:S(2)}, u32[]{:S(2)}) collective-permute-start(bf16[512,640]{1,0:T(8,128)(2,1)S(1)} %copy-done.4), channel_id=1, source_target_pairs={{0,2},{1,3},{2,0},{3,1},{4,6},{5,7},{6,4},{7,5},{8,10},{9,11},{10,... | collective-permute-start | bytes 1966088 | tf_op jit(solution)/shard_map/ppermute | solution.py:324
  95.4 26.0 %collective-permute-start.24 = (bf16[960,256]{1,0:T(8,128)(2,1)}, bf16[960,256]{1,0:T(8,128)(2,1)}, u32[]{:S(2)}, u32[]{:S(2)}) collective-permute-start(bf16[960,256]{1,0:T(8,128)(2,1)} %get-tuple-element.167), channel_id=1, source_target_pairs={{0,2},{1,3},{2,0},{3,1},{4,6},{5,7},{6,4},{7,5},{8,10},{9,11},{10,... | collective-permute-start | bytes 1474568 | tf_op jit(solution)/shard_map/ppermute | solution.py:324
  98.7 13.4 %collective-permute-start.27 = (bf16[256,640]{1,0:T(8,128)(2,1)}, bf16[256,640]{1,0:T(8,128)(2,1)S(1)}, u32[]{:S(2)}, u32[]{:S(2)}) collective-permute-start(bf16[256,640]{1,0:T(8,128)(2,1)} %copy-done.17), channel_id=1, source_target_pairs={{0,1},{1,0},{2,3},{3,2},{4,5},{5,4},{6,7},{7,6},{8,9},{9,8},{10,11... | collective-permute-start | bytes 983048 | tf_op jit(solution)/shard_map/ppermute | solution.py:324
  99.4 3.7 %collective-permute-start.21 = (bf16[20,1280]{1,0:T(8,128)(2,1)S(1)}, bf16[20,1280]{1,0:T(8,128)(2,1)S(1)}, u32[]{:S(2)}, u32[]{:S(2)}) collective-permute-start(bf16[20,1280]{1,0:T(8,128)(2,1)S(1)} %get-tuple-element.205), channel_id=1, source_target_pairs={{0,64},{64,0},{128,192},{192,128},{1,65},{65,1},{129,193},{193,129... | collective-permute-start | bytes 153608 | tf_op jit(solution)/shard_map/ppermute | solution.py:324
  103.1 4.8 %collective-permute-start.22 = (bf16[20,1280]{1,0:T(8,128)(2,1)S(1)}, bf16[20,1280]{1,0:T(8,128)(2,1)S(1)}, u32[]{:S(2)}, u32[]{:S(2)}) collective-permute-start(bf16[20,1280]{1,0:T(8,128)(2,1)S(1)} %get-tuple-element.204), channel_id=1, source_target_pairs={{0,128},{64,192},{128,0},{192,64},{1,129},{65,193},{129,1},{193,65... | collective-permute-start | bytes 153608 | tf_op jit(solution)/shard_map/ppermute | solution.py:324
  107.9 4.3 %collective-permute-start.23 = (bf16[20,1280]{1,0:T(8,128)(2,1)S(1)}, bf16[20,1280]{1,0:T(8,128)(2,1)S(1)}, u32[]{:S(2)}, u32[]{:S(2)}) collective-permute-start(bf16[20,1280]{1,0:T(8,128)(2,1)S(1)} %get-tuple-element.203), channel_id=1, source_target_pairs={{0,192},{64,128},{128,64},{192,0},{1,193},{65,129},{129,65},{193,1... | collective-permute-start | bytes 153608 | tf_op jit(solution)/shard_map/ppermute | solution.py:324
  112.1 20.3 %copy-start.18 = (bf16[256,640]{1,0:T(8,128)(2,1)}, bf16[256,640]{1,0:T(8,128)(2,1)S(1)}, u32[]{:S(2)}) copy-start(bf16[256,640]{1,0:T(8,128)(2,1)S(1)} %collective-permute-done.27.refs_7_) | copy-start | bytes 983044
  121.4 15.0 %copy-start.6 = (bf16[512,640]{1,0:T(8,128)(2,1)}, bf16[512,640]{1,0:T(8,128)(2,1)S(1)}, u32[]{:S(2)}) copy-start(bf16[512,640]{1,0:T(8,128)(2,1)S(1)} %collective-permute-done.25.refs_6_) | copy-start | bytes 1966084
  121.4 11.0 %collective-permute-start.30 = (bf16[512,640]{1,0:T(8,128)(2,1)S(1)}, bf16[512,640]{1,0:T(8,128)(2,1)S(1)}, u32[]{:S(2)}, u32[]{:S(2)}) collective-permute-start(bf16[512,640]{1,0:T(8,128)(2,1)S(1)} %collective-permute-done.25.refs_6_), channel_id=1, source_target_pairs={{0,1},{1,0},{2,3},{3,2},{4,5},{5,4},{6,7},{7,6},{8,9},{9,8},{10,11... | collective-permute-start | bytes 1966088 | tf_op jit(solution)/shard_map/ppermute | solution.py:324
  122.3 24.9 %collective-permute-start.28 = (bf16[960,256]{1,0:T(8,128)(2,1)}, bf16[960,256]{1,0:T(8,128)(2,1)}, u32[]{:S(2)}, u32[]{:S(2)}) collective-permute-start(bf16[960,256]{1,0:T(8,128)(2,1)} %get-tuple-element.174), channel_id=1, source_target_pairs={{0,1},{1,0},{2,3},{3,2},{4,5},{5,4},{6,7},{7,6},{8,9},{9,8},{10,11... | collective-permute-start | bytes 1474568 | tf_op jit(solution)/shard_map/ppermute | solution.py:324
  122.4 24.8 %collective-permute-start.29 = (bf16[960,256]{1,0:T(8,128)(2,1)}, bf16[960,256]{1,0:T(8,128)(2,1)}, u32[]{:S(2)}, u32[]{:S(2)}) collective-permute-start(bf16[960,256]{1,0:T(8,128)(2,1)} %get-tuple-element.175), channel_id=1, source_target_pairs={{0,3},{1,2},{2,1},{3,0},{4,7},{5,6},{6,5},{7,4},{8,11},{9,10},{10,... | collective-permute-start | bytes 1474568 | tf_op jit(solution)/shard_map/ppermute | solution.py:324
  123.7 19.0 %collective-permute-start.31 = (bf16[20,1280]{1,0:T(8,128)(2,1)S(1)}, bf16[20,1280]{1,0:T(8,128)(2,1)S(1)}, u32[]{:S(2)}, u32[]{:S(2)}) collective-permute-start(bf16[20,1280]{1,0:T(8,128)(2,1)S(1)} %add_convert_fusion.2), channel_id=1, source_target_pairs={{0,4},{1,5},{2,6},{3,7},{4,0},{5,1},{6,2},{7,3},{8,12},{9,13},{10,... | collective-permute-start | bytes 153608 | tf_op jit(solution)/shard_map/ppermute | solution.py:324
  127.7 17.2 %collective-permute-start.32 = (bf16[20,1280]{1,0:T(8,128)(2,1)S(1)}, bf16[20,1280]{1,0:T(8,128)(2,1)S(1)}, u32[]{:S(2)}, u32[]{:S(2)}) collective-permute-start(bf16[20,1280]{1,0:T(8,128)(2,1)S(1)} %add_convert_fusion.2), channel_id=1, source_target_pairs={{0,8},{1,9},{2,10},{3,11},{4,12},{5,13},{6,14},{7,15},{8,0},{9,1},... | collective-permute-start | bytes 153608 | tf_op jit(solution)/shard_map/ppermute | solution.py:324
  132.4 14.7 %collective-permute-start.33 = (bf16[20,1280]{1,0:T(8,128)(2,1)S(1)}, bf16[20,1280]{1,0:T(8,128)(2,1)S(1)}, u32[]{:S(2)}, u32[]{:S(2)}) collective-permute-start(bf16[20,1280]{1,0:T(8,128)(2,1)S(1)} %add_convert_fusion.2), channel_id=1, source_target_pairs={{0,12},{1,13},{2,14},{3,15},{4,8},{5,9},{6,10},{7,11},{8,4},{9,5},... | collective-permute-start | bytes 153608 | tf_op jit(solution)/shard_map/ppermute | solution.py:324
  147.2 7.0 %collective-permute-start.34 = (bf16[20,1280]{1,0:T(8,128)(2,1)S(1)}, bf16[20,1280]{1,0:T(8,128)(2,1)S(1)}, u32[]{:S(2)}, u32[]{:S(2)}) collective-permute-start(bf16[20,1280]{1,0:T(8,128)(2,1)S(1)} %add_convert_fusion.1), channel_id=1, source_target_pairs={{0,0},{1,4},{2,8},{3,12},{4,64},{5,68},{6,72},{7,76},{8,128},{9,13... | collective-permute-start | bytes 153608 | tf_op jit(solution)/shard_map/ppermute | solution.py:435
  (14 other events, 70.7 us)

commit v3 on v2

--- a/solution.py
+++ b/solution.py
@@ -416,24 +416,28 @@
     rows = [lax.dynamic_index_in_dim(rows, across ^ step, 0, keepdims=False) for step in range(GROUP)]
     summed = [rows[0]] + [swap(rows[step], "dp", step) for step in range(1, GROUP)]
     opposite = [swap(array, "ctx", 1) for array in crossed]
-
-    place, summed, part2, last, opposite, sent = tie((place, summed, part2, last, opposite, (backs[1], backs[3])))
-    part3, part1 = swap(sent[1], "ctx", 3), swap(sent[0], "ctx", 1)
+    part1 = swap(backs[1], "ctx", 1)
+
+    def deal(which):
+        sets = list(zip(window, sibling, crossed, opposite))
+        other, block = (1, 0) if which == 0 else (2, which - 1)
+        return deal_tiles(place, tile_perm[0], tile_counts[0], sets[0], sets[other], (which, block))
+
+    dealt = [deal(0)]
+
+    place, summed, part1, part2, last, opposite, dealt, sent = tie(
+        (place, summed, part1, part2, last, opposite, dealt, backs[3])
+    )
+    part3 = swap(sent, "ctx", 3)
     crossed.append(last)
     opposite.append(swap(last, "ctx", 1))
     share = total(summed).astype(BF)
-    sets = list(zip(window, sibling, crossed, opposite))
-
-    def deal(which):
-        other, block = (1, 0) if which == 0 else (2, which - 1)
-        return deal_tiles(place, tile_perm[0], tile_counts[0], sets[0], sets[other], (which, block))
-
-    dealt = [deal(0), deal(1), deal(2)]
     around = [share] + [swap(share, "ctx", step * GROUP) for step in range(1, GROUP)]
 
-    place, part1, part3, dealt, around = tie((place, part1, part3, dealt, around))
+    place, part3, opposite, around = tie((place, part3, opposite, around))
     share = lax.ppermute(total(around).astype(BF), ("dp", "ctx"), share_route(GROUP))
     full = join_heads(place, (backs[0], part1, part2, part3), cos, sin)
+    dealt += [deal(1), deal(2)]
     return (*[array[None] for array in dealt], *[array[None] for array in full], share.astype(F32))
 
 

time: 156 us -> 162 us (1.038)
  waiting for transfers between devices: 23.9 us -> 33 us
    ppermute x33, waiting for transfers between devices: 23.9 us -> 33 us  [swap(): return lax.ppermute(array, axis, [(i, i ^ distance) for i in range(count)])]
    ppermute x33, starting transfers between devices: 46.6 us -> 44.6 us  [swap(): return lax.ppermute(array, axis, [(i, i ^ distance) for i in range(count)])]
  transfers between devices with their start and end apart: 35 -> 35, of which waited for: 8 -> 8; matrix products, arithmetic and copies ran while one was open for 2% -> 2% of each run, Pallas kernels for 42% -> 40%
where the time goes in v3:
time: 162 us; the launch traced here: 161 us
  Pallas kernels  68.3 us (42%)
  starting transfers between devices  51.8 us (32%)
  waiting for transfers between devices  33 us (20%)
  other arithmetic  4.14 us (3%)
  local copies, waits for them, and re-layouts  3.05 us (2%)
    ppermute x33, starting transfers between devices, swap(): return lax.ppermute(array, axis, [(i, i ^ distance) for i in range(count)])  44.6 us
    ppermute x33, waiting for transfers between devices, swap(): return lax.ppermute(array, axis, [(i, i ^ distance) for i in range(count)])  33 us
    pallas_call x2, Pallas kernels, window_grads(): pl.pallas_call(window_kernel, grid=(1,), out_shape=[jax.ShapeDtypeStruct(...  15.9 us
    pallas_call x1, Pallas kernels, full_grads(): pl.pallas_call(grads_kernel, grid=(HEADS // GROUP,), out_shape=[jax.Shape...  15.4 us
    pallas_call x1, Pallas kernels, full_probs(): pl.pallas_call(probs_kernel, grid=(heads,), out_shape=[jax.ShapeDtypeStru...  15.2 us
    pallas_call x3, Pallas kernels, deal_tiles(): pl.pallas_call(deal_kernel, grid=(1,), out_shape=jax.ShapeDtypeStruct((CA...  9.56 us
    pallas_call x1, Pallas kernels, weight_shares(): pl.pallas_call(share_kernel, out_shape=[jax.ShapeDtypeStruct((HEAD_DIM, D...  5.32 us
    ppermute x1, starting transfers between devices, shards(): lax.ppermute(total(around).astype(BF), ('dp', 'ctx'), share_route(GROUP))  4.07 us
  transfers between devices with their start and end apart: 35, of which 8 were waited for; matrix products, arithmetic and copies ran while one was open for 2% of the time, Pallas kernels for 40%

profile of v3, /device:TPU:1, one launch (start us, length us, event | category | flops | bytes accessed | tf_op | source)
XLA Modules:
  0.0 161.5 jit_solution(1872152643935274853)
XLA Ops:
  0.7 0.7 slice_convert_fusion.1
  1.5 0.8 fusion
  2.9 3.6 %split_heads.1 = (bf16[960,256]{1,0:T(8,128)(2,1)}, bf16[960,256]{1,0:T(8,128)(2,1)}, bf16[960,256]{1,0:T(8,128)(2,1)}, bf16[960,256]{1,0:T(8,128)(2,1)}) custom-call(s32[3]{0:T(128)} %pad_add_fusion.place.refs_0_, bf16[256,1280]{1,0:T(8,128)(2,1)} %bitcast.43, bf16[256,1280]{1,0:T(8,128)(2,1)} %bitcast.44, bf16[256,1280]{1,0:T(8,128)(2,1)} %bitcast.45, ...), custom_call_target="tpu_custom_call" | custom-call | flops 100000 | bytes 100000 | tf_op jit(solution)/shard_map/split_heads/pallas_call | solution.py:80
  6.5 3.2 %collective-permute-start.1 = (bf16[960,256]{1,0:T(8,128)(2,1)}, bf16[960,256]{1,0:T(8,128)(2,1)S(1)}, u32[]{:S(2)}, u32[]{:S(2)}) collective-permute-start(bf16[960,256]{1,0:T(8,128)(2,1)} %get-tuple-element.108), channel_id=1, source_target_pairs={{0,1},{1,0},{2,3},{3,2},{4,5},{5,4},{6,7},{7,6},{8,9},{9,8},{10,11... | collective-permute-start | bytes 1474568 | tf_op jit(solution)/shard_map/ppermute | solution.py:324
  9.7 3.2 %collective-permute-start = (bf16[20,1280]{1,0:T(8,128)(2,1)S(1)}, bf16[20,1280]{1,0:T(8,128)(2,1)S(1)}, u32[]{:S(2)}, u32[]{:S(2)}) collective-permute-start(bf16[20,1280]{1,0:T(8,128)(2,1)S(1)} %copy-done.26), channel_id=1, source_target_pairs={{0,0},{4,1},{8,2},{12,3},{64,4},{68,5},{72,6},{76,7},{128,8},{132,... | collective-permute-start | bytes 153608 | tf_op jit(solution)/shard_map/ppermute | solution.py:373
  12.9 8.0 %window_grads.2.refs_0_ = bf16[768,640]{1,0:T(8,128)(2,1)} custom-call(s32[3]{0:T(128)} %pad_add_fusion.place.refs_0_, bf16[256,1280]{1,0:T(8,128)(2,1)} %bitcast.29, bf16[256,1280]{1,0:T(8,128)(2,1)} %bitcast.31, bf16[256,1280]{1,0:T(8,128)(2,1)} %bitcast.33, bf16[256,1280]{1,0:T(8,128)(2,1)} %bitcast.35, f32[40,256]{1,0:T(8,128)} %get-tuple-element.208.cos_ref, ...), custom_call_target="tpu_custom_call" | custom-call | flops 100000 | bytes 100000 | tf_op jit(solution)/shard_map/window_grads/pallas_call | solution.py:130
  20.9 3.3 %collective-permute-done.2.piece2.refs_3_ = bf16[960,256]{1,0:T(8,128)(2,1)} collective-permute-done((bf16[960,256]{1,0:T(8,128)(2,1)}, bf16[960,256]{1,0:T(8,128)(2,1)}, u32[]{:S(2)}, u32[]{:S(2)}) %collective-permute-start.2) | collective-permute-done | bytes 491552 | tf_op jit(solution)/shard_map/ppermute | solution.py:324
  24.2 1.2 collective-permute-start.3
  25.4 4.1 %collective-permute-start.4 = (bf16[960,256]{1,0:T(8,128)(2,1)S(1)}, bf16[960,256]{1,0:T(8,128)(2,1)S(1)}, u32[]{:S(2)}, u32[]{:S(2)}) collective-permute-start(bf16[960,256]{1,0:T(8,128)(2,1)S(1)} %copy-done.25), channel_id=1, source_target_pairs={{0,3},{1,2},{2,1},{3,0},{4,7},{5,6},{6,5},{7,4},{8,11},{9,10},{10,... | collective-permute-start | bytes 1474568 | tf_op jit(solution)/shard_map/ppermute | solution.py:324
  29.4 0.8 collective-permute-start.5
  30.2 3.1 %collective-permute-start.6 = (bf16[20,1280]{1,0:T(8,128)(2,1)S(1)}, bf16[20,1280]{1,0:T(8,128)(2,1)S(1)}, u32[]{:S(2)}, u32[]{:S(2)}) collective-permute-start(bf16[20,1280]{1,0:T(8,128)(2,1)S(1)} %collective-permute-done), channel_id=1, source_target_pairs={{0,128},{64,192},{128,0},{192,64},{1,129},{65,193},{129,1},{193,65... | collective-permute-start | bytes 153608 | tf_op jit(solution)/shard_map/ppermute | solution.py:324
  33.3 7.9 %window_grads.3 = (bf16[256,640]{1,0:T(8,128)(2,1)}, bf16[512,640]{1,0:T(8,128)(2,1)}) custom-call(s32[3]{0:T(128)} %pad_add_fusion.place.refs_0_, bf16[256,1280]{1,0:T(8,128)(2,1)} %bitcast.30, bf16[256,1280]{1,0:T(8,128)(2,1)} %bitcast.32, bf16[256,1280]{1,0:T(8,128)(2,1)} %bitcast.34, bf16[256,1280]{1,0:T(8,128)(2,1)} %bitcast.36, ...), custom_call_target="tpu_custom_call" | custom-call | flops 100000 | bytes 100000 | tf_op jit(solution)/shard_map/window_grads/pallas_call | solution.py:130
  41.3 1.1 collective-permute-start.8
  43.0 1.4 collective-permute-start.10
  44.4 2.6 %collective-permute-start.11 = (bf16[80,1280]{1,0:T(8,128)(2,1)S(1)}, bf16[80,1280]{1,0:T(8,128)(2,1)S(1)}, u32[]{:S(2)}, u32[]{:S(2)}) collective-permute-start(bf16[80,1280]{1,0:T(8,128)(2,1)S(1)} %pad_maximum_fusion.refs_6_), channel_id=1, source_target_pairs={{0,32},{1,33},{2,34},{3,35},{4,36},{5,37},{6,38},{7,39},{8,40},{9,... | collective-permute-start | bytes 614408 | tf_op jit(solution)/shard_map/ppermute | solution.py:324
  47.0 15.2 %full_probs.1 = (bf16[4,1024,1024]{2,1,0:T(8,128)(2,1)}, f32[320,1024]{1,0:T(8,128)}, f32[4,1,1024]{2,1,0:T(1,128)}) custom-call(s32[3]{0:T(128)} %pad_add_fusion.place.refs_0_, bf16[960,256]{1,0:T(8,128)(2,1)} %get-tuple-element.118.piece0.refs_1_, bf16[960,256]{1,0:T(8,128)(2,1)} %copy-done.8, bf16[960,256]{1,0:T(8,128)(2,1)} %collective-permute-done.2.piece2.refs_3_, ...), custom_call_target="tpu_custom_call" | custom-call | flops 100000 | bytes 100000 | tf_op jit(solution)/shard_map/full_probs/pallas_call | solution.py:169
  62.3 1.1 collective-permute-start.19
  63.4 1.4 collective-permute-start.13
  65.8 0.7 collective-permute-done.13.refs_5_
  66.5 0.8 copy-done.14
  67.4 5.3 %weight_shares.1 = (bf16[80,1280]{1,0:T(8,128)(2,1)}, bf16[80,1280]{1,0:T(8,128)(2,1)}, bf16[80,1280]{1,0:T(8,128)(2,1)}, bf16[80,1280]{1,0:T(8,128)(2,1)}, bf16[320,1024]{1,0:T(8,128)(2,1)}) custom-call(s32[3]{0:T(128)} %pad_add_fusion.place.refs_0_, f32[320,1024]{1,0:T(8,128)} %get-tuple-element.133.refs_1_.refs_6_, bf16[256,1280]{1,0:T(8,128)(2,1)} %bitcast.40, ...), custom_call_target="tpu_custom_call" | custom-call | flops 100000 | bytes 100000 | tf_op jit(solution)/shard_map/weight_shares/pallas_call | solution.py:202
  72.7 0.7 copy-done.16
  73.5 3.8 %collective-permute-start.17 = (bf16[80,1280]{1,0:T(8,128)(2,1)}, bf16[80,1280]{1,0:T(8,128)(2,1)}, u32[]{:S(2)}, u32[]{:S(2)}) collective-permute-start(bf16[80,1280]{1,0:T(8,128)(2,1)} %get-tuple-element.157), channel_id=1, source_target_pairs={{0,32},{1,33},{2,34},{3,35},{4,36},{5,37},{6,38},{7,39},{8,40},{9,... | collective-permute-start | bytes 614408 | tf_op jit(solution)/shard_map/ppermute | solution.py:324
  77.4 15.4 %full_grads.1 = (bf16[960,256]{1,0:T(8,128)(2,1)}, bf16[960,256]{1,0:T(8,128)(2,1)}, bf16[960,256]{1,0:T(8,128)(2,1)}, bf16[960,256]{1,0:T(8,128)(2,1)}) custom-call(s32[3]{0:T(128)} %pad_add_fusion.place.refs_0_, bf16[960,256]{1,0:T(8,128)(2,1)} %get-tuple-element.118.piece0.refs_1_, bf16[960,256]{1,0:T(8,128)(2,1)} %copy-done.8, ...), custom_call_target="tpu_custom_call" | custom-call | flops 100000 | bytes 100000 | tf_op jit(solution)/shard_map/full_grads/pallas_call | solution.py:240
  92.8 1.2 collective-permute-start.27
  94.0 1.1 add_convert_fusion
  95.2 0.8 collective-permute-start.26
  96.6 0.7 collective-permute-start.25
  97.3 0.7 dynamic-slice_bitcast_fusion
  98.5 2.8 %collective-permute-done.21 = bf16[20,1280]{1,0:T(8,128)(2,1)S(1)} collective-permute-done((bf16[20,1280]{1,0:T(8,128)(2,1)S(1)}, bf16[20,1280]{1,0:T(8,128)(2,1)S(1)}, u32[]{:S(2)}, u32[]{:S(2)}) %collective-permute-start.21) | collective-permute-done | bytes 51232 | tf_op jit(solution)/shard_map/ppermute | solution.py:324
  101.4 1.1 collective-permute-start.28
  102.5 1.5 collective-permute-done.28.refs_7_
  104.0 2.9 %collective-permute-start.22 = (bf16[20,1280]{1,0:T(8,128)(2,1)}, bf16[20,1280]{1,0:T(8,128)(2,1)S(1)}, u32[]{:S(2)}, u32[]{:S(2)}) collective-permute-start(bf16[20,1280]{1,0:T(8,128)(2,1)} %get-tuple-element.200), channel_id=1, source_target_pairs={{0,128},{64,192},{128,0},{192,64},{1,129},{65,193},{129,1},{193,65... | collective-permute-start | bytes 153608 | tf_op jit(solution)/shard_map/ppermute | solution.py:324
  106.9 0.8 collective-permute-start.23
  107.7 0.7 copy.22.counts
  108.3 3.2 %deal_tiles.3 = bf16[512,1280]{1,0:T(8,128)(2,1)} custom-call(s32[3]{0:T(128)} %pad_add_fusion.place.refs_0_, s32[16,16]{1,0:T(8,128)} %bitcast.46, s32[16,4]{1,0:T(8,128)} %copy.22.counts, bf16[768,640]{1,0:T(8,128)(2,1)} %window_grads.2.refs_0_, bf16[768,640]{1,0:T(8,128)(2,1)} %copy-done.1, bf16[768,640]{1,0:T(8,128)(2,1)} %copy-done.2, ...), custom_call_target="tpu_custom_call" | custom-call | flops 100000 | bytes 100000 | tf_op jit(solution)/shard_map/deal_tiles/pallas_call | solution.py:310
  111.6 10.4 %collective-permute-done.25.part2 = bf16[960,256]{1,0:T(8,128)(2,1)} collective-permute-done((bf16[960,256]{1,0:T(8,128)(2,1)}, bf16[960,256]{1,0:T(8,128)(2,1)}, u32[]{:S(2)}, u32[]{:S(2)}) %collective-permute-start.25) | collective-permute-done | bytes 491552 | tf_op jit(solution)/shard_map/ppermute | solution.py:324
  122.0 1.1 collective-permute-start.30
  123.1 0.7 collective-permute-start.29
  123.9 3.9 %collective-permute-start.31 = (bf16[20,1280]{1,0:T(8,128)(2,1)S(1)}, bf16[20,1280]{1,0:T(8,128)(2,1)S(1)}, u32[]{:S(2)}, u32[]{:S(2)}) collective-permute-start(bf16[20,1280]{1,0:T(8,128)(2,1)S(1)} %add_convert_fusion.2), channel_id=1, source_target_pairs={{0,4},{1,5},{2,6},{3,7},{4,0},{5,1},{6,2},{7,3},{8,12},{9,13},{10,... | collective-permute-start | bytes 153608 | tf_op jit(solution)/shard_map/ppermute | solution.py:324
  127.8 4.8 %collective-permute-start.32 = (bf16[20,1280]{1,0:T(8,128)(2,1)S(1)}, bf16[20,1280]{1,0:T(8,128)(2,1)S(1)}, u32[]{:S(2)}, u32[]{:S(2)}) collective-permute-start(bf16[20,1280]{1,0:T(8,128)(2,1)S(1)} %add_convert_fusion.2), channel_id=1, source_target_pairs={{0,8},{1,9},{2,10},{3,11},{4,12},{5,13},{6,14},{7,15},{8,0},{9,1},... | collective-permute-start | bytes 153608 | tf_op jit(solution)/shard_map/ppermute | solution.py:324
  132.6 3.1 %collective-permute-done.31 = bf16[20,1280]{1,0:T(8,128)(2,1)S(1)} collective-permute-done((bf16[20,1280]{1,0:T(8,128)(2,1)S(1)}, bf16[20,1280]{1,0:T(8,128)(2,1)S(1)}, u32[]{:S(2)}, u32[]{:S(2)}) %collective-permute-start.31) | collective-permute-done | bytes 51232 | tf_op jit(solution)/shard_map/ppermute | solution.py:324
  135.7 9.2 %collective-permute-done.32 = bf16[20,1280]{1,0:T(8,128)(2,1)S(1)} collective-permute-done((bf16[20,1280]{1,0:T(8,128)(2,1)S(1)}, bf16[20,1280]{1,0:T(8,128)(2,1)S(1)}, u32[]{:S(2)}, u32[]{:S(2)}) %collective-permute-start.32) | collective-permute-done | bytes 51232 | tf_op jit(solution)/shard_map/ppermute | solution.py:324
  144.9 2.0 %collective-permute-done.33 = bf16[20,1280]{1,0:T(8,128)(2,1)S(1)} collective-permute-done((bf16[20,1280]{1,0:T(8,128)(2,1)S(1)}, bf16[20,1280]{1,0:T(8,128)(2,1)S(1)}, u32[]{:S(2)}, u32[]{:S(2)}) %collective-permute-start.33) | collective-permute-done | bytes 51232 | tf_op jit(solution)/shard_map/ppermute | solution.py:324
  146.9 4.1 %collective-permute-start.34 = (bf16[20,1280]{1,0:T(8,128)(2,1)S(1)}, bf16[20,1280]{1,0:T(8,128)(2,1)S(1)}, u32[]{:S(2)}, u32[]{:S(2)}) collective-permute-start(bf16[20,1280]{1,0:T(8,128)(2,1)S(1)} %add_convert_fusion.1), channel_id=1, source_target_pairs={{0,0},{1,4},{2,8},{3,12},{4,64},{5,68},{6,72},{7,76},{8,128},{9,13... | collective-permute-start | bytes 153608 | tf_op jit(solution)/shard_map/ppermute | solution.py:438
  151.0 3.2 %deal_tiles.5 = bf16[512,1280]{1,0:T(8,128)(2,1)} custom-call(s32[3]{0:T(128)} %pad_add_fusion.place.refs_0_, s32[16,16]{1,0:T(8,128)} %bitcast.47, s32[16,4]{1,0:T(8,128)} %copy.22.counts, bf16[768,640]{1,0:T(8,128)(2,1)} %window_grads.2.refs_0_, bf16[768,640]{1,0:T(8,128)(2,1)} %copy-done.1, bf16[768,640]{1,0:T(8,128)(2,1)} %copy-done.2, ...), custom_call_target="tpu_custom_call" | custom-call | flops 100000 | bytes 100000 | tf_op jit(solution)/shard_map/deal_tiles/pallas_call | solution.py:310
  154.2 3.2 %deal_tiles.4 = bf16[512,1280]{1,0:T(8,128)(2,1)} custom-call(s32[3]{0:T(128)} %pad_add_fusion.place.refs_0_, s32[16,16]{1,0:T(8,128)} %bitcast.48, s32[16,4]{1,0:T(8,128)} %copy.22.counts, bf16[768,640]{1,0:T(8,128)(2,1)} %window_grads.2.refs_0_, bf16[768,640]{1,0:T(8,128)(2,1)} %copy-done.1, bf16[768,640]{1,0:T(8,128)(2,1)} %copy-done.2, ...), custom_call_target="tpu_custom_call" | custom-call | flops 100000 | bytes 100000 | tf_op jit(solution)/shard_map/deal_tiles/pallas_call | solution.py:310
  157.3 3.5 %join_heads.1 = (bf16[256,1280]{1,0:T(8,128)(2,1)}, bf16[256,1280]{1,0:T(8,128)(2,1)}, bf16[256,1280]{1,0:T(8,128)(2,1)}) custom-call(s32[3]{0:T(128)} %pad_add_fusion.place.refs_0_, bf16[960,256]{1,0:T(8,128)(2,1)} %get-tuple-element.188.part0, bf16[960,256]{1,0:T(8,128)(2,1)} %collective-permute-done.24.part1, ...), custom_call_target="tpu_custom_call" | custom-call | flops 100000 | bytes 100000 | tf_op jit(solution)/shard_map/join_heads/pallas_call | solution.py:269
  (100 shorter events, 4.5 us)
Async XLA Ops:
  6.5 14.4 %collective-permute-start.1 = (bf16[960,256]{1,0:T(8,128)(2,1)}, bf16[960,256]{1,0:T(8,128)(2,1)S(1)}, u32[]{:S(2)}, u32[]{:S(2)}) collective-permute-start(bf16[960,256]{1,0:T(8,128)(2,1)} %get-tuple-element.108), channel_id=1, source_target_pairs={{0,1},{1,0},{2,3},{3,2},{4,5},{5,4},{6,7},{7,6},{8,9},{9,8},{10,11... | collective-permute-start | bytes 1474568 | tf_op jit(solution)/shard_map/ppermute | solution.py:324
  9.7 14.5 %collective-permute-start.2 = (bf16[960,256]{1,0:T(8,128)(2,1)}, bf16[960,256]{1,0:T(8,128)(2,1)}, u32[]{:S(2)}, u32[]{:S(2)}) collective-permute-start(bf16[960,256]{1,0:T(8,128)(2,1)} %get-tuple-element.109), channel_id=1, source_target_pairs={{0,2},{1,3},{2,0},{3,1},{4,6},{5,7},{6,4},{7,5},{8,10},{9,11},{10,... | collective-permute-start | bytes 1474568 | tf_op jit(solution)/shard_map/ppermute | solution.py:324
  9.7 11.2 %collective-permute-start = (bf16[20,1280]{1,0:T(8,128)(2,1)S(1)}, bf16[20,1280]{1,0:T(8,128)(2,1)S(1)}, u32[]{:S(2)}, u32[]{:S(2)}) collective-permute-start(bf16[20,1280]{1,0:T(8,128)(2,1)S(1)} %copy-done.26), channel_id=1, source_target_pairs={{0,0},{4,1},{8,2},{12,3},{64,4},{68,5},{72,6},{76,7},{128,8},{132,... | collective-permute-start | bytes 153608 | tf_op jit(solution)/shard_map/ppermute | solution.py:373
  12.9 12.5 %copy-start.25 = (bf16[960,256]{1,0:T(8,128)(2,1)S(1)}, bf16[960,256]{1,0:T(8,128)(2,1)}, u32[]{:S(2)}) copy-start(bf16[960,256]{1,0:T(8,128)(2,1)} %get-tuple-element.115) | copy-start | bytes 1474564
  20.9 20.3 %copy-start.8 = (bf16[960,256]{1,0:T(8,128)(2,1)}, bf16[960,256]{1,0:T(8,128)(2,1)S(1)}, u32[]{:S(2)}) copy-start(bf16[960,256]{1,0:T(8,128)(2,1)S(1)} %collective-permute-done.1.piece1.refs_2_) | copy-start | bytes 1474564
  24.2 17.1 %collective-permute-start.3 = (bf16[768,640]{1,0:T(8,128)(2,1)}, bf16[768,640]{1,0:T(8,128)(2,1)S(1)}, u32[]{:S(2)}, u32[]{:S(2)}) collective-permute-start(bf16[768,640]{1,0:T(8,128)(2,1)} %window_grads.2.refs_0_), channel_id=1, source_target_pairs={{0,1},{1,0},{2,3},{3,2},{4,5},{5,4},{6,7},{7,6},{8,9},{9,8},{10,11... | collective-permute-start | bytes 2949128 | tf_op jit(solution)/shard_map/ppermute | solution.py:324
  25.4 15.9 %collective-permute-start.4 = (bf16[960,256]{1,0:T(8,128)(2,1)S(1)}, bf16[960,256]{1,0:T(8,128)(2,1)S(1)}, u32[]{:S(2)}, u32[]{:S(2)}) collective-permute-start(bf16[960,256]{1,0:T(8,128)(2,1)S(1)} %copy-done.25), channel_id=1, source_target_pairs={{0,3},{1,2},{2,1},{3,0},{4,7},{5,6},{6,5},{7,4},{8,11},{9,10},{10,... | collective-permute-start | bytes 1474568 | tf_op jit(solution)/shard_map/ppermute | solution.py:324
  29.4 11.8 %collective-permute-start.5 = (bf16[20,1280]{1,0:T(8,128)(2,1)S(1)}, bf16[20,1280]{1,0:T(8,128)(2,1)S(1)}, u32[]{:S(2)}, u32[]{:S(2)}) collective-permute-start(bf16[20,1280]{1,0:T(8,128)(2,1)S(1)} %collective-permute-done), channel_id=1, source_target_pairs={{0,64},{64,0},{128,192},{192,128},{1,65},{65,1},{129,193},{193,129... | collective-permute-start | bytes 153608 | tf_op jit(solution)/shard_map/ppermute | solution.py:324
  30.2 11.0 %collective-permute-start.6 = (bf16[20,1280]{1,0:T(8,128)(2,1)S(1)}, bf16[20,1280]{1,0:T(8,128)(2,1)S(1)}, u32[]{:S(2)}, u32[]{:S(2)}) collective-permute-start(bf16[20,1280]{1,0:T(8,128)(2,1)S(1)} %collective-permute-done), channel_id=1, source_target_pairs={{0,128},{64,192},{128,0},{192,64},{1,129},{65,193},{129,1},{193,65... | collective-permute-start | bytes 153608 | tf_op jit(solution)/shard_map/ppermute | solution.py:324
  33.3 7.9 %collective-permute-start.7 = (bf16[20,1280]{1,0:T(8,128)(2,1)S(1)}, bf16[20,1280]{1,0:T(8,128)(2,1)S(1)}, u32[]{:S(2)}, u32[]{:S(2)}) collective-permute-start(bf16[20,1280]{1,0:T(8,128)(2,1)S(1)} %collective-permute-done), channel_id=1, source_target_pairs={{0,192},{64,128},{128,64},{192,0},{1,193},{65,129},{129,65},{193,1... | collective-permute-start | bytes 153608 | tf_op jit(solution)/shard_map/ppermute | solution.py:324
  41.3 20.9 %copy-start.1 = (bf16[768,640]{1,0:T(8,128)(2,1)}, bf16[768,640]{1,0:T(8,128)(2,1)S(1)}, u32[]{:S(2)}) copy-start(bf16[768,640]{1,0:T(8,128)(2,1)S(1)} %collective-permute-done.3.refs_1_) | copy-start | bytes 2949124
  41.3 20.9 %collective-permute-start.8 = (bf16[256,1280]{1,0:T(8,128)(2,1)S(1)}, bf16[256,1280]{1,0:T(8,128)(2,1)S(1)}, u32[]{:S(2)}, u32[]{:S(2)}) collective-permute-start(bf16[256,1280]{1,0:T(8,128)(2,1)S(1)} %bitcast.41), channel_id=1, source_target_pairs={{0,1},{1,0},{2,3},{3,2},{4,5},{5,4},{6,7},{7,6},{8,9},{9,8},{10,11... | collective-permute-start | bytes 1966088 | tf_op jit(solution)/shard_map/ppermute | solution.py:324
  42.4 19.9 %collective-permute-start.9 = (bf16[256,1280]{1,0:T(8,128)(2,1)S(1)}, bf16[256,1280]{1,0:T(8,128)(2,1)S(1)}, u32[]{:S(2)}, u32[]{:S(2)}) collective-permute-start(bf16[256,1280]{1,0:T(8,128)(2,1)S(1)} %bitcast.42), channel_id=1, source_target_pairs={{0,2},{1,3},{2,0},{3,1},{4,6},{5,7},{6,4},{7,5},{8,10},{9,11},{10,... | collective-permute-start | bytes 1966088 | tf_op jit(solution)/shard_map/ppermute | solution.py:324
  42.9 19.4 %copy-start = (bf16[768,640]{1,0:T(8,128)(2,1)S(1)}, bf16[768,640]{1,0:T(8,128)(2,1)}, u32[]{:S(2)}) copy-start(bf16[768,640]{1,0:T(8,128)(2,1)} %window_grads.2.refs_0_) | copy-start | bytes 2949124
  42.9 21.9 %copy-start.4 = (bf16[512,640]{1,0:T(8,128)(2,1)S(1)}, bf16[512,640]{1,0:T(8,128)(2,1)}, u32[]{:S(2)}) copy-start(bf16[512,640]{1,0:T(8,128)(2,1)} %get-tuple-element.167.refs_4_) | copy-start | bytes 1966084
  43.0 23.5 %copy-start.10 = (bf16[80,1280]{1,0:T(8,128)(2,1)}, bf16[80,1280]{1,0:T(8,128)(2,1)S(1)}, u32[]{:S(2)}) copy-start(bf16[80,1280]{1,0:T(8,128)(2,1)S(1)} %pad_maximum_fusion.refs_6_) | copy-start | bytes 614404
  43.0 19.2 %collective-permute-start.10 = (bf16[80,1280]{1,0:T(8,128)(2,1)S(1)}, bf16[80,1280]{1,0:T(8,128)(2,1)S(1)}, u32[]{:S(2)}, u32[]{:S(2)}) collective-permute-start(bf16[80,1280]{1,0:T(8,128)(2,1)S(1)} %pad_maximum_fusion.refs_6_), channel_id=1, source_target_pairs={{0,16},{1,17},{2,18},{3,19},{4,20},{5,21},{6,22},{7,23},{8,24},{9,... | collective-permute-start | bytes 614408 | tf_op jit(solution)/shard_map/ppermute | solution.py:324
  44.4 17.8 %collective-permute-start.11 = (bf16[80,1280]{1,0:T(8,128)(2,1)S(1)}, bf16[80,1280]{1,0:T(8,128)(2,1)S(1)}, u32[]{:S(2)}, u32[]{:S(2)}) collective-permute-start(bf16[80,1280]{1,0:T(8,128)(2,1)S(1)} %pad_maximum_fusion.refs_6_), channel_id=1, source_target_pairs={{0,32},{1,33},{2,34},{3,35},{4,36},{5,37},{6,38},{7,39},{8,40},{9,... | collective-permute-start | bytes 614408 | tf_op jit(solution)/shard_map/ppermute | solution.py:324
  47.0 15.2 %collective-permute-start.12 = (bf16[80,1280]{1,0:T(8,128)(2,1)S(1)}, bf16[80,1280]{1,0:T(8,128)(2,1)S(1)}, u32[]{:S(2)}, u32[]{:S(2)}) collective-permute-start(bf16[80,1280]{1,0:T(8,128)(2,1)S(1)} %pad_maximum_fusion.refs_6_), channel_id=1, source_target_pairs={{0,48},{1,49},{2,50},{3,51},{4,52},{5,53},{6,54},{7,55},{8,56},{9,... | collective-permute-start | bytes 614408 | tf_op jit(solution)/shard_map/ppermute | solution.py:324
  62.3 30.5 %collective-permute-start.19 = (bf16[768,640]{1,0:T(8,128)(2,1)S(1)}, bf16[768,640]{1,0:T(8,128)(2,1)S(1)}, u32[]{:S(2)}, u32[]{:S(2)}) collective-permute-start(bf16[768,640]{1,0:T(8,128)(2,1)S(1)} %copy-done), channel_id=1, source_target_pairs={{0,2},{1,3},{2,0},{3,1},{4,6},{5,7},{6,4},{7,5},{8,10},{9,11},{10,... | collective-permute-start | bytes 2949128 | tf_op jit(solution)/shard_map/ppermute | solution.py:324
  63.4 3.1 %collective-permute-start.13 = (bf16[256,1280]{1,0:T(8,128)(2,1)S(1)}, bf16[256,1280]{1,0:T(8,128)(2,1)S(1)}, u32[]{:S(2)}, u32[]{:S(2)}) collective-permute-start(bf16[256,1280]{1,0:T(8,128)(2,1)S(1)} %collective-permute-done.9.refs_4_), channel_id=1, source_target_pairs={{0,1},{1,0},{2,3},{3,2},{4,5},{5,4},{6,7},{7,6},{8,9},{9,8},{10,11... | collective-permute-start | bytes 1966088 | tf_op jit(solution)/shard_map/ppermute | solution.py:324
  64.8 7.9 %collective-permute-start.15 = (bf16[512,640]{1,0:T(8,128)(2,1)S(1)}, bf16[512,640]{1,0:T(8,128)(2,1)S(1)}, u32[]{:S(2)}, u32[]{:S(2)}) collective-permute-start(bf16[512,640]{1,0:T(8,128)(2,1)S(1)} %copy-done.4), channel_id=1, source_target_pairs={{0,1},{1,0},{2,3},{3,2},{4,5},{5,4},{6,7},{7,6},{8,9},{9,8},{10,11... | collective-permute-start | bytes 1966088 | tf_op jit(solution)/shard_map/ppermute | solution.py:324
  64.8 7.9 %collective-permute-start.14 = (bf16[256,640]{1,0:T(8,128)(2,1)}, bf16[256,640]{1,0:T(8,128)(2,1)S(1)}, u32[]{:S(2)}, u32[]{:S(2)}) collective-permute-start(bf16[256,640]{1,0:T(8,128)(2,1)} %get-tuple-element.172.refs_4_), channel_id=1, source_target_pairs={{0,1},{1,0},{2,3},{3,2},{4,5},{5,4},{6,7},{7,6},{8,9},{9,8},{10,11... | collective-permute-start | bytes 983048 | tf_op jit(solution)/shard_map/ppermute | solution.py:324
  65.3 27.5 %collective-permute-start.20 = (bf16[256,640]{1,0:T(8,128)(2,1)}, bf16[256,640]{1,0:T(8,128)(2,1)}, u32[]{:S(2)}, u32[]{:S(2)}) collective-permute-start(bf16[256,640]{1,0:T(8,128)(2,1)} %get-tuple-element.172.refs_4_), channel_id=1, source_target_pairs={{0,2},{1,3},{2,0},{3,1},{4,6},{5,7},{6,4},{7,5},{8,10},{9,11},{10,... | collective-permute-start | bytes 983048 | tf_op jit(solution)/shard_map/ppermute | solution.py:324
  73.4 19.3 %copy-start.5 = (bf16[512,640]{1,0:T(8,128)(2,1)}, bf16[512,640]{1,0:T(8,128)(2,1)S(1)}, u32[]{:S(2)}) copy-start(bf16[512,640]{1,0:T(8,128)(2,1)S(1)} %collective-permute-done.15.refs_5_) | copy-start | bytes 1966084
  73.4 19.3 %collective-permute-start.16 = (bf16[80,1280]{1,0:T(8,128)(2,1)}, bf16[80,1280]{1,0:T(8,128)(2,1)S(1)}, u32[]{:S(2)}, u32[]{:S(2)}) collective-permute-start(bf16[80,1280]{1,0:T(8,128)(2,1)} %get-tuple-element.156), channel_id=1, source_target_pairs={{0,16},{1,17},{2,18},{3,19},{4,20},{5,21},{6,22},{7,23},{8,24},{9,... | collective-permute-start | bytes 614408 | tf_op jit(solution)/shard_map/ppermute | solution.py:324
  73.5 19.3 %collective-permute-start.17 = (bf16[80,1280]{1,0:T(8,128)(2,1)}, bf16[80,1280]{1,0:T(8,128)(2,1)}, u32[]{:S(2)}, u32[]{:S(2)}) collective-permute-start(bf16[80,1280]{1,0:T(8,128)(2,1)} %get-tuple-element.157), channel_id=1, source_target_pairs={{0,32},{1,33},{2,34},{3,35},{4,36},{5,37},{6,38},{7,39},{8,40},{9,... | collective-permute-start | bytes 614408 | tf_op jit(solution)/shard_map/ppermute | solution.py:324
  77.3 15.4 %collective-permute-start.18 = (bf16[80,1280]{1,0:T(8,128)(2,1)}, bf16[80,1280]{1,0:T(8,128)(2,1)}, u32[]{:S(2)}, u32[]{:S(2)}) collective-permute-start(bf16[80,1280]{1,0:T(8,128)(2,1)} %get-tuple-element.158), channel_id=1, source_target_pairs={{0,48},{1,49},{2,50},{3,51},{4,52},{5,53},{6,54},{7,55},{8,56},{9,... | collective-permute-start | bytes 614408 | tf_op jit(solution)/shard_map/ppermute | solution.py:324
  77.4 16.7 %copy-start.19 = (bf16[80,1280]{1,0:T(8,128)(2,1)S(1)}, bf16[80,1280]{1,0:T(8,128)(2,1)}, u32[]{:S(2)}) copy-start(bf16[80,1280]{1,0:T(8,128)(2,1)} %get-tuple-element.161) | copy-start | bytes 614404
  92.7 14.9 %copy-start.23 = (s32[1,16,4]{1,2,0:T(4,128)S(1)}, s32[1,16,4]{1,2,0:T(4,128)}, u32[]{:S(2)}) copy-start(s32[1,16,4]{1,2,0:T(4,128)} %param.23) | copy-start | bytes 772
  92.8 15.5 %copy-start.2 = (bf16[768,640]{1,0:T(8,128)(2,1)}, bf16[768,640]{1,0:T(8,128)(2,1)S(1)}, u32[]{:S(2)}) copy-start(bf16[768,640]{1,0:T(8,128)(2,1)S(1)} %collective-permute-done.19.refs_2_) | copy-start | bytes 2949124
  92.8 14.1 %collective-permute-start.27 = (bf16[768,640]{1,0:T(8,128)(2,1)S(1)}, bf16[768,640]{1,0:T(8,128)(2,1)S(1)}, u32[]{:S(2)}, u32[]{:S(2)}) collective-permute-start(bf16[768,640]{1,0:T(8,128)(2,1)S(1)} %collective-permute-done.19.refs_2_), channel_id=1, source_target_pairs={{0,1},{1,0},{2,3},{3,2},{4,5},{5,4},{6,7},{7,6},{8,9},{9,8},{10,11... | collective-permute-start | bytes 2949128 | tf_op jit(solution)/shard_map/ppermute | solution.py:324
  95.2 26.8 %collective-permute-start.26 = (bf16[512,640]{1,0:T(8,128)(2,1)S(1)}, bf16[512,640]{1,0:T(8,128)(2,1)S(1)}, u32[]{:S(2)}, u32[]{:S(2)}) collective-permute-start(bf16[512,640]{1,0:T(8,128)(2,1)S(1)} %copy-done.4), channel_id=1, source_target_pairs={{0,2},{1,3},{2,0},{3,1},{4,6},{5,7},{6,4},{7,5},{8,10},{9,11},{10,... | collective-permute-start | bytes 1966088 | tf_op jit(solution)/shard_map/ppermute | solution.py:324
  96.1 15.5 %collective-permute-start.24 = (bf16[960,256]{1,0:T(8,128)(2,1)}, bf16[960,256]{1,0:T(8,128)(2,1)}, u32[]{:S(2)}, u32[]{:S(2)}) collective-permute-start(bf16[960,256]{1,0:T(8,128)(2,1)} %get-tuple-element.165), channel_id=1, source_target_pairs={{0,1},{1,0},{2,3},{3,2},{4,5},{5,4},{6,7},{7,6},{8,9},{9,8},{10,11... | collective-permute-start | bytes 1474568 | tf_op jit(solution)/shard_map/ppermute | solution.py:324
  96.6 25.4 %collective-permute-start.25 = (bf16[960,256]{1,0:T(8,128)(2,1)}, bf16[960,256]{1,0:T(8,128)(2,1)}, u32[]{:S(2)}, u32[]{:S(2)}) collective-permute-start(bf16[960,256]{1,0:T(8,128)(2,1)} %get-tuple-element.166), channel_id=1, source_target_pairs={{0,2},{1,3},{2,0},{3,1},{4,6},{5,7},{6,4},{7,5},{8,10},{9,11},{10,... | collective-permute-start | bytes 1474568 | tf_op jit(solution)/shard_map/ppermute | solution.py:324
  98.0 3.4 %collective-permute-start.21 = (bf16[20,1280]{1,0:T(8,128)(2,1)S(1)}, bf16[20,1280]{1,0:T(8,128)(2,1)S(1)}, u32[]{:S(2)}, u32[]{:S(2)}) collective-permute-start(bf16[20,1280]{1,0:T(8,128)(2,1)S(1)} %get-tuple-element.201), channel_id=1, source_target_pairs={{0,64},{64,0},{128,192},{192,128},{1,65},{65,1},{129,193},{193,129... | collective-permute-start | bytes 153608 | tf_op jit(solution)/shard_map/ppermute | solution.py:324
  101.4 2.6 %collective-permute-start.28 = (bf16[256,640]{1,0:T(8,128)(2,1)}, bf16[256,640]{1,0:T(8,128)(2,1)S(1)}, u32[]{:S(2)}, u32[]{:S(2)}) collective-permute-start(bf16[256,640]{1,0:T(8,128)(2,1)} %collective-permute-done.20.refs_6_), channel_id=1, source_target_pairs={{0,1},{1,0},{2,3},{3,2},{4,5},{5,4},{6,7},{7,6},{8,9},{9,8},{10,11... | collective-permute-start | bytes 983048 | tf_op jit(solution)/shard_map/ppermute | solution.py:324
  104.0 7.6 %collective-permute-start.22 = (bf16[20,1280]{1,0:T(8,128)(2,1)}, bf16[20,1280]{1,0:T(8,128)(2,1)S(1)}, u32[]{:S(2)}, u32[]{:S(2)}) collective-permute-start(bf16[20,1280]{1,0:T(8,128)(2,1)} %get-tuple-element.200), channel_id=1, source_target_pairs={{0,128},{64,192},{128,0},{192,64},{1,129},{65,193},{129,1},{193,65... | collective-permute-start | bytes 153608 | tf_op jit(solution)/shard_map/ppermute | solution.py:324
  106.9 4.7 %collective-permute-start.23 = (bf16[20,1280]{1,0:T(8,128)(2,1)}, bf16[20,1280]{1,0:T(8,128)(2,1)S(1)}, u32[]{:S(2)}, u32[]{:S(2)}) collective-permute-start(bf16[20,1280]{1,0:T(8,128)(2,1)} %get-tuple-element.199), channel_id=1, source_target_pairs={{0,192},{64,128},{128,64},{192,0},{1,193},{65,129},{129,65},{193,1... | collective-permute-start | bytes 153608 | tf_op jit(solution)/shard_map/ppermute | solution.py:324
  108.3 14.8 %copy-start.24 = (bf16[960,256]{1,0:T(8,128)(2,1)S(1)}, bf16[960,256]{1,0:T(8,128)(2,1)}, u32[]{:S(2)}) copy-start(bf16[960,256]{1,0:T(8,128)(2,1)} %get-tuple-element.177) | copy-start | bytes 1474564
  108.3 15.5 %copy-start.18 = (bf16[20,1280]{1,0:T(8,128)(2,1)S(1)}, bf16[20,1280]{1,0:T(8,128)(2,1)}, u32[]{:S(2)}) copy-start(bf16[20,1280]{1,0:T(8,128)(2,1)} %get-tuple-element.180) | copy-start | bytes 153604
  122.0 29.0 %copy-start.6 = (bf16[512,640]{1,0:T(8,128)(2,1)}, bf16[512,640]{1,0:T(8,128)(2,1)S(1)}, u32[]{:S(2)}) copy-start(bf16[512,640]{1,0:T(8,128)(2,1)S(1)} %collective-permute-done.26.refs_6_) | copy-start | bytes 1966084
  122.0 24.8 %collective-permute-start.30 = (bf16[512,640]{1,0:T(8,128)(2,1)S(1)}, bf16[512,640]{1,0:T(8,128)(2,1)S(1)}, u32[]{:S(2)}, u32[]{:S(2)}) collective-permute-start(bf16[512,640]{1,0:T(8,128)(2,1)S(1)} %collective-permute-done.26.refs_6_), channel_id=1, source_target_pairs={{0,1},{1,0},{2,3},{3,2},{4,5},{5,4},{6,7},{7,6},{8,9},{9,8},{10,11... | collective-permute-start | bytes 1966088 | tf_op jit(solution)/shard_map/ppermute | solution.py:324
  123.1 23.7 %collective-permute-start.29 = (bf16[960,256]{1,0:T(8,128)(2,1)S(1)}, bf16[960,256]{1,0:T(8,128)(2,1)S(1)}, u32[]{:S(2)}, u32[]{:S(2)}) collective-permute-start(bf16[960,256]{1,0:T(8,128)(2,1)S(1)} %copy-done.24), channel_id=1, source_target_pairs={{0,3},{1,2},{2,1},{3,0},{4,7},{5,6},{6,5},{7,4},{8,11},{9,10},{10,... | collective-permute-start | bytes 1474568 | tf_op jit(solution)/shard_map/ppermute | solution.py:324
  123.9 11.8 %collective-permute-start.31 = (bf16[20,1280]{1,0:T(8,128)(2,1)S(1)}, bf16[20,1280]{1,0:T(8,128)(2,1)S(1)}, u32[]{:S(2)}, u32[]{:S(2)}) collective-permute-start(bf16[20,1280]{1,0:T(8,128)(2,1)S(1)} %add_convert_fusion.2), channel_id=1, source_target_pairs={{0,4},{1,5},{2,6},{3,7},{4,0},{5,1},{6,2},{7,3},{8,12},{9,13},{10,... | collective-permute-start | bytes 153608 | tf_op jit(solution)/shard_map/ppermute | solution.py:324
  127.8 17.0 %collective-permute-start.32 = (bf16[20,1280]{1,0:T(8,128)(2,1)S(1)}, bf16[20,1280]{1,0:T(8,128)(2,1)S(1)}, u32[]{:S(2)}, u32[]{:S(2)}) collective-permute-start(bf16[20,1280]{1,0:T(8,128)(2,1)S(1)} %add_convert_fusion.2), channel_id=1, source_target_pairs={{0,8},{1,9},{2,10},{3,11},{4,12},{5,13},{6,14},{7,15},{8,0},{9,1},... | collective-permute-start | bytes 153608 | tf_op jit(solution)/shard_map/ppermute | solution.py:324
  132.6 14.3 %collective-permute-start.33 = (bf16[20,1280]{1,0:T(8,128)(2,1)S(1)}, bf16[20,1280]{1,0:T(8,128)(2,1)S(1)}, u32[]{:S(2)}, u32[]{:S(2)}) collective-permute-start(bf16[20,1280]{1,0:T(8,128)(2,1)S(1)} %add_convert_fusion.2), channel_id=1, source_target_pairs={{0,12},{1,13},{2,14},{3,15},{4,8},{5,9},{6,10},{7,11},{8,4},{9,5},... | collective-permute-start | bytes 153608 | tf_op jit(solution)/shard_map/ppermute | solution.py:324
  146.9 13.9 %collective-permute-start.34 = (bf16[20,1280]{1,0:T(8,128)(2,1)S(1)}, bf16[20,1280]{1,0:T(8,128)(2,1)S(1)}, u32[]{:S(2)}, u32[]{:S(2)}) collective-permute-start(bf16[20,1280]{1,0:T(8,128)(2,1)S(1)} %add_convert_fusion.1), channel_id=1, source_target_pairs={{0,0},{1,4},{2,8},{3,12},{4,64},{5,68},{6,72},{7,76},{8,128},{9,13... | collective-permute-start | bytes 153608 | tf_op jit(solution)/shard_map/ppermute | solution.py:438
  (14 other events, 57.5 us)
